TPU v7x, 32 devices: a whole 2x2x4 slice. The times are simulated.
32 devices in a mesh: section: 2 (over y), seq: 8 (over z, x), mp: 2 (over core).
Axes of the slice: x: 2, y: 2, z: 4, core: 2. Of those that a mesh axis runs over, the one named last changes fastest.
Arguments:
- hidden: bfloat16 [1024, 4096], P('seq'), may hold values from -6 to 6
- hidden_gain: bfloat16 [4096], replicated, may hold values from 0.5 to 1.5
- neighbour_states: bfloat16 [128, 128, 896], P('seq'), may hold values from -6 to 6
- encoder_gain: bfloat16 [896], replicated, may hold values from 0.5 to 1.5
- query_weight: bfloat16 [4096, 2048], P('section', 'mp'), may hold values from -0.09375 to 0.09375
- kv_weight: bfloat16 [2, 896, 2048], P(None, None, 'mp'), may hold values from -0.1875 to 0.1875
- attn_grad: bfloat16 [1024, 2048], P('seq', 'mp'), may hold values from -6 to 6
- neighbour_ids: int32 [16, 16], P('seq'), may hold values from 0 to 15, each once within a row
- valid_counts: int32 [16], P('seq'), may hold values from 2 to 16
Outputs:
- hidden_grad: bfloat16 [1024, 4096], P('seq', ('section', 'mp'))
- query_weight_grad: float32 [4096, 2048], P(('section', 'seq'), 'mp')
- kv_weight_grad: float32 [2, 896, 2048], P(None, ('section', 'seq'), 'mp')
- norm_dot: float32 [1024], P('seq')
Inputs may be any that keep to these rules, and one draw needn't show every extreme that they name: `neighbour_ids`: each row lists every one of the 16 pool blocks of its group once.
All inputs are finite; a program needn't handle non-finite values.
Results may differ from a plain program's by a relative error of at most 0.012.
Values may be sent and summed in bfloat16 or wider, within the bound.
No kernel may reach another device: no remote copies, remote signals or barrier semaphores. Data moves between devices by JAX's collectives and lax.ppermute only.
A program may use at most 128 MiB of HBM per device.

v0:
```python
import math

import jax
import jax.numpy as jnp
from jax import lax
from jax.sharding import PartitionSpec as P

HD = 128


EPSILON = 1e-06


def passed_along(array, axis, by):
    size = lax.axis_size(axis)
    pairs = [(i, i + by) for i in range(size) if 0 <= i + by < size]
    return lax.ppermute(array, axis, pairs)


def rms_norm(values, gain_vec):
    widened = values.astype(jnp.float32)
    inv_rms = lax.rsqrt(jnp.mean(widened * widened, axis=-1, keepdims=True) + EPSILON)
    return (widened * inv_rms * gain_vec.astype(jnp.float32), inv_rms)


def block_grads(queries, grad_out, pool_kv, slot_ids, counts):
    block_count, slot_count = slot_ids.shape
    length = pool_kv.shape[2]
    head_count = queries.shape[2]
    head_width = queries.shape[3]
    key_rows = pool_kv[0].reshape(slot_count * length, head_count, head_width)
    value_rows = pool_kv[1].reshape(slot_count * length, head_count, head_width)
    factor = 1.0 / math.sqrt(head_width)
    scores = (
        jnp.einsum("cqhe,khe->chqk", queries, key_rows, preferred_element_type=jnp.float32) * factor
    )
    position = jnp.arange(slot_count, dtype=jnp.int32)
    matches = slot_ids[:, :, None] == position[None, None, :]
    ranking = jnp.sum(jnp.where(matches, position[None, :, None], 0), axis=1)
    usable_pool = ranking < counts[:, None]
    usable = jnp.repeat(usable_pool, length, axis=1)
    scores = jnp.where(usable[:, None, None, :], scores, -1e30)
    attn_probs = jax.nn.softmax(scores, axis=-1)
    grad_probs = jnp.einsum(
        "cqhe,khe->chqk", grad_out, value_rows, preferred_element_type=jnp.float32
    )
    row_delta = jnp.sum(attn_probs * grad_probs, axis=-1, keepdims=True)
    grad_scores = (attn_probs * (grad_probs - row_delta) * factor).astype(jnp.bfloat16)
    probs_low = attn_probs.astype(jnp.bfloat16)
    grad_queries = jnp.einsum(
        "chqk,khe->cqhe", grad_scores, key_rows, preferred_element_type=jnp.float32
    )
    grad_keys = jnp.einsum(
        "chqk,cqhe->khe", grad_scores, queries, preferred_element_type=jnp.float32
    )
    grad_values = jnp.einsum(
        "chqk,cqhe->khe", probs_low, grad_out, preferred_element_type=jnp.float32
    )
    pooled = jnp.stack([grad_keys, grad_values]).reshape(
        2, slot_count, length, head_count * head_width
    )
    return (grad_queries, pooled)


def body(
    hidden,
    hidden_gain,
    neighbour_states,
    encoder_gain,
    query_weight,
    kv_weight,
    attn_grad,
    neighbour_ids,
    valid_counts,
):
    section_idx = lax.axis_index("section")
    on_decoder = section_idx == 1
    on_encoder = section_idx == 0
    row_count = hidden.shape[0]
    model_width = hidden.shape[1]
    half_width = query_weight.shape[0]
    local_heads = query_weight.shape[1]
    head_count = local_heads // HD
    block_count = neighbour_ids.shape[0]
    block_len = row_count // block_count
    offset = block_len - 1
    normed, inv_rms = rms_norm(hidden, hidden_gain)
    hidden_normed = normed.astype(jnp.bfloat16)
    own_cols = lax.dynamic_slice_in_dim(hidden_normed, section_idx * half_width, half_width, 1)
    query_part = jnp.dot(own_cols, query_weight, preferred_element_type=jnp.float32)
    query_other = passed_along(query_part, "section", 1)
    queries = (query_part + query_other).astype(jnp.bfloat16)
    slot_total, nb_length, enc_width = neighbour_states.shape
    pool_rows = slot_total * nb_length
    pool_normed, pool_rms = rms_norm(neighbour_states, encoder_gain)
    pool_low = pool_normed.astype(jnp.bfloat16).reshape(pool_rows, enc_width)

    def project(operand):
        key_proj = jnp.dot(operand, kv_weight[0], preferred_element_type=jnp.float32)
        value_proj = jnp.dot(operand, kv_weight[1], preferred_element_type=jnp.float32)
        return jnp.stack([key_proj, value_proj]).astype(jnp.bfloat16)

    def no_project(operand):
        return jnp.zeros((2, operand.shape[0], local_heads), jnp.bfloat16)

    pool_kv = lax.cond(on_decoder, project, no_project, pool_low)
    leading = jnp.stack([queries[:offset], attn_grad[:offset]])
    following = passed_along(leading, "seq", -1)
    ext_queries = jnp.concatenate([queries[offset:], following[0]], 0).reshape(
        block_count, block_len, head_count, HD
    )
    ext_grads = jnp.concatenate([attn_grad[offset:], following[1]], 0).reshape(
        block_count, block_len, head_count, HD
    )
    pool_view = pool_kv.reshape(2, slot_total, nb_length, head_count, HD)

    def attend(operands):
        q_in, g_in, kv_in = operands
        grad_queries, pooled = block_grads(q_in, g_in, kv_in, neighbour_ids, valid_counts)
        return (
            grad_queries.reshape(row_count, local_heads).astype(jnp.bfloat16),
            pooled.reshape(2, pool_rows, local_heads).astype(jnp.bfloat16),
        )

    def skip_attend(operands):
        return (
            jnp.zeros((row_count, local_heads), jnp.bfloat16),
            jnp.zeros((2, pool_rows, local_heads), jnp.bfloat16),
        )

    ext_dq, own_dkv = lax.cond(on_decoder, attend, skip_attend, (ext_queries, ext_grads, pool_view))
    carried = passed_along(ext_dq[row_count - offset :], "seq", 1)
    own_dq = jnp.concatenate([carried, ext_dq[: row_count - offset]], 0)
    enc_half = enc_width // 2
    back_dq, back_dkv = passed_along((own_dq, own_dkv), "section", -1)
    dq_use = jnp.where(on_encoder, back_dq, own_dq)
    dkv_use = jnp.where(on_encoder, back_dkv, own_dkv)
    enc_cols = lax.dynamic_slice_in_dim(pool_low, section_idx * enc_half, enc_half, 1)
    part_cols = enc_cols
    kv_rows = lax.psum_scatter(
        jnp.einsum("tr,ktc->rkc", part_cols, dkv_use, preferred_element_type=jnp.float32),
        "seq",
        scatter_dimension=0,
        tiled=True,
    )
    kv_grad = jnp.transpose(kv_rows, (1, 0, 2))
    part_cols = own_cols
    query_grad = lax.psum_scatter(
        lax.dot_general(
            part_cols, dq_use, (((0,), (0,)), ((), ())), preferred_element_type=jnp.float32
        ),
        "seq",
        scatter_dimension=0,
        tiled=True,
    )
    partial_grad = lax.dot_general(
        dq_use, query_weight, (((1,), (1,)), ((), ())), preferred_element_type=jnp.float32
    )
    feature_grad = lax.psum_scatter(
        partial_grad.astype(jnp.bfloat16), "mp", scatter_dimension=1, tiled=True
    ).astype(jnp.float32)
    quarter = feature_grad.shape[1]
    start_col = section_idx * half_width + lax.axis_index("mp") * quarter
    gain_part = lax.dynamic_slice_in_dim(hidden_gain, start_col, quarter, 0).astype(jnp.float32)
    hidden_part = lax.dynamic_slice_in_dim(hidden, start_col, quarter, 1).astype(jnp.float32)
    scaled = gain_part * feature_grad
    row_dot = lax.psum(jnp.sum(scaled * hidden_part, axis=1, keepdims=True), ("section", "mp"))
    norm_dot = row_dot[:, 0] / math.sqrt(model_width)
    hidden_grad = (inv_rms * scaled - hidden_part * inv_rms**3 * row_dot / model_width).astype(
        jnp.bfloat16
    )
    return (hidden_grad, query_grad, kv_grad, norm_dot)


def solution(mesh):
    placed = (
        P("seq", None),
        P(),
        P("seq", None, None),
        P(),
        P("section", "mp"),
        P(None, None, "mp"),
        P("seq", "mp"),
        P("seq", None),
        P("seq"),
    )
    return jax.shard_map(
        body,
        mesh=mesh,
        in_specs=placed,
        out_specs=(
            P("seq", ("section", "mp")),
            P(("section", "seq"), "mp"),
            P(None, ("section", "seq"), "mp"),
            P("seq"),
        ),
        check_vma=False,
    )
```

profile of v0, /device:TPU:0, one launch (start us, length us, event | category | flops | bytes accessed | tf_op | source)
XLA Modules:
  0.0 588.8 jit_solution(17099085983725442066)
XLA Ops:
  7.2 0.0 copy-start.9
  7.2 0.0 copy-start.4
  7.2 0.0 reduce-scatter.4.cloned.1.call-start
  7.2 1.5 convert_element_type.58
  8.7 1.5 multiply_reduce_fusion.1
  10.2 0.5 multiply_multiply_fusion
  10.7 0.8 dynamic-slice
  11.6 0.6 copy-done.5
  12.2 2.9 fusion.46
  15.1 4.9 collective-permute-start
  20.0 0.0 copy-done.1
  20.1 1.4 fusion.32
  21.4 0.0 copy-done.9
  21.5 0.7 add_rsqrt_fusion
  22.2 9.0 %collective-permute-done = f32[128,1024]{1,0:T(8,128)S(1)} collective-permute-done((f32[128,1024]{1,0:T(8,128)S(1)}, f32[128,1024]{1,0:T(8,128)S(1)}, u32[]{:S(2)}, u32[]{:S(2)}) %collective-permute-start) | collective-permute-done | bytes 524320 | tf_op jit(solution)/shard_map/ppermute | solution.py:17
  31.2 0.1 add_convert_fusion
  31.3 1.3 collective-permute-start.1
  32.6 4.7 fusion.34
  37.3 6.1 %copy.50 = bf16[2048,896]{0,1:T(8,128)(2,1)} copy(bf16[2048,896]{1,0:T(8,128)(2,1)} %bitcast.107) | data formatting | bytes 7340032 | tf_op jit(solution)/shard_map/reshape | solution.py:96
  43.5 5.3 conditional.2
  43.5 5.3 reshape.78
  48.9 0.0 collective-permute-done.1
  48.9 0.1 pad_maximum_fusion.3
  49.0 4.3 conditional.3
  49.0 4.3 broadcast.52
  53.3 1.3 collective-permute-start.4
  54.6 4.6 collective-permute-start.2
  59.2 2.5 collective-permute-done.2
  61.7 1.3 collective-permute-start.3
  63.0 265.5 %collective-permute-done.3 = bf16[128,1024]{1,0:T(8,128)(2,1)S(1)} collective-permute-done((bf16[128,1024]{1,0:T(8,128)(2,1)S(1)}, bf16[128,1024]{1,0:T(8,128)(2,1)S(1)}, u32[]{:S(2)}, u32[]{:S(2)}) %collective-permute-start.3) | collective-permute-done | bytes 262176 | tf_op jit(solution)/shard_map/ppermute | solution.py:17
  328.6 4.5 convolution_convert_fusion
  333.1 0.0 reduce-scatter.4.cloned.1.call-update
  333.1 0.0 copy-start.6
  333.1 0.3 reduce-scatter.8.cloned.1.call-start
  333.4 0.0 collective-permute-done.4
  333.4 9.8 %fusion.29 = f32[448,2,1024]{2,0,1:T(8,128)} fusion(bf16[2,2048,1024]{1,2,0:T(8,128)(2,1)} %collective-permute-done.4, bf16[2,2048,1024]{1,2,0:T(8,128)(2,1)} %get-tuple-element.34, pred[]{:T(512)S(6)} %eq.19, bf16[2048,896]{0,1:T(8,128)(2,1)} %copy.50, s32[]{:T(128)S(6)} %select_n.38), kind=kOutput, calls=%fused_computation.38 | convolution fusion | flops 3762290688 | bytes 22282244 | tf_op jit(solution)/shard_map/tr,ktc->rkc/dot_general | solution.py:141
  343.2 0.0 reduce-scatter.8.cloned.1.call-update
  343.2 0.0 reduce-scatter.6.cloned.1.call-start
  343.2 4.6 fusion.44
  347.8 0.0 reduce-scatter.6.cloned.1.call-update
  347.9 0.8 dynamic-slice_convert_fusion
  348.6 0.4 copy-done.2
  349.1 1.1 fusion.43
  350.2 5.8 psum.7
  355.9 0.5 broadcast_multiply_fusion
  356.5 1.9 fusion.42
  358.4 70.6 %reduce-scatter.8.cloned.1.call-done = f32[56,2,1024]{2,0,1:T(8,128)} async-done(((f32[448,2,1024]{2,0,1:T(8,128)}), f32[56,2,1024]{2,0,1:T(8,128)}) %reduce-scatter.8.cloned.1.call-update) | async-done | bytes 458768 | tf_op jit(solution)/shard_map/reduce_scatter | solution.py:140
  428.9 153.4 %reduce-scatter.6.cloned.1.call-done = f32[256,1024]{1,0:T(8,128)} async-done(((f32[2048,1024]{1,0:T(8,128)}), f32[256,1024]{1,0:T(8,128)}) %reduce-scatter.6.cloned.1.call-update) | async-done | bytes 1048592 | tf_op jit(solution)/shard_map/reduce_scatter | solution.py:148
  (23 shorter events, 0.3 us)
Async XLA Ops:
  7.2 14.3 %copy-start.9 = (bf16[896]{0:T(1024)(128)(2,1)S(1)}, bf16[896]{0:T(1024)(128)(2,1)}, u32[]{:S(2)}) copy-start(bf16[896]{0:T(1024)(128)(2,1)} %param.16) | copy-start | bytes 5380
  7.2 14.3 %copy-start.4 = (bf16[128,1024]{1,0:T(8,128)(2,1)S(1)}, bf16[128,1024]{1,0:T(8,128)(2,1)}, u32[]{:S(2)}) copy-start(bf16[128,1024]{1,0:T(8,128)(2,1)} %param.19) | copy-start | bytes 786436
  7.2 341.4 %reduce-scatter.4.cloned.1.call-start = ((), (), s32[]{:S(2)}) async-start(), calls=%async_computation.3 | async-start | bytes 786432 | tf_op jit(solution)/shard_map/reduce_scatter | solution.py:159
  10.7 0.8 copy-start.7
  10.7 9.3 %copy-start.1 = (bf16[16,128,896]{2,1,0:T(8,128)(2,1)S(1)}, bf16[16,128,896]{2,1,0:T(8,128)(2,1)}, u32[]{:S(2)}) copy-start(bf16[16,128,896]{2,1,0:T(8,128)(2,1)} %param.15) | copy-start | bytes 11010052
  11.6 0.6 copy-start.5
  15.1 16.0 %collective-permute-start = (f32[128,1024]{1,0:T(8,128)S(1)}, f32[128,1024]{1,0:T(8,128)S(1)}, u32[]{:S(2)}, u32[]{:S(2)}) collective-permute-start(f32[128,1024]{1,0:T(8,128)S(1)} %fusion.46), channel_id=1, source_target_pairs={{0,16},{1,17},{2,18},{3,19},{4,20},{5,21},{6,22},{7,23},{8,24},{9,... | collective-permute-start | bytes 1572872 | tf_op jit(solution)/shard_map/ppermute | solution.py:17
  31.3 17.6 %collective-permute-start.1 = (bf16[2,63,1024]{2,1,0:T(8,128)(2,1)S(1)}, bf16[2,63,1024]{2,1,0:T(8,128)(2,1)S(1)}, u32[]{:S(2)}, u32[]{:S(2)}) collective-permute-start(bf16[2,63,1024]{2,1,0:T(8,128)(2,1)S(1)} %pad_maximum_fusion.2), channel_id=1, source_target_pairs={{2,0},{4,2},{6,4},{8,6},{10,8},{12,10},{14,12},{3,1},{5,3},{7,5},{... | collective-permute-start | bytes 774152 | tf_op jit(solution)/shard_map/ppermute | solution.py:17
  53.3 280.1 %collective-permute-start.4 = (bf16[2,2048,1024]{1,2,0:T(8,128)(2,1)}, bf16[2,2048,1024]{1,2,0:T(8,128)(2,1)}, u32[]{:S(2)}, u32[]{:S(2)}) collective-permute-start(bf16[2,2048,1024]{1,2,0:T(8,128)(2,1)} %get-tuple-element.34), channel_id=1, source_target_pairs={{16,0},{17,1},{18,2},{19,3},{20,4},{21,5},{22,6},{23,7},{24,8},{25... | collective-permute-start | bytes 25165832 | tf_op jit(solution)/shard_map/ppermute | solution.py:17
  54.6 7.1 %collective-permute-start.2 = (bf16[63,1024]{1,0:T(8,128)(2,1)S(1)}, bf16[63,1024]{1,0:T(8,128)(2,1)S(1)}, u32[]{:S(2)}, u32[]{:S(2)}) collective-permute-start(bf16[63,1024]{1,0:T(8,128)(2,1)S(1)} %slice.42), channel_id=1, source_target_pairs={{0,2},{2,4},{4,6},{6,8},{8,10},{10,12},{12,14},{1,3},{3,5},{5,7},{... | collective-permute-start | bytes 387080 | tf_op jit(solution)/shard_map/ppermute | solution.py:17
  61.7 266.8 %collective-permute-start.3 = (bf16[128,1024]{1,0:T(8,128)(2,1)S(1)}, bf16[128,1024]{1,0:T(8,128)(2,1)S(1)}, u32[]{:S(2)}, u32[]{:S(2)}) collective-permute-start(bf16[128,1024]{1,0:T(8,128)(2,1)S(1)} %pad_maximum_fusion.5), channel_id=1, source_target_pairs={{16,0},{17,1},{18,2},{19,3},{20,4},{21,5},{22,6},{23,7},{24,8},{25... | collective-permute-start | bytes 786440 | tf_op jit(solution)/shard_map/ppermute | solution.py:17
  333.1 10.1 %copy-start.6 = (f32[2048]{0:T(1024)S(1)}, f32[2048]{0:T(1024)}, u32[]{:S(2)}) copy-start(f32[2048]{0:T(1024)} %copy-done.5) | copy-start | bytes 24580
  333.1 10.1 %copy-start.8 = (f32[128]{0:T(128)S(1)}, f32[128]{0:T(128)}, u32[]{:S(2)}) copy-start(f32[128]{0:T(128)} %copy-done.7) | copy-start | bytes 1540
  333.1 95.8 %reduce-scatter.8.cloned.1.call-start = ((), (), s32[]{:S(2)}) async-start(), calls=%async_computation.5 | async-start | bytes 4128768 | tf_op jit(solution)/shard_map/reduce_scatter | solution.py:140
  343.2 239.1 %reduce-scatter.6.cloned.1.call-start = ((), (), s32[]{:S(2)}) async-start(), calls=%async_computation.4 | async-start | bytes 9437184 | tf_op jit(solution)/shard_map/reduce_scatter | solution.py:148
  347.8 1.2 copy-start.2
  347.8 8.6 %copy-start.11 = (f32[128]{0:T(128)S(1)}, f32[128]{0:T(128)}, u32[]{:S(2)}) copy-start(f32[128]{0:T(128)} %get-tuple-element.70) | copy-start | bytes 1540
Sparse Core Ops, SparseCore 0:
  333.2 9.0 reduce-scatter.3
  347.0 81.8 reduce-scatter.7
  433.6 148.6 reduce-scatter.5
where the time goes:
time: 590 us; the launch traced here: 589 us
  waiting for transfers between devices  501 us (85%)
  matrix products  21.8 us (4%)
  local copies, waits for them, and re-layouts  17.8 us (3%)
  other arithmetic  14.9 us (3%)
  between operations  14 us (2%)
  starting transfers between devices  13.7 us (2%)
    ppermute x5, waiting for transfers between devices, passed_along(): return lax.ppermute(array, axis, pairs)  277 us
    reduce_scatter x1, waiting for transfers between devices, body(): lax.psum_scatter(lax.dot_general(part_cols, dq_use, (((0,), (0,)), ((), (...  153 us
    reduce_scatter x1, waiting for transfers between devices, body(): lax.psum_scatter(jnp.einsum('tr,ktc->rkc', part_cols, dkv_use, preferred_...  70.6 us
    ppermute x5, starting transfers between devices, passed_along(): return lax.ppermute(array, axis, pairs)  13.3 us
  transfers between devices with their start and end apart: 8, of which 5 were waited for; matrix products, arithmetic and copies ran while one was open for 7% of the time, Pallas kernels for 0%

commit v1 on v0

v1 whole, which is shorter than its diff:
```python
import functools
import math

import jax
import jax.numpy as jnp
from jax import lax
from jax.experimental import pallas as pl
from jax.experimental.pallas import tpu as pltpu
from jax.sharding import PartitionSpec as P

HD = 128
EPSILON = 1e-06
MASKED = -1e30
VMEM_BYTES = 48 * 1024 * 1024
CHUNKS = 2

F32 = jnp.float32
BF16 = jnp.bfloat16


def shape(dims, kind):
    return jax.ShapeDtypeStruct(dims, kind)


def params():
    return pltpu.CompilerParams(vmem_limit_bytes=VMEM_BYTES)


def cost(flops, moved):
    return pl.CostEstimate(flops=flops, bytes_accessed=moved, transcendentals=0)


def nt_dot(left, right):
    return lax.dot_general(left, right, (((1,), (1,)), ((), ())), preferred_element_type=F32)


def swapped(array, axis, mask):
    size = lax.axis_size(axis)
    return lax.ppermute(array, axis, [(i, i ^ mask) for i in range(size)])


def query_kernel(
    step_count, lead, place, hidden, gain, weight, grad_lead, hn_out, rms_out, keep_out, send_out,
    pair_out, cross_out, total,
):
    step = pl.program_id(0)
    section = place[0]
    width = hidden.shape[1]
    half = width // 2
    depth = weight.shape[0]
    cols = keep_out.shape[1]

    @pl.when(step == 0)
    def _():
        wide = hidden[...].astype(F32)
        inv_rms = lax.rsqrt(jnp.mean(wide * wide, axis=1, keepdims=True) + EPSILON)
        rms_out[...] = inv_rms
        hn_out[...] = (wide * inv_rms * gain[...].astype(F32)).astype(BF16)
        total[...] = jnp.zeros_like(total)

    start = pl.multiple_of(section * half + step * depth, depth)
    total[...] += jnp.dot(hn_out[:, pl.ds(start, depth)], weight[...], preferred_element_type=F32)

    @pl.when(step == step_count - 1)
    def _():
        mine = total[:, pl.ds(pl.multiple_of(section * cols, cols), cols)]
        other = total[:, pl.ds(pl.multiple_of((1 - section) * cols, cols), cols)].astype(BF16)
        keep_out[...] = mine
        send_out[...] = other
        pair_out[0] = mine[:lead].astype(BF16)
        pair_out[1] = grad_lead[...]
        cross_out[...] = other[:lead]


def query_part(place, hidden, gain, weight, attn_grad, lead):
    rows, width = hidden.shape
    half, local = weight.shape
    cols = local // 2
    step_count = 4
    depth = half // step_count
    spec = pltpu.PrefetchScalarGridSpec(
        num_scalar_prefetch=1,
        grid=(step_count,),
        in_specs=[
            pl.BlockSpec((rows, width), lambda k, place: (0, 0)),
            pl.BlockSpec((1, width), lambda k, place: (0, 0)),
            pl.BlockSpec((depth, local), lambda k, place: (k, 0)),
            pl.BlockSpec((lead, cols), lambda k, place: (0, place[0])),
        ],
        out_specs=[
            pl.BlockSpec((rows, width), lambda k, place: (0, 0)),
            pl.BlockSpec((rows, 1), lambda k, place: (0, 0)),
            pl.BlockSpec((rows, cols), lambda k, place: (0, 0)),
            pl.BlockSpec((rows, cols), lambda k, place: (0, 0)),
            pl.BlockSpec((2, lead, cols), lambda k, place: (0, 0, 0)),
            pl.BlockSpec((lead, cols), lambda k, place: (0, 0)),
        ],
        scratch_shapes=[pltpu.VMEM((rows, local), F32)],
    )
    return pl.pallas_call(
        functools.partial(query_kernel, step_count, lead),
        grid_spec=spec,
        out_shape=[
            shape((rows, width), BF16),
            shape((rows, 1), F32),
            shape((rows, cols), F32),
            shape((rows, cols), BF16),
            shape((2, lead, cols), BF16),
            shape((lead, cols), BF16),
        ],
        compiler_params=params(),
        cost_estimate=cost(2 * rows * half * local, 2 * half * local + 4 * rows * width),
        name="query_part",
    )(place, hidden, gain.reshape(1, width), weight, attn_grad)


def columns_kernel(count, place, hn, *rest):
    *outs, turned = rest
    turned[...] = hn[...].T
    half = hn.shape[1] // 2
    span = half // count
    for other in range(count):
        start = (place[1] ^ other) * span
        for part in range(2):
            piece = turned[pl.ds(pl.multiple_of(part * half + start, span), span), :]
            outs[other][part * span : (part + 1) * span, :] = piece


def columns_for(place, hn, count):
    rows, width = hn.shape
    span = width // count
    return pl.pallas_call(
        functools.partial(columns_kernel, count),
        grid_spec=pltpu.PrefetchScalarGridSpec(
            num_scalar_prefetch=1,
            grid=(1,),
            in_specs=[pl.BlockSpec((rows, width), lambda k, place: (0, 0))],
            out_specs=[pl.BlockSpec((span, rows), lambda k, place: (0, 0)) for _ in range(count)],
            scratch_shapes=[pltpu.VMEM((width, rows), BF16)],
        ),
        out_shape=[shape((span, rows), BF16) for _ in range(count)],
        compiler_params=params(),
        cost_estimate=cost(0, 4 * rows * width),
        name="hidden_columns",
    )(place, hn)


def pool_kernel(place, states, gain, weight, kv_out, turned_out):
    wide = states[...].astype(F32)
    inv_rms = lax.rsqrt(jnp.mean(wide * wide, axis=1, keepdims=True) + EPSILON)
    normed = (wide * inv_rms * gain[...].astype(F32)).astype(BF16)
    for which in range(2):
        kv_out[which] = jnp.dot(
            normed, weight[which], preferred_element_type=F32
        ).astype(BF16)
    turned_out[...] = normed.T


def pool_project(place, states, gain, weight):
    rows, width = states.shape
    cols = weight.shape[2] // 2
    block = min(rows, 256)
    return pl.pallas_call(
        pool_kernel,
        grid_spec=pltpu.PrefetchScalarGridSpec(
            num_scalar_prefetch=1,
            grid=(rows // block,),
            in_specs=[
                pl.BlockSpec((block, width), lambda k, place: (k, 0)),
                pl.BlockSpec((1, width), lambda k, place: (0, 0)),
                pl.BlockSpec((2, width, cols), lambda k, place: (0, 0, place[0])),
            ],
            out_specs=[
                pl.BlockSpec((2, block, cols), lambda k, place: (0, k, 0)),
                pl.BlockSpec((width, block), lambda k, place: (0, k)),
            ],
        ),
        out_shape=[shape((2, rows, cols), BF16), shape((width, rows), BF16)],
        compiler_params=params(),
        cost_estimate=cost(4 * rows * width * cols, 4 * rows * width + 8 * rows * cols),
        name="pool_project",
    )(place, states, gain.reshape(1, width), weight)


def rows_at(ref, start, size):
    if size % 8 == 0:
        return ref[pl.ds(pl.multiple_of(start, 8), size), :]
    window = (size + 14) // 8 * 8
    rest = start % 8
    wide = ref[pl.ds(pl.multiple_of(start - rest, 8), window), :]
    return pltpu.roll(wide, window - rest, 0)[:size]


def attend_kernel(
    last, slot_count, count, place, ids, counts, keep, other, pair, cross, grad_own, kv, turned_hbm,
    *rest,
):
    if last:
        before, dq_out, lead_out, *rest = rest
    else:
        dq_out, *rest = rest
    send_out, keep_out, turned, bias, turned_kv, product, sem = rest
    fetch = pltpu.make_async_copy(turned_hbm, turned, sem)
    fetch.start()
    rows, cols = keep.shape
    lead = cross.shape[0]
    keys = kv.shape[1]
    block_count = counts.shape[0]
    block_len = rows // block_count
    offset = block_len - 1
    length = keys // slot_count
    factor = 1.0 / math.sqrt(HD)
    slot_of = lax.broadcasted_iota(jnp.int32, (1, keys), 1) // length
    for block in range(block_count):
        line = jnp.full((1, keys), MASKED, F32)
        for slot in range(slot_count):
            opened = jnp.where(slot < counts[block], ids[block, slot], -1)
            line = jnp.where(slot_of == opened, 0.0, line)
        bias[block * block_len : (block + 1) * block_len, :] = jnp.broadcast_to(
            line, (block_len, keys)
        )
    row = lax.broadcasted_iota(jnp.int32, (rows, 1), 0)
    following = row < offset
    own = keep[...] + other[...].astype(F32)
    led = pair[0].astype(F32) + cross[...].astype(F32)
    padding = jnp.zeros((rows - lead, cols), F32)
    queries = jnp.where(following, jnp.concatenate([led, padding], 0), own)
    queries = pltpu.roll(queries, rows - offset, 0)
    grads = jnp.where(
        following, jnp.concatenate([pair[1].astype(F32), padding], 0), grad_own[...].astype(F32)
    )
    grads = pltpu.roll(grads, rows - offset, 0)
    for head in range(cols // HD):
        span = slice(head * HD, (head + 1) * HD)
        query = queries[:, span].astype(BF16)
        grad = grads[:, span].astype(BF16)
        key = kv[0, :, span]
        value = kv[1, :, span]
        scores = nt_dot(query, key) * factor + bias[...]
        peak = jnp.max(scores, axis=1, keepdims=True)
        weights = jnp.exp(scores - peak)
        norm = 1.0 / jnp.sum(weights, axis=1, keepdims=True)
        probs = weights * norm
        grad_probs = nt_dot(grad, value)
        delta = jnp.sum(probs * grad_probs, axis=1, keepdims=True)
        grad_scores = (probs * (grad_probs - delta) * factor).astype(BF16)
        dq = jnp.dot(grad_scores, key, preferred_element_type=F32)
        dq = pltpu.roll(dq, offset, 0).astype(BF16)
        place_at = before.shape[1] if last else 0
        dq_out[:, place_at + head * HD : place_at + (head + 1) * HD] = dq
        if last:
            lead_out[:, place_at + head * HD : place_at + (head + 1) * HD] = dq[:lead]
        turned_query = queries[:, span].T.astype(BF16)
        turned_grad = grads[:, span].T.astype(BF16)
        turned_kv[span, :] = jnp.dot(
            turned_query, grad_scores, preferred_element_type=F32
        ).astype(BF16)
        turned_kv[cols + head * HD : cols + (head + 1) * HD, :] = jnp.dot(
            turned_grad, probs.astype(BF16), preferred_element_type=F32
        ).astype(BF16)
    if last:
        dq_out[:, : before.shape[1]] = before[...]
        lead_out[:, : before.shape[1]] = before[:lead]
    fetch.wait()
    width = turned.shape[0]
    product[:width] = nt_dot(turned[...], turned_kv[...])
    piece = send_out.shape[2]
    half = width // 2
    for step in range(count):
        for part in range(2):
            for outs, inner in ((keep_out, place[2]), (send_out, 1 - place[2])):
                start = part * half + (2 * (place[1] ^ step) + inner) * piece
                outs[step, part] = rows_at(product, start, piece).astype(outs.dtype)


def attend(
    chunk, place, ids, counts, keep, other, pair, cross, attn_grad, kv, turned, before, seq_size
):
    rows, all_cols = keep.shape
    cols = all_cols // CHUNKS
    lead = cross.shape[0]
    keys = kv.shape[1]
    width = turned.shape[0]
    count = seq_size // 2
    piece = width // (2 * seq_size)
    last = before is not None
    in_specs = [
        pl.BlockSpec((rows, cols), lambda k, place, ids, counts: (0, chunk)),
        pl.BlockSpec((rows, cols), lambda k, place, ids, counts: (0, chunk)),
        pl.BlockSpec((2, lead, cols), lambda k, place, ids, counts: (0, 0, chunk)),
        pl.BlockSpec((lead, cols), lambda k, place, ids, counts: (0, chunk)),
        pl.BlockSpec(
            (rows, cols), lambda k, place, ids, counts: (0, place[0] * CHUNKS + chunk)
        ),
        pl.BlockSpec((2, keys, cols), lambda k, place, ids, counts: (0, 0, chunk)),
        pl.BlockSpec(memory_space=pl.ANY),
    ]
    operands = [keep, other, pair, cross, attn_grad, kv, turned]

    def whole(dims):
        return pl.BlockSpec(dims, lambda k, place, ids, counts: (0,) * len(dims))

    out_shape = []
    if last:
        in_specs.append(whole(before.shape))
        operands.append(before)
        out_shape += [shape((rows, all_cols), BF16), shape((lead, all_cols), BF16)]
    else:
        out_shape.append(shape((rows, cols), BF16))
    out_shape += [
        shape((count, 2, piece, 2 * cols), BF16),
        shape((count, 2, piece, 2 * cols), F32),
    ]
    heads = cols // HD
    return pl.pallas_call(
        functools.partial(attend_kernel, last, ids.shape[1], count),
        grid_spec=pltpu.PrefetchScalarGridSpec(
            num_scalar_prefetch=3,
            grid=(1,),
            in_specs=in_specs,
            out_specs=[whole(out.shape) for out in out_shape],
            scratch_shapes=[
                pltpu.VMEM((width, keys), BF16),
                pltpu.VMEM((rows, keys), F32),
                pltpu.VMEM((2 * cols, keys), BF16),
                pltpu.VMEM((width + 16, 2 * cols), F32),
                pltpu.SemaphoreType.DMA,
            ],
        ),
        out_shape=out_shape,
        compiler_params=params(),
        cost_estimate=cost(
            10 * heads * rows * keys * HD + 4 * width * keys * cols,
            4 * keys * cols + 2 * width * keys + 12 * width * cols,
        ),
        name="attend_%d" % chunk,
    )(place, ids, counts, *operands)


def weight_kernel(count, place, *refs):
    columns, grads, (send_out, keep_out) = refs[:count], refs[count : 2 * count], refs[2 * count :]
    piece = send_out.shape[1]
    for part in range(2):
        for outs, inner in ((send_out, 1 - place[2]), (keep_out, place[2])):
            start = pl.multiple_of((2 * part + inner) * piece, piece)
            total = None
            for column, grad in zip(columns, grads):
                term = jnp.dot(
                    column[pl.ds(start, piece), :], grad[...], preferred_element_type=F32
                )
                total = term if total is None else total + term
            outs[part] = total.astype(outs.dtype)


def weight_part(place, columns, grads):
    count = len(columns)
    span, rows = columns[0].shape
    cols = grads[0].shape[1]
    piece = span // 4

    def whole(dims):
        return pl.BlockSpec(dims, lambda k, place: (0,) * len(dims))

    return pl.pallas_call(
        functools.partial(weight_kernel, count),
        grid_spec=pltpu.PrefetchScalarGridSpec(
            num_scalar_prefetch=1,
            grid=(1,),
            in_specs=[whole((span, rows))] * count + [whole((rows, cols))] * count,
            out_specs=[whole((2, piece, cols)), whole((2, piece, cols))],
        ),
        out_shape=[shape((2, piece, cols), BF16), shape((2, piece, cols), F32)],
        compiler_params=params(),
        cost_estimate=cost(2 * count * span * rows * cols, 6 * span * cols + 2 * count * span * rows),
        name="weight_part",
    )(place, *columns, *grads)


def normed_kernel(step_count, place, own, other, weight, keep_out, send_out, total):
    step = pl.program_id(0)
    cols = own.shape[1]
    depth = weight.shape[0]
    section = place[0]
    first = jnp.where(section == 0, own[...], other[...])
    second = jnp.where(section == 0, other[...], own[...])
    total[step] = nt_dot(first, weight[:, :cols]) + nt_dot(second, weight[:, cols:])

    @pl.when(step == step_count - 1)
    def _():
        per = step_count // 2
        for part in range(per):
            keep_out[:, part * depth : (part + 1) * depth] = total[place[3] * per + part]
            send_out[:, part * depth : (part + 1) * depth] = total[
                (1 - place[3]) * per + part
            ].astype(BF16)


def normed_part(place, own, other, weight):
    rows, cols = own.shape
    half, local = weight.shape
    step_count = 4
    depth = half // step_count
    quarter = half // 2

    def whole(dims):
        return pl.BlockSpec(dims, lambda k, place: (0,) * len(dims))

    return pl.pallas_call(
        functools.partial(normed_kernel, step_count),
        grid_spec=pltpu.PrefetchScalarGridSpec(
            num_scalar_prefetch=1,
            grid=(step_count,),
            in_specs=[
                whole((rows, cols)),
                whole((rows, cols)),
                pl.BlockSpec((depth, local), lambda k, place: (k, 0)),
            ],
            out_specs=[whole((rows, quarter)), whole((rows, quarter))],
            scratch_shapes=[pltpu.VMEM((step_count, rows, depth), F32)],
        ),
        out_shape=[shape((rows, quarter), F32), shape((rows, quarter), BF16)],
        compiler_params=params(),
        cost_estimate=cost(2 * rows * half * local, 2 * half * local + 6 * rows * quarter),
        name="normed_part",
    )(place, own, other, weight)


def body(
    hidden,
    hidden_gain,
    neighbour_states,
    encoder_gain,
    query_weight,
    kv_weight,
    attn_grad,
    neighbour_ids,
    valid_counts,
):
    section = lax.axis_index("section")
    seq = lax.axis_index("seq")
    core = lax.axis_index("mp")
    seq_size = lax.axis_size("seq")
    outer = seq_size // 2
    row_count, model_width = hidden.shape
    half_width, local_cols = query_weight.shape
    cols = local_cols // 2
    slot_total, nb_length, enc_width = neighbour_states.shape
    block_count = neighbour_ids.shape[0]
    block_len = row_count // block_count
    offset = block_len - 1
    place = jnp.stack([section, seq // 2, seq % 2, core]).astype(jnp.int32)

    hn, inv_rms, keep, send, pair, cross = query_part(
        place, hidden, hidden_gain, query_weight, attn_grad, block_len
    )
    other = swapped(send, "section", 1)
    pair_in = lax.ppermute(pair, "seq", [(i, i - 1) for i in range(1, seq_size)])
    cross_in = lax.ppermute(
        cross,
        ("section", "seq"),
        [
            (s * seq_size + i, (1 - s) * seq_size + i - 1)
            for s in range(2)
            for i in range(1, seq_size)
        ],
    )
    columns = columns_for(place, hn, outer)
    columns_in = [columns[0]] + [swapped(columns[d], "seq", 2 * d) for d in range(1, outer)]
    kv, turned = pool_project(
        place, neighbour_states.reshape(slot_total * nb_length, enc_width), encoder_gain, kv_weight
    )

    dq_comb = None
    sums = []
    for chunk in range(CHUNKS):
        *dq_parts, chunk_send, chunk_keep = attend(
            chunk,
            place,
            neighbour_ids,
            valid_counts,
            keep,
            other,
            pair_in,
            cross_in,
            attn_grad,
            kv,
            turned,
            dq_comb,
            seq_size,
        )
        dq_comb = dq_parts[0]
        sums.append((swapped(chunk_send, "seq", 1), chunk_keep))
    dq_lead = dq_parts[1]

    carried = lax.ppermute(dq_lead, "seq", [(i, i + 1) for i in range(seq_size - 1)])
    padded = jnp.concatenate([carried, jnp.zeros((row_count - block_len, cols), BF16)], 0)
    own_dq = jnp.where(jnp.arange(row_count)[:, None] < offset, padded, dq_comb)

    pieces = []
    for received, kept in sums:
        summed = kept + received.astype(F32)
        total = summed[0]
        for d in range(1, outer):
            total = total + swapped(summed[d].astype(BF16), "seq", 2 * d).astype(F32)
        pieces.append(total)
    pieces = jnp.stack(pieces)
    mine = lax.dynamic_index_in_dim(pieces, section, 1, keepdims=False)
    theirs = lax.dynamic_index_in_dim(pieces, 1 - section, 1, keepdims=False)
    got = swapped(theirs.astype(BF16), "section", 1).astype(F32)
    by_section = jnp.where(section == 0, jnp.stack([mine, got]), jnp.stack([got, mine]))
    piece = enc_width // (2 * seq_size)
    kv_grad = by_section.reshape(2, CHUNKS, piece, 2, cols // CHUNKS)
    kv_grad = jnp.transpose(kv_grad, (3, 2, 0, 1, 4)).reshape(2, piece, local_cols)

    dq_other = swapped(own_dq, "section", 1)
    grads_in = [own_dq] + [swapped(own_dq, "seq", 2 * d) for d in range(1, outer)]
    weight_send, weight_keep = weight_part(place, columns_in, grads_in)
    weight_sum = weight_keep + swapped(weight_send, "seq", 1).astype(F32)
    mine = lax.dynamic_index_in_dim(weight_sum, section, 0, keepdims=False)
    theirs = lax.dynamic_index_in_dim(weight_sum, 1 - section, 0, keepdims=False)
    got = swapped(theirs.astype(BF16), "section", 1).astype(F32)
    query_grad = jnp.where(
        section == 0, jnp.concatenate([mine, got], 1), jnp.concatenate([got, mine], 1)
    )

    normed_keep, normed_send = normed_part(place, own_dq, dq_other, query_weight)
    feature_grad = normed_keep + swapped(normed_send, "mp", 1).astype(F32)
    quarter = feature_grad.shape[1]
    start_col = section * half_width + core * quarter
    gain_part = lax.dynamic_slice_in_dim(hidden_gain, start_col, quarter, 0).astype(F32)
    hidden_part = lax.dynamic_slice_in_dim(hidden, start_col, quarter, 1).astype(F32)
    scaled = gain_part * feature_grad
    row_dot = jnp.sum(scaled * hidden_part, axis=1)
    row_dot = row_dot + swapped(row_dot, "mp", 1)
    row_dot = (row_dot + swapped(row_dot, "section", 1))[:, None]
    norm_dot = row_dot[:, 0] / math.sqrt(model_width)
    hidden_grad = (inv_rms * scaled - hidden_part * inv_rms**3 * row_dot / model_width).astype(
        BF16
    )
    return (hidden_grad, query_grad, kv_grad, norm_dot)


def solution(mesh):
    placed = (
        P("seq", None),
        P(),
        P("seq", None, None),
        P(),
        P("section", "mp"),
        P(None, None, "mp"),
        P("seq", "mp"),
        P("seq", None),
        P("seq"),
    )
    return jax.shard_map(
        body,
        mesh=mesh,
        in_specs=placed,
        out_specs=(
            P("seq", ("section", "mp")),
            P(("section", "seq"), "mp"),
            P(None, ("section", "seq"), "mp"),
            P("seq"),
        ),
        check_vma=False,
    )
```

time: 590 us -> 123 us (0.21)
  waiting for transfers between devices: 501 us -> 22.3 us
  Pallas kernels: 0 us -> 37.8 us
  starting transfers between devices: 13.7 us -> 40.8 us
  matrix products: 21.8 us -> 0 us
  between operations: 14 us -> 1.02 us
  other arithmetic: 14.9 us -> 8.5 us
  local copies, waits for them, and re-layouts: 17.8 us -> 11.8 us
    ppermute x5 -> x25, waiting for transfers between devices: 277 us -> 22.3 us  [the longest x22 20.6 us: swapped(): return lax.ppermute(array, axis, [(i, i ^ mask) for i in range(size)])]
    reduce_scatter x3 -> x0, waiting for transfers between devices: 224 us -> none  [the longest x1 153 us: body(): lax.psum_scatter(lax.dot_general(part_cols, dq_use, (((0,), (0,)), ((), (...]
    pallas_call x0 -> x7, Pallas kernels: none -> 37.8 us  [the longest x2 14.1 us: attend(): pl.pallas_call(functools.partial(attend_kernel, last, ids.shape[1], count...]
    ppermute x5 -> x25, starting transfers between devices: 13.3 us -> 40.8 us  [the longest x22 34.7 us: swapped(): return lax.ppermute(array, axis, [(i, i ^ mask) for i in range(size)])]
    dot_general x4 -> x0, matrix products: 21.8 us -> none  [the longest x1 9.75 us: body(): jnp.einsum('tr,ktc->rkc', part_cols, dkv_use, preferred_element_type=jnp....]
    reshape x2 -> x3, local copies, waits for them, and re-layouts: 11.5 us -> 1.85 us  [the longest x1 1.13 us: body(): jnp.transpose(kv_grad, (3, 2, 0, 1, 4)).reshape(2, piece, local_cols)]
    unnamed x18 -> x30, local copies, waits for them, and re-layouts: 1.06 us -> 9.15 us
    convert_element_type x5 -> x3, other arithmetic: 7.03 us -> 0.76 us  [the longest x1 0.69 us: body(): lax.dynamic_slice_in_dim(hidden_gain, start_col, quarter, 0).astype(F32)]
  transfers between devices with their start and end apart: 8 -> 25, of which waited for: 5 -> 9; matrix products, arithmetic and copies ran while one was open for 7% -> 7% of each run, Pallas kernels for 0% -> 27%
where the time goes in v1:
time: 123 us; the launch traced here: 122 us
  starting transfers between devices  40.8 us (33%)
  Pallas kernels  37.8 us (31%)
  waiting for transfers between devices  22.3 us (18%)
  local copies, waits for them, and re-layouts  11.8 us (10%)
  other arithmetic  8.5 us (7%)
    ppermute x22, starting transfers between devices, swapped(): return lax.ppermute(array, axis, [(i, i ^ mask) for i in range(size)])  34.7 us
    ppermute x22, waiting for transfers between devices, swapped(): return lax.ppermute(array, axis, [(i, i ^ mask) for i in range(size)])  20.6 us
    pallas_call x2, Pallas kernels, attend(): pl.pallas_call(functools.partial(attend_kernel, last, ids.shape[1], count...  14.1 us
    pallas_call x1, Pallas kernels, pool_project(): pl.pallas_call(pool_kernel, grid_spec=pltpu.PrefetchScalarGridSpec(num_sc...  10.9 us
    unnamed x30, local copies, waits for them, and re-layouts  9.15 us
    pallas_call x1, Pallas kernels, query_part(): pl.pallas_call(functools.partial(query_kernel, step_count, lead), grid_sp...  4.75 us
    ppermute x1, starting transfers between devices, body(): lax.ppermute(dq_lead, 'seq', [(i, i + 1) for i in range(seq_size - 1)])  3.57 us
    pallas_call x1, Pallas kernels, normed_part(): pl.pallas_call(functools.partial(normed_kernel, step_count), grid_spec=pl...  3.3 us
  transfers between devices with their start and end apart: 25, of which 9 were waited for; matrix products, arithmetic and copies ran while one was open for 7% of the time, Pallas kernels for 27%

profile of v1, /device:TPU:0, one launch (start us, length us, event | category | flops | bytes accessed | tf_op | source)
XLA Modules:
  0.0 122.2 jit_solution(9223027019689594959)
XLA Ops:
  0.7 0.7 reshape.46.gain
  1.5 1.2 %copy-done.1 = bf16[128,4096]{1,0:T(8,128)(2,1)S(1)} copy-done((bf16[128,4096]{1,0:T(8,128)(2,1)S(1)}, bf16[128,4096]{1,0:T(8,128)(2,1)}, u32[]{:S(2)}) %copy-start.1) | copy-done | bytes 1048600
  2.7 0.9 copy-done.3
  3.6 4.7 %query_part.1 = (bf16[128,4096]{1,0:T(8,128)(2,1)S(1)}, f32[128,1]{1,0:T(8,128)S(1)}, f32[128,512]{1,0:T(8,128)S(1)}, bf16[128,512]{1,0:T(8,128)(2,1)S(1)}, bf16...) custom-call(s32[4]{0:T(128)S(1)} %pad_add_fusion.place, bf16[128,4096]{1,0:T(8,128)(2,1)S(1)} %copy-done.1, ...), custom_call_target="tpu_custom_call" | custom-call | flops 536870912 | bytes 6291456 | tf_op jit(solution)/shard_map/query_part/pallas_call | solution.py:100
  8.4 3.0 %collective-permute-start = (bf16[128,512]{1,0:T(8,128)(2,1)S(1)}, bf16[128,512]{1,0:T(8,128)(2,1)S(1)}, u32[]{:S(2)}, u32[]{:S(2)}) collective-permute-start(bf16[128,512]{1,0:T(8,128)(2,1)S(1)} %get-tuple-element.29), channel_id=1, source_target_pairs={{0,16},{16,0},{1,17},{17,1},{2,18},{18,2},{3,19},{19,3},{4,20},{20... | collective-permute-start | bytes 393224 | tf_op jit(solution)/shard_map/ppermute | solution.py:39
  11.4 1.3 %collective-permute-start.1 = (bf16[2,64,512]{2,1,0:T(8,128)(2,1)S(1)}, bf16[2,64,512]{2,1,0:T(8,128)(2,1)S(1)}, u32[]{:S(2)}, u32[]{:S(2)}) collective-permute-start(bf16[2,64,512]{2,1,0:T(8,128)(2,1)S(1)} %get-tuple-element.30), channel_id=1, source_target_pairs={{2,0},{4,2},{6,4},{8,6},{10,8},{12,10},{14,12},{3,1},{5,3},{7,5},{... | collective-permute-start | bytes 393224 | tf_op jit(solution)/shard_map/ppermute | solution.py:457
  12.7 1.3 %collective-permute-start.2 = (bf16[64,512]{1,0:T(8,128)(2,1)S(1)}, bf16[64,512]{1,0:T(8,128)(2,1)S(1)}, u32[]{:S(2)}, u32[]{:S(2)}) collective-permute-start(bf16[64,512]{1,0:T(8,128)(2,1)S(1)} %get-tuple-element.31), channel_id=1, source_target_pairs={{2,16},{4,18},{6,20},{8,22},{10,24},{12,26},{14,28},{18,0},{20,2},... | collective-permute-start | bytes 196616 | tf_op jit(solution)/shard_map/ppermute | solution.py:458
  14.0 1.8 %hidden_columns.1 = (bf16[1024,128]{1,0:T(8,128)(2,1)S(1)}, bf16[1024,128]{1,0:T(8,128)(2,1)}, bf16[1024,128]{1,0:T(8,128)(2,1)}, bf16[1024,128]{1,0:T(8,128)(2,1)}) custom-call(s32[4]{0:T(128)S(1)} %pad_add_fusion.place, bf16[128,4096]{1,0:T(8,128)(2,1)S(1)} %get-tuple-element.39.hn), custom_call_target="tpu_custom_call" | custom-call | bytes 2097152 | tf_op jit(solution)/shard_map/hidden_columns/pallas_call | solution.py:132
  15.8 0.7 copy-done.10
  16.5 6.7 %collective-permute-start.10 = (bf16[1024,128]{1,0:T(8,128)(2,1)}, bf16[1024,128]{1,0:T(8,128)(2,1)}, u32[]{:S(2)}, u32[]{:S(2)}) collective-permute-start(bf16[1024,128]{1,0:T(8,128)(2,1)} %get-tuple-element.43), channel_id=1, source_target_pairs={{0,12},{2,14},{4,8},{6,10},{8,4},{10,6},{12,0},{14,2},{1,13},{3,15... | collective-permute-start | bytes 786440 | tf_op jit(solution)/shard_map/ppermute | solution.py:39
  23.3 10.9 %pool_project.1 = (bf16[2,2048,512]{2,1,0:T(8,128)(2,1)}, bf16[896,2048]{1,0:T(8,128)(2,1)S(1)}) custom-call(s32[4]{0:T(128)S(1)} %pad_add_fusion.place, bf16[2048,896]{1,0:T(8,128)(2,1)} %bitcast.51, bf16[1,896]{1,0:T(2,128)(2,1)S(1)} %reshape.48.gain, bf16[2,896,1024]{2,1,0:T(8,128)(2,1)} %weight.4), custom_call_target="tpu_custom_call" | custom-call | flops 3758096384 | bytes 15728640 | tf_op jit(solution)/shard_map/pool_project/pallas_call | solution.py:163
  34.7 7.1 %attend_0.1 = (bf16[128,256]{1,0:T(8,128)(2,1)S(1)}, bf16[4,2,56,512]{3,2,1,0:T(8,128)(2,1)S(1)}, f32[4,2,56,512]{3,2,1,0:T(8,128)S(1)}) custom-call(s32[4]{0:T(128)S(1)} %pad_add_fusion.place, s32[2,16]{1,0:T(2,128)S(1)} %copy-done.12, s32[2]{0:T(128)S(1)} %copy-done.13, f32[128,512]{1,0:T(8,128)S(1)} %get-tuple-element.28.keep, ...), custom_call_target="tpu_custom_call" | custom-call | flops 2550136832 | bytes 8519680 | tf_op jit(solution)/shard_map/attend_0/pallas_call | solution.py:315
  41.8 0.8 copy-done.9
  42.6 7.0 %attend_1.1 = (bf16[128,512]{1,0:T(8,128)(2,1)S(1)}, bf16[64,512]{1,0:T(8,128)(2,1)S(1)}, bf16[4,2,56,512]{3,2,1,0:T(8,128)(2,1)S(1)}, f32[4,2,56,512]{3,2,1,0:T(8,128)S(1)}) custom-call(s32[4]{0:T(128)S(1)} %pad_add_fusion.place, s32[2,16]{1,0:T(2,128)S(1)} %copy-done.12, s32[2]{0:T(128)S(1)} %copy-done.13, f32[128,512]{1,0:T(8,128)S(1)} %get-tuple-element.28.keep, ...), custom_call_target="tpu_custom_call" | custom-call | flops 2550136832 | bytes 8519680 | tf_op jit(solution)/shard_map/attend_1/pallas_call | solution.py:315
  49.6 0.8 copy-done.8
  50.4 3.6 %collective-permute-start.3 = (bf16[64,512]{1,0:T(8,128)(2,1)S(1)}, bf16[64,512]{1,0:T(8,128)(2,1)S(1)}, u32[]{:S(2)}, u32[]{:S(2)}) collective-permute-start(bf16[64,512]{1,0:T(8,128)(2,1)S(1)} %get-tuple-element.35), channel_id=1, source_target_pairs={{0,2},{2,4},{4,6},{6,8},{8,10},{10,12},{12,14},{1,3},{3,5},{5,7},{... | collective-permute-start | bytes 196616 | tf_op jit(solution)/shard_map/ppermute | solution.py:495
  54.0 1.7 %collective-permute-done.3 = bf16[64,512]{1,0:T(8,128)(2,1)S(1)} collective-permute-done((bf16[64,512]{1,0:T(8,128)(2,1)S(1)}, bf16[64,512]{1,0:T(8,128)(2,1)S(1)}, u32[]{:S(2)}, u32[]{:S(2)}) %collective-permute-start.3) | collective-permute-done | bytes 65568 | tf_op jit(solution)/shard_map/ppermute | solution.py:495
  55.8 1.6 %collective-permute-start.4 = (bf16[128,512]{1,0:T(8,128)(2,1)S(1)}, bf16[128,512]{1,0:T(8,128)(2,1)S(1)}, u32[]{:S(2)}, u32[]{:S(2)}) collective-permute-start(bf16[128,512]{1,0:T(8,128)(2,1)S(1)} %pad_select_fusion.own.refs_4_), channel_id=1, source_target_pairs={{0,16},{16,0},{1,17},{17,1},{2,18},{18,2},{3,19},{19,3},{4,20},{20... | collective-permute-start | bytes 393224 | tf_op jit(solution)/shard_map/ppermute | solution.py:39
  57.3 2.4 %collective-permute-start.16 = (bf16[4,2,56,512]{3,2,1,0:T(8,128)(2,1)}, bf16[4,2,56,512]{3,2,1,0:T(8,128)(2,1)}, u32[]{:S(2)}, u32[]{:S(2)}) collective-permute-start(bf16[4,2,56,512]{3,2,1,0:T(8,128)(2,1)} %copy-done.9), channel_id=1, source_target_pairs={{0,2},{2,0},{4,6},{6,4},{8,10},{10,8},{12,14},{14,12},{1,3},{3,1},... | collective-permute-start | bytes 1376264 | tf_op jit(solution)/shard_map/ppermute | solution.py:39
  59.7 1.1 collective-permute-done.4.other
  61.5 3.2 %collective-permute-start.11 = (bf16[128,512]{1,0:T(8,128)(2,1)S(1)}, bf16[128,512]{1,0:T(8,128)(2,1)}, u32[]{:S(2)}, u32[]{:S(2)}) collective-permute-start(bf16[128,512]{1,0:T(8,128)(2,1)S(1)} %pad_select_fusion.own.refs_4_), channel_id=1, source_target_pairs={{0,4},{2,6},{4,0},{6,2},{8,12},{10,14},{12,8},{14,10},{1,5},{3,7},... | collective-permute-start | bytes 393224 | tf_op jit(solution)/shard_map/ppermute | solution.py:39
  64.7 2.2 %copy-done = bf16[2048,1024]{1,0:T(8,128)(2,1)S(1)} copy-done((bf16[2048,1024]{1,0:T(8,128)(2,1)S(1)}, bf16[2048,1024]{1,0:T(8,128)(2,1)}, u32[]{:S(2)}) %copy-start) | copy-done | bytes 4194328
  66.9 0.9 copy-done.6
  67.8 3.3 %normed_part.1 = (f32[128,1024]{1,0:T(8,128)S(1)}, bf16[128,1024]{1,0:T(8,128)(2,1)}) custom-call(s32[4]{0:T(128)S(1)} %pad_add_fusion.place, bf16[128,512]{1,0:T(8,128)(2,1)S(1)} %pad_select_fusion.own.refs_4_, bf16[128,512]{1,0:T(8,128)(2,1)S(1)} %copy-done.6, bf16[2048,1024]{1,0:T(8,128)(2,1)S(1)} %copy-done), custom_call_target="tpu_custom_call" | custom-call | flops 536870912 | bytes 4980736 | tf_op jit(solution)/shard_map/normed_part/pallas_call | solution.py:408
  71.1 2.9 %collective-permute-start.12 = (bf16[128,512]{1,0:T(8,128)(2,1)S(1)}, bf16[128,512]{1,0:T(8,128)(2,1)}, u32[]{:S(2)}, u32[]{:S(2)}) collective-permute-start(bf16[128,512]{1,0:T(8,128)(2,1)S(1)} %pad_select_fusion.own.refs_4_), channel_id=1, source_target_pairs={{0,8},{2,10},{4,12},{6,14},{8,0},{10,2},{12,4},{14,6},{1,9},{3,11}... | collective-permute-start | bytes 393224 | tf_op jit(solution)/shard_map/ppermute | solution.py:39
  74.1 0.7 dynamic-slice_convert_fusion.1
  74.8 0.9 fusion.20
  75.7 0.7 collective-permute-start.20
  76.4 2.3 %collective-permute-done.12.refs_6_ = bf16[128,512]{1,0:T(8,128)(2,1)} collective-permute-done((bf16[128,512]{1,0:T(8,128)(2,1)S(1)}, bf16[128,512]{1,0:T(8,128)(2,1)}, u32[]{:S(2)}, u32[]{:S(2)}) %collective-permute-start.12) | collective-permute-done | bytes 131104 | tf_op jit(solution)/shard_map/ppermute | solution.py:39
  78.7 2.3 %collective-permute-done.13.refs_7_ = bf16[128,512]{1,0:T(8,128)(2,1)} collective-permute-done((bf16[128,512]{1,0:T(8,128)(2,1)S(1)}, bf16[128,512]{1,0:T(8,128)(2,1)}, u32[]{:S(2)}, u32[]{:S(2)}) %collective-permute-start.13) | collective-permute-done | bytes 131104 | tf_op jit(solution)/shard_map/ppermute | solution.py:39
  81.0 0.9 copy-done.11
  81.9 3.0 %weight_part.1 = (bf16[2,256,512]{2,1,0:T(8,128)(2,1)S(1)}, f32[2,256,512]{2,1,0:T(8,128)S(1)}) custom-call(s32[4]{0:T(128)S(1)} %pad_add_fusion.place, bf16[1024,128]{1,0:T(8,128)(2,1)S(1)} %copy-done.11, bf16[1024,128]{1,0:T(8,128)(2,1)} %collective-permute-done.8.refs_1_, bf16[1024,128]{1,0:T(8,128)(2,1)} %collective-permute-done.9.refs_2_, ...), custom_call_target="tpu_custom_call" | custom-call | flops 536870912 | bytes 4194304 | tf_op jit(solution)/shard_map/weight_part/pallas_call | solution.py:364
  85.6 1.2 fusion.4
  86.8 1.2 fusion.21
  88.1 1.4 %collective-permute-start.17 = (bf16[2,56,512]{2,1,0:T(8,128)(2,1)S(1)}, bf16[2,56,512]{2,1,0:T(8,128)(2,1)S(1)}, u32[]{:S(2)}, u32[]{:S(2)}) collective-permute-start(bf16[2,56,512]{2,1,0:T(8,128)(2,1)S(1)} %get-tuple-element.58), channel_id=1, source_target_pairs={{0,4},{2,6},{4,0},{6,2},{8,12},{10,14},{12,8},{14,10},{1,5},{3,7},... | collective-permute-start | bytes 344072 | tf_op jit(solution)/shard_map/ppermute | solution.py:39
  89.5 1.0 collective-permute-start.18
  90.5 2.6 %collective-permute-start.19 = (bf16[2,56,512]{2,1,0:T(8,128)(2,1)S(1)}, bf16[2,56,512]{2,1,0:T(8,128)(2,1)S(1)}, u32[]{:S(2)}, u32[]{:S(2)}) collective-permute-start(bf16[2,56,512]{2,1,0:T(8,128)(2,1)S(1)} %get-tuple-element.59), channel_id=1, source_target_pairs={{0,12},{2,14},{4,8},{6,10},{8,4},{10,6},{12,0},{14,2},{1,13},{3,15... | collective-permute-start | bytes 344072 | tf_op jit(solution)/shard_map/ppermute | solution.py:39
  93.3 1.6 %collective-permute-start.7 = (f32[128]{0:T(128)S(1)}, f32[128]{0:T(128)S(1)}, u32[]{:S(2)}, u32[]{:S(2)}) collective-permute-start(f32[128]{0:T(128)S(1)} %add.65), channel_id=1, source_target_pairs={{0,16},{16,0},{1,17},{17,1},{2,18},{18,2},{3,19},{19,3},{4,20},{20... | collective-permute-start | bytes 1544 | tf_op jit(solution)/shard_map/ppermute | solution.py:39
  94.9 2.0 %collective-permute-done.7 = f32[128]{0:T(128)S(1)} collective-permute-done((f32[128]{0:T(128)S(1)}, f32[128]{0:T(128)S(1)}, u32[]{:S(2)}, u32[]{:S(2)}) %collective-permute-start.7) | collective-permute-done | bytes 544 | tf_op jit(solution)/shard_map/ppermute | solution.py:39
  97.4 1.9 %fusion.3 = bf16[128,1024]{1,0:T(8,128)(2,1)} fusion(f32[128,1024]{1,0:T(8,128)S(1)} %get-tuple-element.37, bf16[128,1024]{1,0:T(8,128)(2,1)} %collective-permute-done.5, f32[128]{0:T(128)S(1)} %get-tuple-element.53, f32[128]{0:T(128)S(1)} %get-tuple-element.51, f32[1024]{0:T(1024)S(1)} %dynamic-slice_convert_fusion.1, f32[128]{0:T(128)S(1)} %get-tuple-element.50, ...), kind=kLoop, calls=%fused_computation.13 | loop fusion | flops 1310720 | bytes 1316356 | tf_op jit(solution)/shard_map/convert_element_type | solution.py:537
  99.3 1.8 %collective-permute-start.22 = (bf16[2,56,512]{2,1,0:T(8,128)(2,1)S(1)}, bf16[2,56,512]{2,1,0:T(8,128)(2,1)S(1)}, u32[]{:S(2)}, u32[]{:S(2)}) collective-permute-start(bf16[2,56,512]{2,1,0:T(8,128)(2,1)S(1)} %get-tuple-element.63), channel_id=1, source_target_pairs={{0,8},{2,10},{4,12},{6,14},{8,0},{10,2},{12,4},{14,6},{1,9},{3,11}... | collective-permute-start | bytes 344072 | tf_op jit(solution)/shard_map/ppermute | solution.py:39
  101.4 2.3 %collective-permute-start.23 = (bf16[2,56,512]{2,1,0:T(8,128)(2,1)S(1)}, bf16[2,56,512]{2,1,0:T(8,128)(2,1)S(1)}, u32[]{:S(2)}, u32[]{:S(2)}) collective-permute-start(bf16[2,56,512]{2,1,0:T(8,128)(2,1)S(1)} %get-tuple-element.62), channel_id=1, source_target_pairs={{0,12},{2,14},{4,8},{6,10},{8,4},{10,6},{12,0},{14,2},{1,13},{3,15... | collective-permute-start | bytes 344072 | tf_op jit(solution)/shard_map/ppermute | solution.py:39
  103.8 7.4 %collective-permute-done.22 = bf16[2,56,512]{2,1,0:T(8,128)(2,1)S(1)} collective-permute-done((bf16[2,56,512]{2,1,0:T(8,128)(2,1)S(1)}, bf16[2,56,512]{2,1,0:T(8,128)(2,1)S(1)}, u32[]{:S(2)}, u32[]{:S(2)}) %collective-permute-start.22) | collective-permute-done | bytes 114720 | tf_op jit(solution)/shard_map/ppermute | solution.py:39
  111.3 1.6 %collective-permute-start.24 = (bf16[2,56,512]{2,1,0:T(8,128)(2,1)S(1)}, bf16[2,56,512]{2,1,0:T(8,128)(2,1)S(1)}, u32[]{:S(2)}, u32[]{:S(2)}) collective-permute-start(bf16[2,56,512]{2,1,0:T(8,128)(2,1)S(1)} %fusion.18), channel_id=1, source_target_pairs={{0,16},{16,0},{1,17},{17,1},{2,18},{18,2},{3,19},{19,3},{4,20},{20... | collective-permute-start | bytes 344072 | tf_op jit(solution)/shard_map/ppermute | solution.py:39
  113.8 3.5 %collective-permute-done.24 = bf16[2,56,512]{2,1,0:T(8,128)(2,1)S(1)} collective-permute-done((bf16[2,56,512]{2,1,0:T(8,128)(2,1)S(1)}, bf16[2,56,512]{2,1,0:T(8,128)(2,1)S(1)}, u32[]{:S(2)}, u32[]{:S(2)}) %collective-permute-start.24) | collective-permute-done | bytes 114720 | tf_op jit(solution)/shard_map/ppermute | solution.py:39
  118.0 1.1 reshape.49
  119.2 1.8 %collective-permute-done.15 = bf16[256,512]{1,0:T(8,128)(2,1)S(1)} collective-permute-done((bf16[256,512]{1,0:T(8,128)(2,1)S(1)}, bf16[256,512]{1,0:T(8,128)(2,1)S(1)}, u32[]{:S(2)}, u32[]{:S(2)}) %collective-permute-start.15) | collective-permute-done | bytes 262176 | tf_op jit(solution)/shard_map/ppermute | solution.py:39
  121.1 1.2 maximum_select_fusion
  (68 shorter events, 5.1 us)
Async XLA Ops:
  0.6 22.6 %copy-start.14 = (bf16[896]{0:T(1024)(128)(2,1)S(1)}, bf16[896]{0:T(1024)(128)(2,1)}, u32[]{:S(2)}) copy-start(bf16[896]{0:T(1024)(128)(2,1)} %param.12) | copy-start | bytes 5380
  1.5 1.2 %copy-start.1 = (bf16[128,4096]{1,0:T(8,128)(2,1)S(1)}, bf16[128,4096]{1,0:T(8,128)(2,1)}, u32[]{:S(2)}) copy-start(bf16[128,4096]{1,0:T(8,128)(2,1)} %hidden.1) | copy-start | bytes 3145732
  2.7 0.9 copy-start.3
  8.4 14.8 %copy-start.7 = (f32[128,1]{1,0:T(8,128)}, f32[128,1]{1,0:T(8,128)S(1)}, u32[]{:S(2)}) copy-start(f32[128,1]{1,0:T(8,128)S(1)} %get-tuple-element.27) | copy-start | bytes 1540
  8.4 26.3 %collective-permute-start = (bf16[128,512]{1,0:T(8,128)(2,1)S(1)}, bf16[128,512]{1,0:T(8,128)(2,1)S(1)}, u32[]{:S(2)}, u32[]{:S(2)}) collective-permute-start(bf16[128,512]{1,0:T(8,128)(2,1)S(1)} %get-tuple-element.29), channel_id=1, source_target_pairs={{0,16},{16,0},{1,17},{17,1},{2,18},{18,2},{3,19},{19,3},{4,20},{20... | collective-permute-start | bytes 393224 | tf_op jit(solution)/shard_map/ppermute | solution.py:39
  11.4 23.3 %collective-permute-start.1 = (bf16[2,64,512]{2,1,0:T(8,128)(2,1)S(1)}, bf16[2,64,512]{2,1,0:T(8,128)(2,1)S(1)}, u32[]{:S(2)}, u32[]{:S(2)}) collective-permute-start(bf16[2,64,512]{2,1,0:T(8,128)(2,1)S(1)} %get-tuple-element.30), channel_id=1, source_target_pairs={{2,0},{4,2},{6,4},{8,6},{10,8},{12,10},{14,12},{3,1},{5,3},{7,5},{... | collective-permute-start | bytes 393224 | tf_op jit(solution)/shard_map/ppermute | solution.py:457
  12.7 21.4 %collective-permute-start.2 = (bf16[64,512]{1,0:T(8,128)(2,1)S(1)}, bf16[64,512]{1,0:T(8,128)(2,1)S(1)}, u32[]{:S(2)}, u32[]{:S(2)}) collective-permute-start(bf16[64,512]{1,0:T(8,128)(2,1)S(1)} %get-tuple-element.31), channel_id=1, source_target_pairs={{2,16},{4,18},{6,20},{8,22},{10,24},{12,26},{14,28},{18,0},{20,2},... | collective-permute-start | bytes 196616 | tf_op jit(solution)/shard_map/ppermute | solution.py:458
  15.8 0.7 copy-start.10
  16.5 54.6 %collective-permute-start.10 = (bf16[1024,128]{1,0:T(8,128)(2,1)}, bf16[1024,128]{1,0:T(8,128)(2,1)}, u32[]{:S(2)}, u32[]{:S(2)}) collective-permute-start(bf16[1024,128]{1,0:T(8,128)(2,1)} %get-tuple-element.43), channel_id=1, source_target_pairs={{0,12},{2,14},{4,8},{6,10},{8,4},{10,6},{12,0},{14,2},{1,13},{3,15... | collective-permute-start | bytes 786440 | tf_op jit(solution)/shard_map/ppermute | solution.py:39
  23.2 50.8 %collective-permute-start.8 = (bf16[1024,128]{1,0:T(8,128)(2,1)}, bf16[1024,128]{1,0:T(8,128)(2,1)}, u32[]{:S(2)}, u32[]{:S(2)}) collective-permute-start(bf16[1024,128]{1,0:T(8,128)(2,1)} %get-tuple-element.41), channel_id=1, source_target_pairs={{0,4},{2,6},{4,0},{6,2},{8,12},{10,14},{12,8},{14,10},{1,5},{3,7},... | collective-permute-start | bytes 786440 | tf_op jit(solution)/shard_map/ppermute | solution.py:39
  23.2 11.5 %copy-start.4 = (bf16[128,1024]{1,0:T(8,128)(2,1)S(1)}, bf16[128,1024]{1,0:T(8,128)(2,1)}, u32[]{:S(2)}) copy-start(bf16[128,1024]{1,0:T(8,128)(2,1)} %grad_own.3) | copy-start | bytes 786436
  23.3 11.5 %copy-start.12 = (s32[2,16]{1,0:T(2,128)S(1)}, s32[2,16]{1,0:T(2,128)}, u32[]{:S(2)}) copy-start(s32[2,16]{1,0:T(2,128)} %ids.3) | copy-start | bytes 388
  23.3 11.5 %copy-start.13 = (s32[2]{0:T(128)S(1)}, s32[2]{0:T(128)}, u32[]{:S(2)}) copy-start(s32[2]{0:T(128)} %counts.3) | copy-start | bytes 28
  34.1 39.8 %collective-permute-start.9 = (bf16[1024,128]{1,0:T(8,128)(2,1)}, bf16[1024,128]{1,0:T(8,128)(2,1)}, u32[]{:S(2)}, u32[]{:S(2)}) collective-permute-start(bf16[1024,128]{1,0:T(8,128)(2,1)} %get-tuple-element.42), channel_id=1, source_target_pairs={{0,8},{2,10},{4,12},{6,14},{8,0},{10,2},{12,4},{14,6},{1,9},{3,11}... | collective-permute-start | bytes 786440 | tf_op jit(solution)/shard_map/ppermute | solution.py:39
  41.8 0.8 copy-start.9
  42.6 43.0 %copy-start.2 = (bf16[128,4096]{1,0:T(8,128)(2,1)S(1)}, bf16[128,4096]{1,0:T(8,128)(2,1)}, u32[]{:S(2)}) copy-start(bf16[128,4096]{1,0:T(8,128)(2,1)} %hidden.1) | copy-start | bytes 3145732
  49.6 0.8 copy-start.8
  50.4 5.3 %collective-permute-start.3 = (bf16[64,512]{1,0:T(8,128)(2,1)S(1)}, bf16[64,512]{1,0:T(8,128)(2,1)S(1)}, u32[]{:S(2)}, u32[]{:S(2)}) collective-permute-start(bf16[64,512]{1,0:T(8,128)(2,1)S(1)} %get-tuple-element.35), channel_id=1, source_target_pairs={{0,2},{2,4},{4,6},{6,8},{8,10},{10,12},{12,14},{1,3},{3,5},{5,7},{... | collective-permute-start | bytes 196616 | tf_op jit(solution)/shard_map/ppermute | solution.py:495
  55.8 5.0 %collective-permute-start.4 = (bf16[128,512]{1,0:T(8,128)(2,1)S(1)}, bf16[128,512]{1,0:T(8,128)(2,1)S(1)}, u32[]{:S(2)}, u32[]{:S(2)}) collective-permute-start(bf16[128,512]{1,0:T(8,128)(2,1)S(1)} %pad_select_fusion.own.refs_4_), channel_id=1, source_target_pairs={{0,16},{16,0},{1,17},{17,1},{2,18},{18,2},{3,19},{19,3},{4,20},{20... | collective-permute-start | bytes 393224 | tf_op jit(solution)/shard_map/ppermute | solution.py:39
  57.3 29.5 %collective-permute-start.16 = (bf16[4,2,56,512]{3,2,1,0:T(8,128)(2,1)}, bf16[4,2,56,512]{3,2,1,0:T(8,128)(2,1)}, u32[]{:S(2)}, u32[]{:S(2)}) collective-permute-start(bf16[4,2,56,512]{3,2,1,0:T(8,128)(2,1)} %copy-done.9), channel_id=1, source_target_pairs={{0,2},{2,0},{4,6},{6,4},{8,10},{10,8},{12,14},{14,12},{1,3},{3,1},... | collective-permute-start | bytes 1376264 | tf_op jit(solution)/shard_map/ppermute | solution.py:39
  60.8 0.7 copy-start.5
  61.5 14.3 %collective-permute-start.11 = (bf16[128,512]{1,0:T(8,128)(2,1)S(1)}, bf16[128,512]{1,0:T(8,128)(2,1)}, u32[]{:S(2)}, u32[]{:S(2)}) collective-permute-start(bf16[128,512]{1,0:T(8,128)(2,1)S(1)} %pad_select_fusion.own.refs_4_), channel_id=1, source_target_pairs={{0,4},{2,6},{4,0},{6,2},{8,12},{10,14},{12,8},{14,10},{1,5},{3,7},... | collective-permute-start | bytes 393224 | tf_op jit(solution)/shard_map/ppermute | solution.py:39
  64.7 2.2 %copy-start = (bf16[2048,1024]{1,0:T(8,128)(2,1)S(1)}, bf16[2048,1024]{1,0:T(8,128)(2,1)}, u32[]{:S(2)}) copy-start(bf16[2048,1024]{1,0:T(8,128)(2,1)} %weight.5) | copy-start | bytes 12582916
  66.9 0.9 copy-start.6
  71.1 7.6 %collective-permute-start.12 = (bf16[128,512]{1,0:T(8,128)(2,1)S(1)}, bf16[128,512]{1,0:T(8,128)(2,1)}, u32[]{:S(2)}, u32[]{:S(2)}) collective-permute-start(bf16[128,512]{1,0:T(8,128)(2,1)S(1)} %pad_select_fusion.own.refs_4_), channel_id=1, source_target_pairs={{0,8},{2,10},{4,12},{6,14},{8,0},{10,2},{12,4},{14,6},{1,9},{3,11}... | collective-permute-start | bytes 393224 | tf_op jit(solution)/shard_map/ppermute | solution.py:39
  74.0 7.0 %collective-permute-start.13 = (bf16[128,512]{1,0:T(8,128)(2,1)S(1)}, bf16[128,512]{1,0:T(8,128)(2,1)}, u32[]{:S(2)}, u32[]{:S(2)}) collective-permute-start(bf16[128,512]{1,0:T(8,128)(2,1)S(1)} %pad_select_fusion.own.refs_4_), channel_id=1, source_target_pairs={{0,12},{2,14},{4,8},{6,10},{8,4},{10,6},{12,0},{14,2},{1,13},{3,15... | collective-permute-start | bytes 393224 | tf_op jit(solution)/shard_map/ppermute | solution.py:39
  74.0 11.6 %collective-permute-start.5 = (bf16[128,1024]{1,0:T(8,128)(2,1)}, bf16[128,1024]{1,0:T(8,128)(2,1)}, u32[]{:S(2)}, u32[]{:S(2)}) collective-permute-start(bf16[128,1024]{1,0:T(8,128)(2,1)} %get-tuple-element.38), channel_id=1, source_target_pairs={{0,1},{1,0},{2,3},{3,2},{4,5},{5,4},{6,7},{7,6},{8,9},{9,8},{10,11... | collective-permute-start | bytes 786440 | tf_op jit(solution)/shard_map/ppermute | solution.py:39
  75.7 14.7 %collective-permute-start.20 = (bf16[4,2,56,512]{3,2,1,0:T(8,128)(2,1)}, bf16[4,2,56,512]{3,2,1,0:T(8,128)(2,1)S(1)}, u32[]{:S(2)}, u32[]{:S(2)}) collective-permute-start(bf16[4,2,56,512]{3,2,1,0:T(8,128)(2,1)} %copy-done.8), channel_id=1, source_target_pairs={{0,2},{2,0},{4,6},{6,4},{8,10},{10,8},{12,14},{14,12},{1,3},{3,1},... | collective-permute-start | bytes 1376264 | tf_op jit(solution)/shard_map/ppermute | solution.py:39
  81.0 1.0 copy-start.11
  84.9 27.9 %collective-permute-start.14 = (bf16[2,256,512]{2,1,0:T(8,128)(2,1)S(1)}, bf16[2,256,512]{2,1,0:T(8,128)(2,1)S(1)}, u32[]{:S(2)}, u32[]{:S(2)}) collective-permute-start(bf16[2,256,512]{2,1,0:T(8,128)(2,1)S(1)} %get-tuple-element.45), channel_id=1, source_target_pairs={{0,2},{2,0},{4,6},{6,4},{8,10},{10,8},{12,14},{14,12},{1,3},{3,1},... | collective-permute-start | bytes 1572872 | tf_op jit(solution)/shard_map/ppermute | solution.py:39
  86.8 6.5 %collective-permute-start.6 = (f32[128]{0:T(128)S(1)}, f32[128]{0:T(128)S(1)}, u32[]{:S(2)}, u32[]{:S(2)}) collective-permute-start(f32[128]{0:T(128)S(1)} %fusion.4), channel_id=1, source_target_pairs={{0,1},{1,0},{2,3},{3,2},{4,5},{5,4},{6,7},{7,6},{8,9},{9,8},{10,11... | collective-permute-start | bytes 1544 | tf_op jit(solution)/shard_map/ppermute | solution.py:39
  88.1 11.2 %collective-permute-start.17 = (bf16[2,56,512]{2,1,0:T(8,128)(2,1)S(1)}, bf16[2,56,512]{2,1,0:T(8,128)(2,1)S(1)}, u32[]{:S(2)}, u32[]{:S(2)}) collective-permute-start(bf16[2,56,512]{2,1,0:T(8,128)(2,1)S(1)} %get-tuple-element.58), channel_id=1, source_target_pairs={{0,4},{2,6},{4,0},{6,2},{8,12},{10,14},{12,8},{14,10},{1,5},{3,7},... | collective-permute-start | bytes 344072 | tf_op jit(solution)/shard_map/ppermute | solution.py:39
  89.5 11.9 %collective-permute-start.18 = (bf16[2,56,512]{2,1,0:T(8,128)(2,1)S(1)}, bf16[2,56,512]{2,1,0:T(8,128)(2,1)S(1)}, u32[]{:S(2)}, u32[]{:S(2)}) collective-permute-start(bf16[2,56,512]{2,1,0:T(8,128)(2,1)S(1)} %get-tuple-element.60), channel_id=1, source_target_pairs={{0,8},{2,10},{4,12},{6,14},{8,0},{10,2},{12,4},{14,6},{1,9},{3,11}... | collective-permute-start | bytes 344072 | tf_op jit(solution)/shard_map/ppermute | solution.py:39
  90.5 13.2 %collective-permute-start.19 = (bf16[2,56,512]{2,1,0:T(8,128)(2,1)S(1)}, bf16[2,56,512]{2,1,0:T(8,128)(2,1)S(1)}, u32[]{:S(2)}, u32[]{:S(2)}) collective-permute-start(bf16[2,56,512]{2,1,0:T(8,128)(2,1)S(1)} %get-tuple-element.59), channel_id=1, source_target_pairs={{0,12},{2,14},{4,8},{6,10},{8,4},{10,6},{12,0},{14,2},{1,13},{3,15... | collective-permute-start | bytes 344072 | tf_op jit(solution)/shard_map/ppermute | solution.py:39
  93.3 3.6 %collective-permute-start.7 = (f32[128]{0:T(128)S(1)}, f32[128]{0:T(128)S(1)}, u32[]{:S(2)}, u32[]{:S(2)}) collective-permute-start(f32[128]{0:T(128)S(1)} %add.65), channel_id=1, source_target_pairs={{0,16},{16,0},{1,17},{17,1},{2,18},{18,2},{3,19},{19,3},{4,20},{20... | collective-permute-start | bytes 1544 | tf_op jit(solution)/shard_map/ppermute | solution.py:39
  96.9 6.9 %collective-permute-start.21 = (bf16[2,56,512]{2,1,0:T(8,128)(2,1)S(1)}, bf16[2,56,512]{2,1,0:T(8,128)(2,1)S(1)}, u32[]{:S(2)}, u32[]{:S(2)}) collective-permute-start(bf16[2,56,512]{2,1,0:T(8,128)(2,1)S(1)} %get-tuple-element.61), channel_id=1, source_target_pairs={{0,4},{2,6},{4,0},{6,2},{8,12},{10,14},{12,8},{14,10},{1,5},{3,7},... | collective-permute-start | bytes 344072 | tf_op jit(solution)/shard_map/ppermute | solution.py:39
  99.3 11.9 %collective-permute-start.22 = (bf16[2,56,512]{2,1,0:T(8,128)(2,1)S(1)}, bf16[2,56,512]{2,1,0:T(8,128)(2,1)S(1)}, u32[]{:S(2)}, u32[]{:S(2)}) collective-permute-start(bf16[2,56,512]{2,1,0:T(8,128)(2,1)S(1)} %get-tuple-element.63), channel_id=1, source_target_pairs={{0,8},{2,10},{4,12},{6,14},{8,0},{10,2},{12,4},{14,6},{1,9},{3,11}... | collective-permute-start | bytes 344072 | tf_op jit(solution)/shard_map/ppermute | solution.py:39
  101.4 9.8 %collective-permute-start.23 = (bf16[2,56,512]{2,1,0:T(8,128)(2,1)S(1)}, bf16[2,56,512]{2,1,0:T(8,128)(2,1)S(1)}, u32[]{:S(2)}, u32[]{:S(2)}) collective-permute-start(bf16[2,56,512]{2,1,0:T(8,128)(2,1)S(1)} %get-tuple-element.62), channel_id=1, source_target_pairs={{0,12},{2,14},{4,8},{6,10},{8,4},{10,6},{12,0},{14,2},{1,13},{3,15... | collective-permute-start | bytes 344072 | tf_op jit(solution)/shard_map/ppermute | solution.py:39
  111.3 6.0 %collective-permute-start.24 = (bf16[2,56,512]{2,1,0:T(8,128)(2,1)S(1)}, bf16[2,56,512]{2,1,0:T(8,128)(2,1)S(1)}, u32[]{:S(2)}, u32[]{:S(2)}) collective-permute-start(bf16[2,56,512]{2,1,0:T(8,128)(2,1)S(1)} %fusion.18), channel_id=1, source_target_pairs={{0,16},{16,0},{1,17},{17,1},{2,18},{18,2},{3,19},{19,3},{4,20},{20... | collective-permute-start | bytes 344072 | tf_op jit(solution)/shard_map/ppermute | solution.py:39
  113.1 7.9 %collective-permute-start.15 = (bf16[256,512]{1,0:T(8,128)(2,1)S(1)}, bf16[256,512]{1,0:T(8,128)(2,1)S(1)}, u32[]{:S(2)}, u32[]{:S(2)}) collective-permute-start(bf16[256,512]{1,0:T(8,128)(2,1)S(1)} %fusion.6), channel_id=1, source_target_pairs={{0,16},{16,0},{1,17},{17,1},{2,18},{18,2},{3,19},{19,3},{4,20},{20... | collective-permute-start | bytes 786440 | tf_op jit(solution)/shard_map/ppermute | solution.py:39

commit v2 on v0

v2 whole, which is shorter than its diff:
```python
import functools
import math

import jax
import jax.numpy as jnp
from jax import lax
from jax.experimental import pallas as pl
from jax.experimental.pallas import tpu as pltpu
from jax.sharding import PartitionSpec as P

HD = 128
EPSILON = 1e-06
MASKED = -1e30
VMEM_BYTES = 24 * 1024 * 1024
QUERY_VMEM_BYTES = 56 * 1024 * 1024
CHUNKS = 2
FIRST_ATTEND_FLOPS = 20_000_000_000
STEPS = 4

F32 = jnp.float32
BF16 = jnp.bfloat16

IN_VMEM = pl.BlockSpec(memory_space=pltpu.VMEM)
IN_SMEM = pl.BlockSpec(memory_space=pltpu.SMEM)
IN_HBM = pl.BlockSpec(memory_space=pltpu.HBM)


def shape(dims, kind):
    return jax.ShapeDtypeStruct(dims, kind)


def call(
    kernel, name, out_shape, operands, in_specs=None, scratch=(), flops=0, limit=VMEM_BYTES
):
    return pl.pallas_call(
        kernel,
        in_specs=in_specs or [IN_VMEM] * len(operands),
        out_specs=[IN_VMEM] * len(out_shape),
        out_shape=out_shape,
        scratch_shapes=scratch,
        compiler_params=pltpu.CompilerParams(vmem_limit_bytes=limit),
        cost_estimate=pl.CostEstimate(flops=flops, bytes_accessed=0, transcendentals=0),
        name=name,
    )(*operands)


def nt_dot(left, right):
    return lax.dot_general(left, right, (((1,), (1,)), ((), ())), preferred_element_type=F32)


def swapped(array, axis, mask):
    size = lax.axis_size(axis)
    return lax.ppermute(array, axis, [(i, i ^ mask) for i in range(size)])


def after(value, *others):
    return lax.optimization_barrier((value, *others))[0]


def lanes_at(ref, start, size):
    return ref[:, pl.ds(pl.multiple_of(start, size), size)]


def split_column(column):
    high = column.astype(BF16).astype(F32)
    rest = column - high
    middle = rest.astype(BF16).astype(F32)
    low = rest - middle
    lane = lax.broadcasted_iota(jnp.int32, (column.shape[0], HD), 1)
    terms = jnp.where(lane == 0, high, jnp.where(lane == 1, middle, jnp.where(lane == 2, low, 0.0)))
    return terms.astype(BF16)


def joined_column(terms):
    return jnp.sum(terms.astype(F32), axis=1, keepdims=True)


def query_kernel(
    gain, hidden_hbm, weight_hbm, grad_hbm, hn_half, hn_lead, rms_out, keep_out, send_out, pair_out,
    cross_out, hidden_part, gain_part, hidden, hn_out, weight, total, gain_row, sems,
):
    section = lax.axis_index("section")
    core = lax.axis_index("mp")
    rows, width = hidden.shape
    half = width // 2
    quarter = hidden_part.shape[1]
    lead = cross_out.shape[0]
    depth = weight.shape[0] // STEPS
    cols = keep_out.shape[1]
    fetch = pltpu.make_async_copy(hidden_hbm, hidden, sems.at[STEPS])
    fetch.start()
    loads = []
    for step in range(STEPS):
        part = pl.ds(step * depth, depth)
        loads.append(pltpu.make_async_copy(weight_hbm.at[part], weight.at[part], sems.at[step]))
        loads[-1].start()
    grads = pltpu.make_async_copy(
        grad_hbm.at[pl.ds(0, lead), pl.ds(pl.multiple_of(section * cols, cols), cols)],
        pair_out.at[1],
        sems.at[STEPS + 1],
    )
    grads.start()
    gain_row[...] = gain[...].astype(F32).reshape(1, width)
    fetch.wait()
    wide = hidden[...].astype(F32)
    inv_rms = lax.rsqrt(jnp.mean(wide * wide, axis=1, keepdims=True) + EPSILON)
    rms_out[...] = inv_rms
    hn_out[...] = (wide * inv_rms * gain_row[...]).astype(BF16)
    hn_half[...] = lanes_at(hn_out, core * half, half)
    hn_lead[...] = hn_half[:lead]
    own = (2 * section + core) * quarter
    hidden_part[...] = lanes_at(hidden, own, quarter)
    gain_part[...] = lanes_at(gain_row, own, quarter)
    for step in range(STEPS):
        loads[step].wait()
        term = jnp.dot(
            lanes_at(hn_out, section * half + step * depth, depth),
            weight[step * depth : (step + 1) * depth],
            preferred_element_type=F32,
        )
        total[...] = term if step == 0 else total[...] + term
    keep_out[...] = lanes_at(total, section * cols, cols)
    send_out[...] = lanes_at(total, (1 - section) * cols, cols).astype(BF16)
    pair_out[0] = keep_out[:lead].astype(BF16)
    cross_out[...] = send_out[:lead]
    grads.wait()


def query_part(hidden, gain, weight, attn_grad, lead):
    rows, width = hidden.shape
    half, local = weight.shape
    cols = local // 2
    quarter = width // 4
    return call(
        query_kernel,
        "query_part",
        [
            shape((rows, half), BF16),
            shape((lead, half), BF16),
            shape((rows, 1), F32),
            shape((rows, cols), F32),
            shape((rows, cols), BF16),
            shape((2, lead, cols), BF16),
            shape((lead, cols), BF16),
            shape((rows, quarter), BF16),
            shape((1, quarter), F32),
        ],
        [gain, hidden, weight, attn_grad],
        [IN_VMEM, IN_HBM, IN_HBM, IN_HBM],
        [
            pltpu.VMEM((rows, width), BF16),
            pltpu.VMEM((rows, width), BF16),
            pltpu.VMEM((half, local), BF16),
            pltpu.VMEM((rows, local), F32),
            pltpu.VMEM((1, width), F32),
            pltpu.SemaphoreType.DMA((STEPS + 2,)),
        ],
        0,
        QUERY_VMEM_BYTES,
    )


def columns_kernel(count, offset, hn, led, *rest):
    *outs, turned = rest
    lead = led.shape[0]
    follow = lax.broadcasted_iota(jnp.int32, (lead, 1), 0) < offset
    turned[:, :lead] = jnp.where(follow, led[...], hn[:lead]).T
    turned[:, lead:] = hn[lead:].T
    span = outs[0].shape[0]
    outer = lax.axis_index("seq") // 2
    for step in range(count):
        start = pl.multiple_of((outer ^ step) * span, span)
        outs[step][...] = turned[pl.ds(start, span), :]


def columns_for(hn, led, count, offset):
    rows, half = hn.shape
    return call(
        functools.partial(columns_kernel, count, offset),
        "hidden_columns",
        [shape((half // count, rows), BF16)] * count,
        [hn, led],
        None,
        [pltpu.VMEM((half, rows), BF16)],
    )


def pool_kernel(gain, states, weight, kv_out, turned_out):
    rows, width = states.shape
    cols = kv_out.shape[2]
    block = min(rows, 1024)
    start = pl.multiple_of(lax.axis_index("section") * cols, cols)
    gain_row = gain[...].astype(F32).reshape(1, width)
    for base in range(0, rows, block):
        part = slice(base, base + block)
        wide = states[part].astype(F32)
        inv_rms = lax.rsqrt(jnp.mean(wide * wide, axis=1, keepdims=True) + EPSILON)
        normed = (wide * inv_rms * gain_row).astype(BF16)
        for which in range(2):
            kv_out[which, part] = jnp.dot(
                normed, weight[which, :, pl.ds(start, cols)], preferred_element_type=F32
            ).astype(BF16)
        turned_out[:, part] = normed.T


def pool_project(states, gain, weight):
    rows, width = states.shape
    cols = weight.shape[2] // 2
    return call(
        pool_kernel,
        "pool_project",
        [shape((2, rows, cols), BF16), shape((width, rows), BF16)],
        [gain, states, weight],
    )


def rows_at(ref, start, size):
    if size % 8 == 0:
        return ref[pl.ds(pl.multiple_of(start, 8), size), :]
    window = (size + 14) // 8 * 8
    rest = start % 8
    wide = ref[pl.ds(pl.multiple_of(start - rest, 8), window), :]
    return pltpu.roll(wide, window - rest, 0)[:size]


def attend_kernel(
    chunk, slot_count, ids, counts, keep, other, pair, cross, grad_own, kv, *rest
):
    last = chunk == CHUNKS - 1
    if chunk > 0:
        before, dots_before, *rest = rest
    dq_out, dots_out, *rest = rest
    if last:
        lead_out, *rest = rest
    turned_kv, bias = rest
    section = lax.axis_index("section")
    rows, all_cols = keep.shape
    cols = all_cols // CHUNKS
    left = chunk * cols
    here = slice(left, left + cols)
    lead = cross.shape[0]
    keys = kv.shape[1]
    block_count = counts.shape[0]
    block_len = rows // block_count
    offset = block_len - 1
    length = keys // slot_count
    factor = 1.0 / math.sqrt(HD)
    slot_of = lax.broadcasted_iota(jnp.int32, (1, keys), 1) // length
    for block in range(block_count):
        line = jnp.full((1, keys), MASKED, F32)
        for slot in range(slot_count):
            opened = jnp.where(slot < counts[block], ids[block, slot], -1)
            line = jnp.where(slot_of == opened, 0.0, line)
        bias[block * block_len : (block + 1) * block_len, :] = jnp.broadcast_to(
            line, (block_len, keys)
        )
    following = lax.broadcasted_iota(jnp.int32, (rows, 1), 0) < offset
    own = keep[:, here] + other[:, here].astype(F32)
    led = pair[0, :, here].astype(F32) + cross[:, here].astype(F32)
    padding = jnp.zeros((rows - lead, cols), F32)
    queries = jnp.where(following, jnp.concatenate([led, padding], 0), own)
    own = lanes_at(grad_own, section * all_cols + left, cols).astype(F32)
    led = pair[1, :, here].astype(F32)
    grads = jnp.where(following, jnp.concatenate([led, padding], 0), own)
    rolled_queries = pltpu.roll(queries, rows - offset, 0)
    rolled_grads = pltpu.roll(grads, rows - offset, 0)
    dots = dots_before[...] if chunk > 0 else jnp.zeros((rows, 1), F32)
    if chunk > 0:
        dq_out[:, :left] = before[...]
    for head in range(cols // HD):
        span = slice(head * HD, (head + 1) * HD)
        at = slice(left + head * HD, left + (head + 1) * HD)
        query = rolled_queries[:, span].astype(BF16)
        grad = rolled_grads[:, span].astype(BF16)
        key = kv[0, :, at]
        value = kv[1, :, at]
        scores = nt_dot(query, key) * factor + bias[...]
        peak = jnp.max(scores, axis=1, keepdims=True)
        weights = jnp.exp(scores - peak)
        norm = 1.0 / jnp.sum(weights, axis=1, keepdims=True)
        probs = weights * norm
        grad_probs = nt_dot(grad, value)
        delta = jnp.sum(probs * grad_probs, axis=1, keepdims=True)
        grad_scores = (probs * (grad_probs - delta) * factor).astype(BF16)
        dq = jnp.dot(grad_scores, key, preferred_element_type=F32)
        dq = pltpu.roll(dq, offset, 0).astype(BF16)
        dots = dots + jnp.sum(dq.astype(F32) * queries[:, span], axis=1, keepdims=True)
        dq_out[:, at] = dq
        turned_query = rolled_queries[:, span].T.astype(BF16)
        turned_grad = rolled_grads[:, span].T.astype(BF16)
        turned_kv[span, :] = jnp.dot(
            turned_query, grad_scores, preferred_element_type=F32
        ).astype(BF16)
        turned_kv[cols + head * HD : cols + (head + 1) * HD, :] = jnp.dot(
            turned_grad, probs.astype(BF16), preferred_element_type=F32
        ).astype(BF16)
    if last:
        dots_out[...] = split_column(dots)
        lead_out[:, :all_cols] = dq_out[:lead]
        lead_out[:, all_cols:] = dots_out[:lead]
    else:
        dots_out[...] = dots


def kv_part_kernel(count, turned, turned_kv, send_out, keep_out, product):
    outer, inner_own = lax.axis_index("seq") // 2, lax.axis_index("seq") % 2
    width = turned.shape[0]
    product[:width] = nt_dot(turned[...], turned_kv[...])
    piece = send_out.shape[2]
    half = width // 2
    for step in range(count):
        for part in range(2):
            for outs, inner in ((keep_out, inner_own), (send_out, 1 - inner_own)):
                start = part * half + (2 * (outer ^ step) + inner) * piece
                outs[step, part] = rows_at(product, start, piece).astype(outs.dtype)


def attend(chunk, ids, counts, keep, other, pair, cross, attn_grad, kv, before):
    rows, all_cols = keep.shape
    cols = all_cols // CHUNKS
    lead = cross.shape[0]
    keys = kv.shape[1]
    last = chunk == CHUNKS - 1
    operands = [ids, counts, keep, other, pair, cross, attn_grad, kv, *before]
    out_shape = [
        shape((rows, (chunk + 1) * cols), BF16),
        shape((rows, HD), BF16) if last else shape((rows, 1), F32),
    ]
    if last:
        out_shape.append(shape((lead, all_cols + HD), BF16))
    out_shape.append(shape((2 * cols, keys), BF16))
    return call(
        functools.partial(attend_kernel, chunk, ids.shape[1]),
        "attend_%d" % chunk,
        out_shape,
        operands,
        [IN_SMEM] * 2 + [IN_VMEM] * (len(operands) - 2),
        [pltpu.VMEM((rows, keys), F32)],
        0 if last else FIRST_ATTEND_FLOPS,
    )


def kv_part(chunk, turned, turned_kv):
    width = turned.shape[0]
    cols = turned_kv.shape[0]
    seq_size = lax.axis_size("seq")
    count = seq_size // 2
    dims = (count, 2, width // (2 * seq_size), cols)
    return call(
        functools.partial(kv_part_kernel, count),
        "kv_part_%d" % chunk,
        [shape(dims, BF16), shape(dims, F32)],
        [turned, turned_kv],
        None,
        [pltpu.VMEM((width + 16, cols), F32)],
    )


def own_kernel(offset, dq, dots, carried, out):
    lead = carried.shape[0]
    cols = dq.shape[1]
    early = lax.broadcasted_iota(jnp.int32, (lead, 1), 0) < offset
    out[:lead, :cols] = jnp.where(early, carried[:, :cols], dq[:lead])
    out[:lead, cols:] = jnp.where(early, carried[:, cols:], dots[:lead])
    out[lead:, :cols] = dq[lead:]
    out[lead:, cols:] = dots[lead:]


def fold_kernel(kept, received, keep_out, send_out):
    for place in range(keep_out.shape[0]):
        even, odd = 2 * place, 2 * place + 1
        keep_out[place] = kept[even] + received[even].astype(F32)
        send_out[place] = (kept[odd] + received[odd].astype(F32)).astype(BF16)


def fold(kept, received):
    count, *dims = kept.shape
    half = (count // 2, *dims)
    return call(fold_kernel, "fold", [shape(half, F32), shape(half, BF16)], [kept, received])


def outer_kernel(*refs):
    *refs, mine, theirs = refs
    section = lax.axis_index("section")
    for chunk in range(CHUNKS):
        kept, received = refs[2 * chunk : 2 * chunk + 2]
        for out, part in ((mine, section), (theirs, 1 - section)):
            out[chunk] = (kept[0, part] + received[0, part].astype(F32)).astype(out.dtype)


def outer_sums(parts):
    _, _, piece, cols = parts[0].shape
    return call(
        outer_kernel,
        "outer_sums",
        [shape((CHUNKS, piece, cols), F32), shape((CHUNKS, piece, cols), BF16)],
        parts,
    )


def kv_kernel(mine, got, out):
    section = lax.axis_index("section")
    cols = mine.shape[2] // 2
    for chunk in range(CHUNKS):
        for which in range(2):
            for source, part in ((mine, section), (got, 1 - section)):
                start = pl.multiple_of((part * CHUNKS + chunk) * cols, cols)
                out[which, :, pl.ds(start, cols)] = source[
                    chunk, :, which * cols : (which + 1) * cols
                ].astype(F32)


def weight_kernel(order, *refs):
    *refs, send_out, keep_out = refs
    count = len(order)
    mine, theirs, grads = refs[:count], refs[count : 2 * count], refs[2 * count :]
    inner_own = lax.axis_index("seq") % 2
    core = lax.axis_index("mp")
    piece = send_out.shape[1]
    gathered = [ref[index] for ref in grads for index in range(ref.shape[0])]
    for outs, inner in ((send_out, 1 - inner_own), (keep_out, inner_own)):
        rows = pl.ds(pl.multiple_of(inner * piece, piece), piece)
        for part in range(2):
            total = None
            for step, grad in zip(order, gathered):
                column = jnp.where(core == part, mine[step][rows, :], theirs[step][rows, :])
                term = jnp.dot(column, grad, preferred_element_type=F32)
                total = term if total is None else total + term
            outs[part] = total.astype(outs.dtype)


def weight_part(order, mine, theirs, grads):
    span = mine[0].shape[0]
    dims = (2, span // 2, grads[0].shape[2])
    return call(
        functools.partial(weight_kernel, order),
        "weight_part",
        [shape(dims, BF16), shape(dims, F32)],
        [*mine, *theirs, *grads],
    )


def stack_kernel(*refs):
    *refs, out = refs
    start = 0
    for ref in refs:
        out[start : start + ref.shape[0]] = ref[...]
        start += ref.shape[0]


def outer_gather(piece, count, ahead):
    stages, order = [piece], [0]
    bit = count // 2
    while bit:
        whole = stages[0]
        if len(stages) > 1:
            whole = call(
                stack_kernel,
                "stacked",
                [shape((len(order), *piece.shape[1:]), BF16)],
                [after(stages[0], *ahead), *stages[1:]],
            )[0]
        stages.append(swapped(whole, "seq", 2 * bit))
        order += [step ^ bit for step in order]
        bit //= 2
    return stages, order, whole


def weight_sum_kernel(kept, received, mine, theirs):
    section = lax.axis_index("section")
    mine[...] = kept[section] + received[section].astype(F32)
    theirs[...] = (kept[1 - section] + received[1 - section].astype(F32)).astype(BF16)


def side_kernel(mine, got, out):
    section = lax.axis_index("section")
    cols = mine.shape[1]
    out[:, pl.ds(pl.multiple_of(section * cols, cols), cols)] = mine[...]
    out[:, pl.ds(pl.multiple_of((1 - section) * cols, cols), cols)] = got[...].astype(F32)


def normed_kernel(own, other, weight, keep_out, send_out, dots_out, total):
    cols = own.shape[1] - HD
    swap = lax.axis_index("section") == 1
    core = lax.axis_index("mp")
    quarter = keep_out.shape[1]
    first = jnp.where(swap, other[:, :cols], own[:, :cols])
    second = jnp.where(swap, own[:, :cols], other[:, :cols])
    total[...] = nt_dot(first, weight[:, :cols]) + nt_dot(second, weight[:, cols:])
    keep_out[...] = lanes_at(total, core * quarter, quarter)
    send_out[:, :quarter] = lanes_at(total, (1 - core) * quarter, quarter).astype(BF16)
    dots = joined_column(own[:, cols:]) + joined_column(other[:, cols:])
    dots_out[...] = dots
    send_out[:, quarter:] = split_column(dots)


def normed_part(own, other, weight):
    rows = own.shape[0]
    half, local = weight.shape
    quarter = half // 2
    return call(
        normed_kernel,
        "normed_part",
        [shape((rows, quarter), F32), shape((rows, quarter + HD), BF16), shape((rows, 1), F32)],
        [own, other, weight],
        None,
        [pltpu.VMEM((rows, half), F32)],
    )


def hidden_kernel(width, kept, received, dots, hidden, gain, inv_rms, grad_out, dot_out):
    quarter = kept.shape[1]
    inv = inv_rms[...]
    row_dot = (dots[...] + joined_column(received[:, quarter:])) / inv
    wide = jnp.broadcast_to(row_dot * (1.0 / math.sqrt(width)), (row_dot.shape[0], HD))
    dot_out[...] = wide.T[:1]
    scaled = gain[...] * (kept[...] + received[:, :quarter].astype(F32))
    grad_out[...] = (
        inv * scaled - hidden[...].astype(F32) * (inv * inv * inv * row_dot * (1.0 / width))
    ).astype(BF16)


def body(
    hidden,
    hidden_gain,
    neighbour_states,
    encoder_gain,
    query_weight,
    kv_weight,
    attn_grad,
    neighbour_ids,
    valid_counts,
):
    seq_size = lax.axis_size("seq")
    outer = seq_size // 2
    row_count, model_width = hidden.shape
    local_cols = query_weight.shape[1]
    cols = local_cols // 2
    slot_total, nb_length, enc_width = neighbour_states.shape
    block_len = row_count // neighbour_ids.shape[0]
    offset = block_len - 1
    piece = enc_width // (2 * seq_size)
    backward = [(i, i - 1) for i in range(1, seq_size)]

    hn_half, hn_lead, inv_rms, keep, send, pair, cross, hidden_part, gain_part = query_part(
        hidden, hidden_gain, query_weight, attn_grad, block_len
    )
    other = swapped(send, "section", 1)
    pair_in = lax.ppermute(pair, "seq", backward)
    cross_in = lax.ppermute(
        cross,
        ("section", "seq"),
        [(s * seq_size + i, (1 - s) * seq_size + j) for s in range(2) for i, j in backward],
    )
    led = lax.ppermute(hn_lead, "seq", backward)
    kv, turned = pool_project(
        neighbour_states.reshape(slot_total * nb_length, enc_width), encoder_gain, kv_weight
    )

    def attention(chunk, ahead, before):
        return attend(
            chunk, neighbour_ids, valid_counts, after(keep, ahead), other, pair_in, cross_in,
            attn_grad, kv, before,
        )

    def outer_swap(pieces):
        return [swapped(piece, "seq", 2 * (step + 1)) for step, piece in enumerate(pieces)]

    *before, turned_kv = attention(0, turned, ())
    kv_send, kept_first = kv_part(0, turned, turned_kv)
    pair_first = swapped(kv_send, "seq", 1)
    columns = columns_for(hn_half, after(led, kept_first), outer, offset)
    columns_mine = [columns[0]] + outer_swap(columns[1:])
    dq, dots, dq_lead, turned_kv = attention(1, columns[0], before)
    kv_send, kept_second = kv_part(1, turned, turned_kv)
    dq = after(dq, kept_second)
    carried = lax.ppermute(dq_lead, "seq", [(i, i + 1) for i in range(seq_size - 1)])
    pair_second = swapped(kv_send, "seq", 1)
    columns_theirs = [swapped(column, "mp", 1) for column in columns_mine]
    gathered, order, stacked = outer_gather(dq[None], outer, (kept_second, *columns_theirs))

    own_dq = call(
        functools.partial(own_kernel, offset),
        "own_tokens",
        [shape((row_count, cols + HD), BF16)],
        [dq, after(dots, stacked), carried],
    )[0]
    dq_other = swapped(own_dq, "section", 1)

    def fold_on(kept, received, bit, ahead):
        kept, send = fold(after(kept, ahead), received)
        return kept, swapped(send, "seq", 2 * bit), 2 * bit

    def folded(kept, received, bit, ahead):
        while bit < outer:
            kept, received, bit = fold_on(kept, received, bit, ahead)
            ahead = kept
        return kept, received

    first = fold_on(kept_first, pair_first, 1, own_dq) if outer > 1 else (kept_first, pair_first, 1)
    normed_keep, normed_send, normed_dots = normed_part(
        own_dq, after(dq_other, first[0]), query_weight
    )
    normed_in = swapped(normed_send, "mp", 1)
    first = folded(*first, normed_dots)
    second = (kept_second, pair_second, 1)
    if outer > 1:
        second = fold_on(*second, first[0])

    columns_mine[0] = after(columns_mine[0], second[0])
    weight_send, weight_keep = weight_part(order, columns_mine, columns_theirs, gathered)
    weight_in = swapped(weight_send, "seq", 1)

    hidden_grad, norm_dot = call(
        functools.partial(hidden_kernel, model_width),
        "hidden_grad",
        [shape(hidden_part.shape, BF16), shape((1, row_count), F32)],
        [normed_keep, normed_in, after(normed_dots, weight_keep), hidden_part, gain_part, inv_rms],
    )

    second = folded(*second, norm_dot)

    weight_shape = weight_keep.shape[1:]
    mine, theirs = call(
        weight_sum_kernel,
        "weight_sum",
        [shape(weight_shape, F32), shape(weight_shape, BF16)],
        [after(weight_keep, second[0]), weight_in],
    )
    got = swapped(theirs, "section", 1)
    kv_mine, kv_theirs = outer_sums([after(first[0], mine), first[1], *second])
    kv_got = swapped(kv_theirs, "section", 1)

    query_grad = call(
        side_kernel, "query_grad", [shape((weight_shape[0], local_cols), F32)],
        [after(mine, kv_mine), got],
    )[0]
    kv_grad = call(
        kv_kernel, "kv_grad", [shape((2, piece, local_cols), F32)],
        [after(kv_mine, query_grad), kv_got],
    )[0]
    return (hidden_grad, query_grad, kv_grad, norm_dot.reshape(row_count))


def solution(mesh):
    placed = (
        P("seq", None),
        P(),
        P("seq", None, None),
        P(),
        P("section", "mp"),
        P(None, None, "mp"),
        P("seq", "mp"),
        P("seq", None),
        P("seq"),
    )
    return jax.shard_map(
        body,
        mesh=mesh,
        in_specs=placed,
        out_specs=(
            P("seq", ("section", "mp")),
            P(("section", "seq"), "mp"),
            P(None, ("section", "seq"), "mp"),
            P("seq"),
        ),
        check_vma=False,
    )
```

time: 590 us -> 102 us (0.17)
  waiting for transfers between devices: 501 us -> 37.8 us
  Pallas kernels: 0 us -> 28 us
  matrix products: 21.8 us -> 0 us
  starting transfers between devices: 13.7 us -> 33.2 us
  local copies, waits for them, and re-layouts: 17.8 us -> 2.08 us
  other arithmetic: 14.9 us -> 0 us
  between operations: 14 us -> 0.97 us
    ppermute x5 -> x25, waiting for transfers between devices: 277 us -> 37.8 us  [the longest x21 37.7 us: swapped(): return lax.ppermute(array, axis, [(i, i ^ mask) for i in range(size)])]
    reduce_scatter x3 -> x0, waiting for transfers between devices: 224 us -> none  [the longest x1 153 us: body(): lax.psum_scatter(lax.dot_general(part_cols, dq_use, (((0,), (0,)), ((), (...]
    pallas_call x0 -> x20, Pallas kernels: none -> 28 us  [call(): pl.pallas_call(kernel, in_specs=in_specs or [IN_VMEM] * len(operands), ou...]
    dot_general x4 -> x0, matrix products: 21.8 us -> none  [the longest x1 9.75 us: body(): jnp.einsum('tr,ktc->rkc', part_cols, dkv_use, preferred_element_type=jnp....]
    ppermute x5 -> x25, starting transfers between devices: 13.3 us -> 33.2 us  [the longest x21 26 us: swapped(): return lax.ppermute(array, axis, [(i, i ^ mask) for i in range(size)])]
    reshape x2 -> x0, local copies, waits for them, and re-layouts: 11.5 us -> none  [the longest x1 6.14 us: body(): pool_low = pool_normed.astype(jnp.bfloat16).reshape(pool_rows, enc_width)]
    convert_element_type x6 -> x0, other arithmetic: 8.94 us -> none  [the longest x1 4.74 us: body(): pool_low = pool_normed.astype(jnp.bfloat16).reshape(pool_rows, enc_width)]
  transfers between devices with their start and end apart: 8 -> 25, of which waited for: 5 -> 11; matrix products, arithmetic and copies ran while one was open for 7% -> 0% of each run, Pallas kernels for 0% -> 20%
where the time goes in v2:
time: 102 us
  waiting for transfers between devices  37.8 us (37%)
  starting transfers between devices  33.2 us (33%)
  Pallas kernels  28 us (27%)
  local copies, waits for them, and re-layouts  2.08 us (2%)
    ppermute x21, waiting for transfers between devices, swapped(): return lax.ppermute(array, axis, [(i, i ^ mask) for i in range(size)])  37.7 us
    pallas_call x20, Pallas kernels, call(): pl.pallas_call(kernel, in_specs=in_specs or [IN_VMEM] * len(operands), ou...  28 us
    ppermute x21, starting transfers between devices, swapped(): return lax.ppermute(array, axis, [(i, i ^ mask) for i in range(size)])  26 us
    ppermute x1, starting transfers between devices, body(): lax.ppermute(dq_lead, 'seq', [(i, i + 1) for i in range(seq_size - 1)])  3.31 us
    unnamed x24, local copies, waits for them, and re-layouts  2.08 us
  transfers between devices with their start and end apart: 25, of which 11 were waited for; matrix products, arithmetic and copies ran while one was open for 0% of the time, Pallas kernels for 20%

profile of v2, /device:TPU:0, one launch (start us, length us, event | category | flops | bytes accessed | tf_op | source)
XLA Modules:
  0.0 102.0 jit_solution(14382878878197897092)
XLA Ops:
  0.7 5.2 %query_part.1 = (bf16[128,2048]{1,0:T(8,128)(2,1)}, bf16[64,2048]{1,0:T(8,128)(2,1)}, f32[128,1]{1,0:T(8,128)}, f32[128,512]{1,0:T(8,128)}, bf16[128,512]{1,0:T(...) custom-call(bf16[4096]{0:T(1024)(128)(2,1)} %gain.2, ...), custom_call_target="tpu_custom_call" | custom-call | tf_op jit(solution)/shard_map/query_part/pallas_call | solution.py:35
  5.9 3.0 %collective-permute-start.1 = (bf16[128,512]{1,0:T(8,128)(2,1)}, bf16[128,512]{1,0:T(8,128)(2,1)S(1)}, u32[]{:S(2)}, u32[]{:S(2)}) collective-permute-start(bf16[128,512]{1,0:T(8,128)(2,1)} %get-tuple-element.71), channel_id=1, source_target_pairs={{0,16},{16,0},{1,17},{17,1},{2,18},{18,2},{3,19},{19,3},{4,20},{20... | collective-permute-start | bytes 393224 | tf_op jit(solution)/shard_map/ppermute | solution.py:53
  8.9 1.3 %collective-permute-start.2 = (bf16[2,64,512]{2,1,0:T(8,128)(2,1)}, bf16[2,64,512]{2,1,0:T(8,128)(2,1)S(1)}, u32[]{:S(2)}, u32[]{:S(2)}) collective-permute-start(bf16[2,64,512]{2,1,0:T(8,128)(2,1)} %get-tuple-element.72), channel_id=1, source_target_pairs={{2,0},{4,2},{6,4},{8,6},{10,8},{12,10},{14,12},{3,1},{5,3},{7,5},{... | collective-permute-start | bytes 393224 | tf_op jit(solution)/shard_map/ppermute | solution.py:549
  10.2 1.3 %collective-permute-start.3 = (bf16[64,512]{1,0:T(8,128)(2,1)}, bf16[64,512]{1,0:T(8,128)(2,1)S(1)}, u32[]{:S(2)}, u32[]{:S(2)}) collective-permute-start(bf16[64,512]{1,0:T(8,128)(2,1)} %get-tuple-element.73), channel_id=1, source_target_pairs={{2,16},{4,18},{6,20},{8,22},{10,24},{12,26},{14,28},{18,0},{20,2},... | collective-permute-start | bytes 196616 | tf_op jit(solution)/shard_map/ppermute | solution.py:550
  11.5 1.3 %collective-permute-start = (bf16[64,2048]{1,0:T(8,128)(2,1)}, bf16[64,2048]{1,0:T(8,128)(2,1)S(1)}, u32[]{:S(2)}, u32[]{:S(2)}) collective-permute-start(bf16[64,2048]{1,0:T(8,128)(2,1)} %get-tuple-element.68), channel_id=1, source_target_pairs={{2,0},{4,2},{6,4},{8,6},{10,8},{12,10},{14,12},{3,1},{5,3},{7,5},{... | collective-permute-start | bytes 786440 | tf_op jit(solution)/shard_map/ppermute | solution.py:555
  12.8 2.0 %copy-done.2 = bf16[2,896,1024]{2,1,0:T(8,128)(2,1)S(1)} copy-done((bf16[2,896,1024]{2,1,0:T(8,128)(2,1)S(1)}, bf16[2,896,1024]{2,1,0:T(8,128)(2,1)}, u32[]{:S(2)}) %copy-start.2) | copy-done | bytes 3670040
  14.9 5.3 %pool_project.1 = (bf16[2,2048,512]{2,1,0:T(8,128)(2,1)S(1)}, bf16[896,2048]{1,0:T(8,128)(2,1)S(1)}) custom-call(bf16[896]{0:T(1024)(128)(2,1)S(1)} %copy-done.9, bf16[2048,896]{1,0:T(8,128)(2,1)S(1)} %bitcast.3, bf16[2,896,1024]{2,1,0:T(8,128)(2,1)S(1)} %copy-done.2), custom_call_target="tpu_custom_call" | custom-call | tf_op jit(solution)/shard_map/pool_project/pallas_call | solution.py:35
  20.2 3.1 %attend_0.1 = (bf16[128,256]{1,0:T(8,128)(2,1)S(1)}, f32[128,1]{1,0:T(8,128)S(1)}, bf16[512,2048]{1,0:T(8,128)(2,1)S(1)}) custom-call(s32[2,16]{1,0:T(2,128)S(1)} %copy-done.10, s32[2]{0:T(128)S(1)} %copy-done.11, f32[128,512]{1,0:T(8,128)S(1)} %copy-done.6, bf16[128,512]{1,0:T(8,128)(2,1)S(1)} %collective-permute-done.1.other, ...), custom_call_target="tpu_custom_call" | custom-call | flops 20000000000 | tf_op jit(solution)/shard_map/attend_0/pallas_call | solution.py:35
  23.3 0.0 copy-start.4
  23.3 2.2 %kv_part_0.1 = (bf16[4,2,56,512]{3,2,1,0:T(8,128)(2,1)S(1)}, f32[4,2,56,512]{3,2,1,0:T(8,128)S(1)}) custom-call(bf16[896,2048]{1,0:T(8,128)(2,1)S(1)} %get-tuple-element.69.turned, bf16[512,2048]{1,0:T(8,128)(2,1)S(1)} %get-tuple-element.75.turned_kv), custom_call_target="tpu_custom_call" | custom-call | tf_op jit(solution)/shard_map/kv_part_0/pallas_call | solution.py:35
  25.6 4.0 %collective-permute-start.14 = (bf16[4,2,56,512]{3,2,1,0:T(8,128)(2,1)S(1)}, bf16[4,2,56,512]{3,2,1,0:T(8,128)(2,1)S(1)}, u32[]{:S(2)}, u32[]{:S(2)}) collective-permute-start(bf16[4,2,56,512]{3,2,1,0:T(8,128)(2,1)S(1)} %get-tuple-element.94), channel_id=1, source_target_pairs={{0,2},{2,0},{4,6},{6,4},{8,10},{10,8},{12,14},{14,12},{1,3},{3,1},... | collective-permute-start | bytes 1376264 | tf_op jit(solution)/shard_map/ppermute | solution.py:53
  29.5 0.7 hidden_columns.1
  30.2 3.0 %collective-permute-start.5 = (bf16[512,128]{1,0:T(8,128)(2,1)S(1)}, bf16[512,128]{1,0:T(8,128)(2,1)S(1)}, u32[]{:S(2)}, u32[]{:S(2)}) collective-permute-start(bf16[512,128]{1,0:T(8,128)(2,1)S(1)} %get-tuple-element.87), channel_id=1, source_target_pairs={{0,4},{2,6},{4,0},{6,2},{8,12},{10,14},{12,8},{14,10},{1,5},{3,7},... | collective-permute-start | bytes 393224 | tf_op jit(solution)/shard_map/ppermute | solution.py:53
  33.2 3.1 %collective-permute-start.7 = (bf16[512,128]{1,0:T(8,128)(2,1)S(1)}, bf16[512,128]{1,0:T(8,128)(2,1)S(1)}, u32[]{:S(2)}, u32[]{:S(2)}) collective-permute-start(bf16[512,128]{1,0:T(8,128)(2,1)S(1)} %get-tuple-element.88), channel_id=1, source_target_pairs={{0,8},{2,10},{4,12},{6,14},{8,0},{10,2},{12,4},{14,6},{1,9},{3,11}... | collective-permute-start | bytes 393224 | tf_op jit(solution)/shard_map/ppermute | solution.py:53
  36.3 1.2 %collective-permute-done.5.refs_1_ = bf16[512,128]{1,0:T(8,128)(2,1)S(1)} collective-permute-done((bf16[512,128]{1,0:T(8,128)(2,1)S(1)}, bf16[512,128]{1,0:T(8,128)(2,1)S(1)}, u32[]{:S(2)}, u32[]{:S(2)}) %collective-permute-start.5) | collective-permute-done | bytes 131104 | tf_op jit(solution)/shard_map/ppermute | solution.py:53
  37.5 3.1 %attend_1.1 = (bf16[128,512]{1,0:T(8,128)(2,1)S(1)}, bf16[128,128]{1,0:T(8,128)(2,1)S(1)}, bf16[64,640]{1,0:T(8,128)(2,1)S(1)}, bf16[512,2048]{1,0:T(8,128)(2,1)S(1)}) custom-call(s32[2,16]{1,0:T(2,128)S(1)} %copy-done.10, s32[2]{0:T(128)S(1)} %copy-done.11, f32[128,512]{1,0:T(8,128)S(1)} %copy-done.6, bf16[128,512]{1,0:T(8,128)(2,1)S(1)} %collective-permute-done.1.other, ...), custom_call_target="tpu_custom_call" | custom-call | tf_op jit(solution)/shard_map/attend_1/pallas_call | solution.py:35
  40.6 2.4 %kv_part_1.1 = (bf16[4,2,56,512]{3,2,1,0:T(8,128)(2,1)S(1)}, f32[4,2,56,512]{3,2,1,0:T(8,128)S(1)}) custom-call(bf16[896,2048]{1,0:T(8,128)(2,1)S(1)} %get-tuple-element.69.turned, bf16[512,2048]{1,0:T(8,128)(2,1)S(1)} %get-tuple-element.83.turned_kv), custom_call_target="tpu_custom_call" | custom-call | tf_op jit(solution)/shard_map/kv_part_1/pallas_call | solution.py:35
  43.0 2.1 %collective-permute-done.7.refs_2_ = bf16[512,128]{1,0:T(8,128)(2,1)S(1)} collective-permute-done((bf16[512,128]{1,0:T(8,128)(2,1)S(1)}, bf16[512,128]{1,0:T(8,128)(2,1)S(1)}, u32[]{:S(2)}, u32[]{:S(2)}) %collective-permute-start.7) | collective-permute-done | bytes 131104 | tf_op jit(solution)/shard_map/ppermute | solution.py:53
  45.1 1.3 %collective-permute-start.17 = (bf16[4,2,56,512]{3,2,1,0:T(8,128)(2,1)S(1)}, bf16[4,2,56,512]{3,2,1,0:T(8,128)(2,1)S(1)}, u32[]{:S(2)}, u32[]{:S(2)}) collective-permute-start(bf16[4,2,56,512]{3,2,1,0:T(8,128)(2,1)S(1)} %get-tuple-element.104), channel_id=1, source_target_pairs={{0,2},{2,0},{4,6},{6,4},{8,10},{10,8},{12,14},{14,12},{1,3},{3,1},... | collective-permute-start | bytes 1376264 | tf_op jit(solution)/shard_map/ppermute | solution.py:53
  46.5 0.5 collective-permute-start.10
  47.0 1.7 %collective-permute-start.11 = (bf16[1,128,512]{2,1,0:T(8,128)(2,1)S(1)}, bf16[1,128,512]{2,1,0:T(8,128)(2,1)S(1)}, u32[]{:S(2)}, u32[]{:S(2)}) collective-permute-start(bf16[1,128,512]{2,1,0:T(8,128)(2,1)S(1)} %bitcast.4), channel_id=1, source_target_pairs={{0,8},{2,10},{4,12},{6,14},{8,0},{10,2},{12,4},{14,6},{1,9},{3,11}... | collective-permute-start | bytes 393224 | tf_op jit(solution)/shard_map/ppermute | solution.py:53
  48.7 3.3 %collective-permute-start.12 = (bf16[64,640]{1,0:T(8,128)(2,1)S(1)}, bf16[64,640]{1,0:T(8,128)(2,1)S(1)}, u32[]{:S(2)}, u32[]{:S(2)}) collective-permute-start(bf16[64,640]{1,0:T(8,128)(2,1)S(1)} %get-tuple-element.92), channel_id=1, source_target_pairs={{0,2},{2,4},{4,6},{6,8},{8,10},{10,12},{12,14},{1,3},{3,5},{5,7},{... | collective-permute-start | bytes 245768 | tf_op jit(solution)/shard_map/ppermute | solution.py:577
  52.0 4.1 %collective-permute-done.11.refs_1_.refs_9_ = bf16[1,128,512]{2,1,0:T(8,128)(2,1)S(1)} collective-permute-done((bf16[1,128,512]{2,1,0:T(8,128)(2,1)S(1)}, bf16[1,128,512]{2,1,0:T(8,128)(2,1)S(1)}, u32[]{:S(2)}, u32[]{:S(2)}) %collective-permute-start.11) | collective-permute-done | bytes 131104 | tf_op jit(solution)/shard_map/ppermute | solution.py:53
  56.2 0.1 collective-permute-start.18
  56.3 0.1 fold.4
  56.4 2.1 %collective-permute-start.16 = (bf16[2,2,56,512]{3,2,1,0:T(8,128)(2,1)S(1)}, bf16[2,2,56,512]{3,2,1,0:T(8,128)(2,1)S(1)}, u32[]{:S(2)}, u32[]{:S(2)}) collective-permute-start(bf16[2,2,56,512]{3,2,1,0:T(8,128)(2,1)S(1)} %get-tuple-element.101), channel_id=1, source_target_pairs={{0,4},{2,6},{4,0},{6,2},{8,12},{10,14},{12,8},{14,10},{1,5},{3,7},... | collective-permute-start | bytes 688136 | tf_op jit(solution)/shard_map/ppermute | solution.py:53
  58.5 1.5 %collective-permute-start.13 = (bf16[128,640]{1,0:T(8,128)(2,1)S(1)}, bf16[128,640]{1,0:T(8,128)(2,1)S(1)}, u32[]{:S(2)}, u32[]{:S(2)}) collective-permute-start(bf16[128,640]{1,0:T(8,128)(2,1)S(1)} %own_tokens.1.own), channel_id=1, source_target_pairs={{0,16},{16,0},{1,17},{17,1},{2,18},{18,2},{3,19},{19,3},{4,20},{20... | collective-permute-start | bytes 491528 | tf_op jit(solution)/shard_map/ppermute | solution.py:53
  60.0 3.8 %collective-permute-done.13.other = bf16[128,640]{1,0:T(8,128)(2,1)S(1)} collective-permute-done((bf16[128,640]{1,0:T(8,128)(2,1)S(1)}, bf16[128,640]{1,0:T(8,128)(2,1)S(1)}, u32[]{:S(2)}, u32[]{:S(2)}) %collective-permute-start.13) | collective-permute-done | bytes 163872 | tf_op jit(solution)/shard_map/ppermute | solution.py:53
  63.8 1.6 %normed_part.1 = (f32[128,1024]{1,0:T(8,128)S(1)}, bf16[128,1152]{1,0:T(8,128)(2,1)S(1)}, f32[128,1]{1,0:T(8,128)S(1)}) custom-call(bf16[128,640]{1,0:T(8,128)(2,1)S(1)} %own_tokens.1.own, bf16[128,640]{1,0:T(8,128)(2,1)S(1)} %collective-permute-done.13.other, bf16[2048,1024]{1,0:T(8,128)(2,1)S(1)} %copy-done), custom_call_target="tpu_custom_call" | custom-call | tf_op jit(solution)/shard_map/normed_part/pallas_call | solution.py:35
  65.4 3.7 %collective-permute-done.16.received = bf16[2,2,56,512]{3,2,1,0:T(8,128)(2,1)S(1)} collective-permute-done((bf16[2,2,56,512]{3,2,1,0:T(8,128)(2,1)S(1)}, bf16[2,2,56,512]{3,2,1,0:T(8,128)(2,1)S(1)}, u32[]{:S(2)}, u32[]{:S(2)}) %collective-permute-start.16) | collective-permute-done | bytes 229408 | tf_op jit(solution)/shard_map/ppermute | solution.py:53
  69.1 0.1 fold.6
  69.2 1.2 %weight_part.1 = (bf16[2,256,512]{2,1,0:T(8,128)(2,1)S(1)}, f32[2,256,512]{2,1,0:T(8,128)S(1)}) custom-call(bf16[512,128]{1,0:T(8,128)(2,1)S(1)} %get-tuple-element.106.refs_0_, bf16[512,128]{1,0:T(8,128)(2,1)S(1)} %collective-permute-done.5.refs_1_, bf16[512,128]{1,0:T(8,128)(2,1)S(1)} %collective-permute-done.7.refs_2_, ...), custom_call_target="tpu_custom_call" | custom-call | tf_op jit(solution)/shard_map/weight_part/pallas_call | solution.py:35
  70.5 0.4 collective-permute-start.20
  70.9 0.3 collective-permute-start.19
  71.2 1.3 %collective-permute-done.15.received = bf16[128,1152]{1,0:T(8,128)(2,1)S(1)} collective-permute-done((bf16[128,1152]{1,0:T(8,128)(2,1)S(1)}, bf16[128,1152]{1,0:T(8,128)(2,1)S(1)}, u32[]{:S(2)}, u32[]{:S(2)}) %collective-permute-start.15) | collective-permute-done | bytes 294944 | tf_op jit(solution)/shard_map/ppermute | solution.py:53
  72.5 1.0 hidden_grad.1
  73.4 5.5 %collective-permute-done.19.received = bf16[2,2,56,512]{3,2,1,0:T(8,128)(2,1)S(1)} collective-permute-done((bf16[2,2,56,512]{3,2,1,0:T(8,128)(2,1)S(1)}, bf16[2,2,56,512]{3,2,1,0:T(8,128)(2,1)S(1)}, u32[]{:S(2)}, u32[]{:S(2)}) %collective-permute-start.19) | collective-permute-done | bytes 229408 | tf_op jit(solution)/shard_map/ppermute | solution.py:53
  78.9 4.3 %collective-permute-done.20.received = bf16[2,256,512]{2,1,0:T(8,128)(2,1)S(1)} collective-permute-done((bf16[2,256,512]{2,1,0:T(8,128)(2,1)S(1)}, bf16[2,256,512]{2,1,0:T(8,128)(2,1)S(1)}, u32[]{:S(2)}, u32[]{:S(2)}) %collective-permute-start.20) | collective-permute-done | bytes 524320 | tf_op jit(solution)/shard_map/ppermute | solution.py:53
  83.2 0.1 weight_sum.1
  83.3 1.6 %collective-permute-start.23 = (bf16[256,512]{1,0:T(8,128)(2,1)S(1)}, bf16[256,512]{1,0:T(8,128)(2,1)S(1)}, u32[]{:S(2)}, u32[]{:S(2)}) collective-permute-start(bf16[256,512]{1,0:T(8,128)(2,1)S(1)} %get-tuple-element.125), channel_id=1, source_target_pairs={{0,16},{16,0},{1,17},{17,1},{2,18},{18,2},{3,19},{19,3},{4,20},{20... | collective-permute-start | bytes 786440 | tf_op jit(solution)/shard_map/ppermute | solution.py:53
  84.9 2.4 %collective-permute-start.21 = (bf16[1,2,56,512]{3,2,1,0:T(8,128)(2,1)S(1)}, bf16[1,2,56,512]{3,2,1,0:T(8,128)(2,1)S(1)}, u32[]{:S(2)}, u32[]{:S(2)}) collective-permute-start(bf16[1,2,56,512]{3,2,1,0:T(8,128)(2,1)S(1)} %get-tuple-element.121), channel_id=1, source_target_pairs={{0,8},{2,10},{4,12},{6,14},{8,0},{10,2},{12,4},{14,6},{1,9},{3,11}... | collective-permute-start | bytes 344072 | tf_op jit(solution)/shard_map/ppermute | solution.py:53
  87.3 0.5 collective-permute-start.22
  87.8 7.3 %collective-permute-done.21.refs_1_ = bf16[1,2,56,512]{3,2,1,0:T(8,128)(2,1)S(1)} collective-permute-done((bf16[1,2,56,512]{3,2,1,0:T(8,128)(2,1)S(1)}, bf16[1,2,56,512]{3,2,1,0:T(8,128)(2,1)S(1)}, u32[]{:S(2)}, u32[]{:S(2)}) %collective-permute-start.21) | collective-permute-done | bytes 114720 | tf_op jit(solution)/shard_map/ppermute | solution.py:53
  95.1 1.2 %collective-permute-done.22.refs_3_ = bf16[1,2,56,512]{3,2,1,0:T(8,128)(2,1)S(1)} collective-permute-done((bf16[1,2,56,512]{3,2,1,0:T(8,128)(2,1)S(1)}, bf16[1,2,56,512]{3,2,1,0:T(8,128)(2,1)S(1)}, u32[]{:S(2)}, u32[]{:S(2)}) %collective-permute-start.22) | collective-permute-done | bytes 114720 | tf_op jit(solution)/shard_map/ppermute | solution.py:53
  96.4 0.6 collective-permute-start.24
  97.0 1.0 %query_grad.1 = f32[256,1024]{1,0:T(8,128)} custom-call(f32[256,512]{1,0:T(8,128)S(1)} %get-tuple-element.124.mine, bf16[256,512]{1,0:T(8,128)(2,1)S(1)} %collective-permute-done.23.got), custom_call_target="tpu_custom_call" | custom-call | tf_op jit(solution)/shard_map/query_grad/pallas_call | solution.py:35
  98.0 3.2 %collective-permute-done.24.got = bf16[2,56,512]{2,1,0:T(8,128)(2,1)S(1)} collective-permute-done((bf16[2,56,512]{2,1,0:T(8,128)(2,1)S(1)}, bf16[2,56,512]{2,1,0:T(8,128)(2,1)S(1)}, u32[]{:S(2)}, u32[]{:S(2)}) %collective-permute-start.24) | collective-permute-done | bytes 114720 | tf_op jit(solution)/shard_map/ppermute | solution.py:53
  101.2 0.8 kv_grad.1
  (46 shorter events, 0.3 us)
Async XLA Ops:
  0.6 12.2 %copy-start.9 = (bf16[896]{0:T(1024)(128)(2,1)S(1)}, bf16[896]{0:T(1024)(128)(2,1)}, u32[]{:S(2)}) copy-start(bf16[896]{0:T(1024)(128)(2,1)} %gain.3) | copy-start | bytes 5380
  0.6 12.2 %copy-start.1 = (bf16[16,128,896]{2,1,0:T(8,128)(2,1)S(1)}, bf16[16,128,896]{2,1,0:T(8,128)(2,1)}, u32[]{:S(2)}) copy-start(bf16[16,128,896]{2,1,0:T(8,128)(2,1)} %param.11) | copy-start | bytes 11010052
  5.9 14.3 %collective-permute-start.1 = (bf16[128,512]{1,0:T(8,128)(2,1)}, bf16[128,512]{1,0:T(8,128)(2,1)S(1)}, u32[]{:S(2)}, u32[]{:S(2)}) collective-permute-start(bf16[128,512]{1,0:T(8,128)(2,1)} %get-tuple-element.71), channel_id=1, source_target_pairs={{0,16},{16,0},{1,17},{17,1},{2,18},{18,2},{3,19},{19,3},{4,20},{20... | collective-permute-start | bytes 393224 | tf_op jit(solution)/shard_map/ppermute | solution.py:53
  8.9 11.3 %collective-permute-start.2 = (bf16[2,64,512]{2,1,0:T(8,128)(2,1)}, bf16[2,64,512]{2,1,0:T(8,128)(2,1)S(1)}, u32[]{:S(2)}, u32[]{:S(2)}) collective-permute-start(bf16[2,64,512]{2,1,0:T(8,128)(2,1)} %get-tuple-element.72), channel_id=1, source_target_pairs={{2,0},{4,2},{6,4},{8,6},{10,8},{12,10},{14,12},{3,1},{5,3},{7,5},{... | collective-permute-start | bytes 393224 | tf_op jit(solution)/shard_map/ppermute | solution.py:549
  10.2 10.0 %collective-permute-start.3 = (bf16[64,512]{1,0:T(8,128)(2,1)}, bf16[64,512]{1,0:T(8,128)(2,1)S(1)}, u32[]{:S(2)}, u32[]{:S(2)}) collective-permute-start(bf16[64,512]{1,0:T(8,128)(2,1)} %get-tuple-element.73), channel_id=1, source_target_pairs={{2,16},{4,18},{6,20},{8,22},{10,24},{12,26},{14,28},{18,0},{20,2},... | collective-permute-start | bytes 196616 | tf_op jit(solution)/shard_map/ppermute | solution.py:550
  11.5 18.0 %collective-permute-start = (bf16[64,2048]{1,0:T(8,128)(2,1)}, bf16[64,2048]{1,0:T(8,128)(2,1)S(1)}, u32[]{:S(2)}, u32[]{:S(2)}) collective-permute-start(bf16[64,2048]{1,0:T(8,128)(2,1)} %get-tuple-element.68), channel_id=1, source_target_pairs={{2,0},{4,2},{6,4},{8,6},{10,8},{12,10},{14,12},{3,1},{5,3},{7,5},{... | collective-permute-start | bytes 786440 | tf_op jit(solution)/shard_map/ppermute | solution.py:555
  12.8 2.0 %copy-start.2 = (bf16[2,896,1024]{2,1,0:T(8,128)(2,1)S(1)}, bf16[2,896,1024]{2,1,0:T(8,128)(2,1)}, u32[]{:S(2)}) copy-start(bf16[2,896,1024]{2,1,0:T(8,128)(2,1)} %weight.2) | copy-start | bytes 11010052
  14.9 5.3 %copy-start.3 = (bf16[128,1024]{1,0:T(8,128)(2,1)S(1)}, bf16[128,1024]{1,0:T(8,128)(2,1)}, u32[]{:S(2)}) copy-start(bf16[128,1024]{1,0:T(8,128)(2,1)} %grad_own.3) | copy-start | bytes 786436
  14.9 5.3 %copy-start.6 = (f32[128,512]{1,0:T(8,128)S(1)}, f32[128,512]{1,0:T(8,128)}, u32[]{:S(2)}) copy-start(f32[128,512]{1,0:T(8,128)} %get-tuple-element.79.keep) | copy-start | bytes 786436
  14.9 5.3 %copy-start.10 = (s32[2,16]{1,0:T(2,128)S(1)}, s32[2,16]{1,0:T(2,128)}, u32[]{:S(2)}) copy-start(s32[2,16]{1,0:T(2,128)} %ids.3) | copy-start | bytes 388
  14.9 5.4 %copy-start.11 = (s32[2]{0:T(128)S(1)}, s32[2]{0:T(128)}, u32[]{:S(2)}) copy-start(s32[2]{0:T(128)} %counts.3) | copy-start | bytes 28
  23.3 6.2 %copy-start.4 = (bf16[128,2048]{1,0:T(8,128)(2,1)S(1)}, bf16[128,2048]{1,0:T(8,128)(2,1)}, u32[]{:S(2)}) copy-start(bf16[128,2048]{1,0:T(8,128)(2,1)} %get-tuple-element.67.hn) | copy-start | bytes 1572868
  25.6 30.7 %collective-permute-start.14 = (bf16[4,2,56,512]{3,2,1,0:T(8,128)(2,1)S(1)}, bf16[4,2,56,512]{3,2,1,0:T(8,128)(2,1)S(1)}, u32[]{:S(2)}, u32[]{:S(2)}) collective-permute-start(bf16[4,2,56,512]{3,2,1,0:T(8,128)(2,1)S(1)} %get-tuple-element.94), channel_id=1, source_target_pairs={{0,2},{2,0},{4,6},{6,4},{8,10},{10,8},{12,14},{14,12},{1,3},{3,1},... | collective-permute-start | bytes 1376264 | tf_op jit(solution)/shard_map/ppermute | solution.py:53
  30.2 7.3 %collective-permute-start.5 = (bf16[512,128]{1,0:T(8,128)(2,1)S(1)}, bf16[512,128]{1,0:T(8,128)(2,1)S(1)}, u32[]{:S(2)}, u32[]{:S(2)}) collective-permute-start(bf16[512,128]{1,0:T(8,128)(2,1)S(1)} %get-tuple-element.87), channel_id=1, source_target_pairs={{0,4},{2,6},{4,0},{6,2},{8,12},{10,14},{12,8},{14,10},{1,5},{3,7},... | collective-permute-start | bytes 393224 | tf_op jit(solution)/shard_map/ppermute | solution.py:53
  33.2 11.9 %collective-permute-start.7 = (bf16[512,128]{1,0:T(8,128)(2,1)S(1)}, bf16[512,128]{1,0:T(8,128)(2,1)S(1)}, u32[]{:S(2)}, u32[]{:S(2)}) collective-permute-start(bf16[512,128]{1,0:T(8,128)(2,1)S(1)} %get-tuple-element.88), channel_id=1, source_target_pairs={{0,8},{2,10},{4,12},{6,14},{8,0},{10,2},{12,4},{14,6},{1,9},{3,11}... | collective-permute-start | bytes 393224 | tf_op jit(solution)/shard_map/ppermute | solution.py:53
  36.3 10.2 %collective-permute-start.9 = (bf16[512,128]{1,0:T(8,128)(2,1)S(1)}, bf16[512,128]{1,0:T(8,128)(2,1)S(1)}, u32[]{:S(2)}, u32[]{:S(2)}) collective-permute-start(bf16[512,128]{1,0:T(8,128)(2,1)S(1)} %get-tuple-element.89), channel_id=1, source_target_pairs={{0,12},{2,14},{4,8},{6,10},{8,4},{10,6},{12,0},{14,2},{1,13},{3,15... | collective-permute-start | bytes 393224 | tf_op jit(solution)/shard_map/ppermute | solution.py:53
  36.3 10.2 %collective-permute-start.4 = (bf16[512,128]{1,0:T(8,128)(2,1)S(1)}, bf16[512,128]{1,0:T(8,128)(2,1)S(1)}, u32[]{:S(2)}, u32[]{:S(2)}) collective-permute-start(bf16[512,128]{1,0:T(8,128)(2,1)S(1)} %get-tuple-element.106.refs_0_), channel_id=1, source_target_pairs={{0,1},{1,0},{2,3},{3,2},{4,5},{5,4},{6,7},{7,6},{8,9},{9,8},{10,11... | collective-permute-start | bytes 393224 | tf_op jit(solution)/shard_map/ppermute | solution.py:53
  37.5 9.5 %collective-permute-start.6 = (bf16[512,128]{1,0:T(8,128)(2,1)S(1)}, bf16[512,128]{1,0:T(8,128)(2,1)S(1)}, u32[]{:S(2)}, u32[]{:S(2)}) collective-permute-start(bf16[512,128]{1,0:T(8,128)(2,1)S(1)} %collective-permute-done.5.refs_1_), channel_id=1, source_target_pairs={{0,1},{1,0},{2,3},{3,2},{4,5},{5,4},{6,7},{7,6},{8,9},{9,8},{10,11... | collective-permute-start | bytes 393224 | tf_op jit(solution)/shard_map/ppermute | solution.py:53
  40.6 23.2 %copy-start = (bf16[2048,1024]{1,0:T(8,128)(2,1)S(1)}, bf16[2048,1024]{1,0:T(8,128)(2,1)}, u32[]{:S(2)}) copy-start(bf16[2048,1024]{1,0:T(8,128)(2,1)} %weight.3) | copy-start | bytes 12582916
  45.1 24.0 %collective-permute-start.17 = (bf16[4,2,56,512]{3,2,1,0:T(8,128)(2,1)S(1)}, bf16[4,2,56,512]{3,2,1,0:T(8,128)(2,1)S(1)}, u32[]{:S(2)}, u32[]{:S(2)}) collective-permute-start(bf16[4,2,56,512]{3,2,1,0:T(8,128)(2,1)S(1)} %get-tuple-element.104), channel_id=1, source_target_pairs={{0,2},{2,0},{4,6},{6,4},{8,10},{10,8},{12,14},{14,12},{1,3},{3,1},... | collective-permute-start | bytes 1376264 | tf_op jit(solution)/shard_map/ppermute | solution.py:53
  46.5 2.2 %collective-permute-start.8 = (bf16[512,128]{1,0:T(8,128)(2,1)S(1)}, bf16[512,128]{1,0:T(8,128)(2,1)S(1)}, u32[]{:S(2)}, u32[]{:S(2)}) collective-permute-start(bf16[512,128]{1,0:T(8,128)(2,1)S(1)} %collective-permute-done.7.refs_2_), channel_id=1, source_target_pairs={{0,1},{1,0},{2,3},{3,2},{4,5},{5,4},{6,7},{7,6},{8,9},{9,8},{10,11... | collective-permute-start | bytes 393224 | tf_op jit(solution)/shard_map/ppermute | solution.py:53
  46.5 5.5 %collective-permute-start.10 = (bf16[512,128]{1,0:T(8,128)(2,1)S(1)}, bf16[512,128]{1,0:T(8,128)(2,1)S(1)}, u32[]{:S(2)}, u32[]{:S(2)}) collective-permute-start(bf16[512,128]{1,0:T(8,128)(2,1)S(1)} %collective-permute-done.9.refs_3_), channel_id=1, source_target_pairs={{0,1},{1,0},{2,3},{3,2},{4,5},{5,4},{6,7},{7,6},{8,9},{9,8},{10,11... | collective-permute-start | bytes 393224 | tf_op jit(solution)/shard_map/ppermute | solution.py:53
  47.0 9.2 %collective-permute-start.11 = (bf16[1,128,512]{2,1,0:T(8,128)(2,1)S(1)}, bf16[1,128,512]{2,1,0:T(8,128)(2,1)S(1)}, u32[]{:S(2)}, u32[]{:S(2)}) collective-permute-start(bf16[1,128,512]{2,1,0:T(8,128)(2,1)S(1)} %bitcast.4), channel_id=1, source_target_pairs={{0,8},{2,10},{4,12},{6,14},{8,0},{10,2},{12,4},{14,6},{1,9},{3,11}... | collective-permute-start | bytes 393224 | tf_op jit(solution)/shard_map/ppermute | solution.py:53
  48.7 7.6 %collective-permute-start.12 = (bf16[64,640]{1,0:T(8,128)(2,1)S(1)}, bf16[64,640]{1,0:T(8,128)(2,1)S(1)}, u32[]{:S(2)}, u32[]{:S(2)}) collective-permute-start(bf16[64,640]{1,0:T(8,128)(2,1)S(1)} %get-tuple-element.92), channel_id=1, source_target_pairs={{0,2},{2,4},{4,6},{6,8},{8,10},{10,12},{12,14},{1,3},{3,5},{5,7},{... | collective-permute-start | bytes 245768 | tf_op jit(solution)/shard_map/ppermute | solution.py:577
  56.2 13.0 %collective-permute-start.18 = (bf16[2,128,512]{2,1,0:T(8,128)(2,1)S(1)}, bf16[2,128,512]{2,1,0:T(8,128)(2,1)S(1)}, u32[]{:S(2)}, u32[]{:S(2)}) collective-permute-start(bf16[2,128,512]{2,1,0:T(8,128)(2,1)S(1)} %stacked.1), channel_id=1, source_target_pairs={{0,4},{2,6},{4,0},{6,2},{8,12},{10,14},{12,8},{14,10},{1,5},{3,7},... | collective-permute-start | bytes 786440 | tf_op jit(solution)/shard_map/ppermute | solution.py:53
  56.4 12.7 %collective-permute-start.16 = (bf16[2,2,56,512]{3,2,1,0:T(8,128)(2,1)S(1)}, bf16[2,2,56,512]{3,2,1,0:T(8,128)(2,1)S(1)}, u32[]{:S(2)}, u32[]{:S(2)}) collective-permute-start(bf16[2,2,56,512]{3,2,1,0:T(8,128)(2,1)S(1)} %get-tuple-element.101), channel_id=1, source_target_pairs={{0,4},{2,6},{4,0},{6,2},{8,12},{10,14},{12,8},{14,10},{1,5},{3,7},... | collective-permute-start | bytes 688136 | tf_op jit(solution)/shard_map/ppermute | solution.py:53
  58.5 5.3 %collective-permute-start.13 = (bf16[128,640]{1,0:T(8,128)(2,1)S(1)}, bf16[128,640]{1,0:T(8,128)(2,1)S(1)}, u32[]{:S(2)}, u32[]{:S(2)}) collective-permute-start(bf16[128,640]{1,0:T(8,128)(2,1)S(1)} %own_tokens.1.own), channel_id=1, source_target_pairs={{0,16},{16,0},{1,17},{17,1},{2,18},{18,2},{3,19},{19,3},{4,20},{20... | collective-permute-start | bytes 491528 | tf_op jit(solution)/shard_map/ppermute | solution.py:53
  63.8 8.7 %copy-start.5 = (bf16[128,1024]{1,0:T(8,128)(2,1)S(1)}, bf16[128,1024]{1,0:T(8,128)(2,1)}, u32[]{:S(2)}) copy-start(bf16[128,1024]{1,0:T(8,128)(2,1)} %get-tuple-element.109.hidden) | copy-start | bytes 786436
  63.8 8.7 %copy-start.7 = (f32[128,1]{1,0:T(8,128)S(1)}, f32[128,1]{1,0:T(8,128)}, u32[]{:S(2)}) copy-start(f32[128,1]{1,0:T(8,128)} %get-tuple-element.111.inv_rms) | copy-start | bytes 1540
  63.8 8.7 %copy-start.8 = (f32[1,1024]{1,0:T(1,128)S(1)}, f32[1,1024]{1,0:T(1,128)}, u32[]{:S(2)}) copy-start(f32[1,1024]{1,0:T(1,128)} %get-tuple-element.110.gain) | copy-start | bytes 12292
  70.5 12.7 %collective-permute-start.20 = (bf16[2,256,512]{2,1,0:T(8,128)(2,1)S(1)}, bf16[2,256,512]{2,1,0:T(8,128)(2,1)S(1)}, u32[]{:S(2)}, u32[]{:S(2)}) collective-permute-start(bf16[2,256,512]{2,1,0:T(8,128)(2,1)S(1)} %get-tuple-element.118), channel_id=1, source_target_pairs={{0,2},{2,0},{4,6},{6,4},{8,10},{10,8},{12,14},{14,12},{1,3},{3,1},... | collective-permute-start | bytes 1572872 | tf_op jit(solution)/shard_map/ppermute | solution.py:53
  70.9 1.6 %collective-permute-start.15 = (bf16[128,1152]{1,0:T(8,128)(2,1)S(1)}, bf16[128,1152]{1,0:T(8,128)(2,1)S(1)}, u32[]{:S(2)}, u32[]{:S(2)}) collective-permute-start(bf16[128,1152]{1,0:T(8,128)(2,1)S(1)} %get-tuple-element.98), channel_id=1, source_target_pairs={{0,1},{1,0},{2,3},{3,2},{4,5},{5,4},{6,7},{7,6},{8,9},{9,8},{10,11... | collective-permute-start | bytes 884744 | tf_op jit(solution)/shard_map/ppermute | solution.py:53
  70.9 8.0 %collective-permute-start.19 = (bf16[2,2,56,512]{3,2,1,0:T(8,128)(2,1)S(1)}, bf16[2,2,56,512]{3,2,1,0:T(8,128)(2,1)S(1)}, u32[]{:S(2)}, u32[]{:S(2)}) collective-permute-start(bf16[2,2,56,512]{3,2,1,0:T(8,128)(2,1)S(1)} %get-tuple-element.115), channel_id=1, source_target_pairs={{0,4},{2,6},{4,0},{6,2},{8,12},{10,14},{12,8},{14,10},{1,5},{3,7},... | collective-permute-start | bytes 688136 | tf_op jit(solution)/shard_map/ppermute | solution.py:53
  83.3 13.7 %collective-permute-start.23 = (bf16[256,512]{1,0:T(8,128)(2,1)S(1)}, bf16[256,512]{1,0:T(8,128)(2,1)S(1)}, u32[]{:S(2)}, u32[]{:S(2)}) collective-permute-start(bf16[256,512]{1,0:T(8,128)(2,1)S(1)} %get-tuple-element.125), channel_id=1, source_target_pairs={{0,16},{16,0},{1,17},{17,1},{2,18},{18,2},{3,19},{19,3},{4,20},{20... | collective-permute-start | bytes 786440 | tf_op jit(solution)/shard_map/ppermute | solution.py:53
  84.9 10.2 %collective-permute-start.21 = (bf16[1,2,56,512]{3,2,1,0:T(8,128)(2,1)S(1)}, bf16[1,2,56,512]{3,2,1,0:T(8,128)(2,1)S(1)}, u32[]{:S(2)}, u32[]{:S(2)}) collective-permute-start(bf16[1,2,56,512]{3,2,1,0:T(8,128)(2,1)S(1)} %get-tuple-element.121), channel_id=1, source_target_pairs={{0,8},{2,10},{4,12},{6,14},{8,0},{10,2},{12,4},{14,6},{1,9},{3,11}... | collective-permute-start | bytes 344072 | tf_op jit(solution)/shard_map/ppermute | solution.py:53
  87.3 9.0 %collective-permute-start.22 = (bf16[1,2,56,512]{3,2,1,0:T(8,128)(2,1)S(1)}, bf16[1,2,56,512]{3,2,1,0:T(8,128)(2,1)S(1)}, u32[]{:S(2)}, u32[]{:S(2)}) collective-permute-start(bf16[1,2,56,512]{3,2,1,0:T(8,128)(2,1)S(1)} %get-tuple-element.122), channel_id=1, source_target_pairs={{0,8},{2,10},{4,12},{6,14},{8,0},{10,2},{12,4},{14,6},{1,9},{3,11}... | collective-permute-start | bytes 344072 | tf_op jit(solution)/shard_map/ppermute | solution.py:53
  96.4 4.9 %collective-permute-start.24 = (bf16[2,56,512]{2,1,0:T(8,128)(2,1)S(1)}, bf16[2,56,512]{2,1,0:T(8,128)(2,1)S(1)}, u32[]{:S(2)}, u32[]{:S(2)}) collective-permute-start(bf16[2,56,512]{2,1,0:T(8,128)(2,1)S(1)} %get-tuple-element.127), channel_id=1, source_target_pairs={{0,16},{16,0},{1,17},{17,1},{2,18},{18,2},{3,19},{19,3},{4,20},{20... | collective-permute-start | bytes 344072 | tf_op jit(solution)/shard_map/ppermute | solution.py:53

commit v3 on v2

--- a/solution.py
+++ b/solution.py
@@ -12,9 +12,8 @@
 EPSILON = 1e-06
 MASKED = -1e30
 VMEM_BYTES = 24 * 1024 * 1024
-QUERY_VMEM_BYTES = 56 * 1024 * 1024
+QUERY_VMEM_BYTES = 52 * 1024 * 1024
 CHUNKS = 2
-FIRST_ATTEND_FLOPS = 20_000_000_000
 STEPS = 4
 
 F32 = jnp.float32
@@ -302,17 +301,19 @@
         dots_out[...] = dots
 
 
-def kv_part_kernel(count, turned, turned_kv, send_out, keep_out, product):
+def kv_part_kernel(groups, turned, turned_kv, *rest):
+    *outs, product = rest
     outer, inner_own = lax.axis_index("seq") // 2, lax.axis_index("seq") % 2
     width = turned.shape[0]
     product[:width] = nt_dot(turned[...], turned_kv[...])
-    piece = send_out.shape[2]
+    piece = outs[0].shape[2]
     half = width // 2
-    for step in range(count):
-        for part in range(2):
-            for outs, inner in ((keep_out, inner_own), (send_out, 1 - inner_own)):
-                start = part * half + (2 * (outer ^ step) + inner) * piece
-                outs[step, part] = rows_at(product, start, piece).astype(outs.dtype)
+    for place, steps in enumerate(groups):
+        for index, step in enumerate(steps):
+            for part in range(2):
+                for out, inner in ((outs[2 * place], 1 - inner_own), (outs[2 * place + 1], inner_own)):
+                    start = part * half + (2 * (outer ^ step) + inner) * piece
+                    out[index, part] = rows_at(product, start, piece).astype(out.dtype)
 
 
 def attend(chunk, ids, counts, keep, other, pair, cross, attn_grad, kv, before):
@@ -336,20 +337,17 @@
         operands,
         [IN_SMEM] * 2 + [IN_VMEM] * (len(operands) - 2),
         [pltpu.VMEM((rows, keys), F32)],
-        0 if last else FIRST_ATTEND_FLOPS,
-    )
-
-
-def kv_part(chunk, turned, turned_kv):
+    )
+
+
+def kv_part(chunk, turned, turned_kv, groups):
     width = turned.shape[0]
     cols = turned_kv.shape[0]
-    seq_size = lax.axis_size("seq")
-    count = seq_size // 2
-    dims = (count, 2, width // (2 * seq_size), cols)
-    return call(
-        functools.partial(kv_part_kernel, count),
+    dims = (2, width // (2 * lax.axis_size("seq")), cols)
+    return call(
+        functools.partial(kv_part_kernel, groups),
         "kv_part_%d" % chunk,
-        [shape(dims, BF16), shape(dims, F32)],
+        [shape((len(steps), *dims), kind) for steps in groups for kind in (BF16, F32)],
         [turned, turned_kv],
         None,
         [pltpu.VMEM((width + 16, cols), F32)],
@@ -379,63 +377,82 @@
     return call(fold_kernel, "fold", [shape(half, F32), shape(half, BF16)], [kept, received])
 
 
+def add_kernel(kept, received, out):
+    out[...] = (kept[...] + received[...].astype(F32)).astype(out.dtype)
+
+
+def added(kept, received, kind):
+    return call(add_kernel, "added", [shape(kept.shape, kind)], [kept, received])[0]
+
+
 def outer_kernel(*refs):
-    *refs, mine, theirs = refs
+    *refs, mine, next_out, side_out, cross_out = refs
     section = lax.axis_index("section")
     for chunk in range(CHUNKS):
         kept, received = refs[2 * chunk : 2 * chunk + 2]
-        for out, part in ((mine, section), (theirs, 1 - section)):
-            out[chunk] = (kept[0, part] + received[0, part].astype(F32)).astype(out.dtype)
+        for out, place, part in (
+            (next_out, 1, section),
+            (cross_out, 1, 1 - section),
+            (side_out, 0, 1 - section),
+            (mine, 0, section),
+        ):
+            out[chunk] = (kept[place, part] + received[place, part].astype(F32)).astype(out.dtype)
 
 
 def outer_sums(parts):
     _, _, piece, cols = parts[0].shape
-    return call(
-        outer_kernel,
-        "outer_sums",
-        [shape((CHUNKS, piece, cols), F32), shape((CHUNKS, piece, cols), BF16)],
-        parts,
-    )
-
-
-def kv_kernel(mine, got, out):
+    dims = (CHUNKS, piece, cols)
+    return call(
+        outer_kernel, "outer_sums", [shape(dims, F32)] + [shape(dims, BF16)] * 3, parts
+    )
+
+
+def kv_grad_kernel(mine, following, side, cross, out):
     section = lax.axis_index("section")
     cols = mine.shape[2] // 2
     for chunk in range(CHUNKS):
         for which in range(2):
-            for source, part in ((mine, section), (got, 1 - section)):
+            span = slice(which * cols, (which + 1) * cols)
+            own = mine[chunk, :, span] + following[chunk, :, span].astype(F32)
+            other = side[chunk, :, span].astype(F32) + cross[chunk, :, span].astype(F32)
+            for value, part in ((own, section), (other, 1 - section)):
                 start = pl.multiple_of((part * CHUNKS + chunk) * cols, cols)
-                out[which, :, pl.ds(start, cols)] = source[
-                    chunk, :, which * cols : (which + 1) * cols
-                ].astype(F32)
+                out[which, :, pl.ds(start, cols)] = value
 
 
 def weight_kernel(order, *refs):
-    *refs, send_out, keep_out = refs
+    *refs, keep_out, pair_out, side_out, cross_out = refs
     count = len(order)
     mine, theirs, grads = refs[:count], refs[count : 2 * count], refs[2 * count :]
+    section = lax.axis_index("section")
     inner_own = lax.axis_index("seq") % 2
-    core = lax.axis_index("mp")
-    piece = send_out.shape[1]
+    swap = lax.axis_index("mp") != section
+    piece = keep_out.shape[0]
     gathered = [ref[index] for ref in grads for index in range(ref.shape[0])]
-    for outs, inner in ((send_out, 1 - inner_own), (keep_out, inner_own)):
+    for outs, inner, other in (
+        (pair_out, 1 - inner_own, False),
+        (cross_out, 1 - inner_own, True),
+        (side_out, inner_own, True),
+        (keep_out, inner_own, False),
+    ):
         rows = pl.ds(pl.multiple_of(inner * piece, piece), piece)
-        for part in range(2):
-            total = None
-            for step, grad in zip(order, gathered):
-                column = jnp.where(core == part, mine[step][rows, :], theirs[step][rows, :])
-                term = jnp.dot(column, grad, preferred_element_type=F32)
-                total = term if total is None else total + term
-            outs[part] = total.astype(outs.dtype)
+        total = None
+        for step, grad in zip(order, gathered):
+            same, opposite = mine[step][rows, :], theirs[step][rows, :]
+            if other:
+                same, opposite = opposite, same
+            column = jnp.where(swap, opposite, same)
+            term = jnp.dot(column, grad, preferred_element_type=F32)
+            total = term if total is None else total + term
+        outs[...] = total.astype(outs.dtype)
 
 
 def weight_part(order, mine, theirs, grads):
-    span = mine[0].shape[0]
-    dims = (2, span // 2, grads[0].shape[2])
+    dims = (mine[0].shape[0] // 2, grads[0].shape[2])
     return call(
         functools.partial(weight_kernel, order),
         "weight_part",
-        [shape(dims, BF16), shape(dims, F32)],
+        [shape(dims, F32)] + [shape(dims, BF16)] * 3,
         [*mine, *theirs, *grads],
     )
 
@@ -466,20 +483,16 @@
     return stages, order, whole
 
 
-def weight_sum_kernel(kept, received, mine, theirs):
+def query_grad_kernel(kept, paired, side, cross, out):
     section = lax.axis_index("section")
-    mine[...] = kept[section] + received[section].astype(F32)
-    theirs[...] = (kept[1 - section] + received[1 - section].astype(F32)).astype(BF16)
-
-
-def side_kernel(mine, got, out):
-    section = lax.axis_index("section")
-    cols = mine.shape[1]
-    out[:, pl.ds(pl.multiple_of(section * cols, cols), cols)] = mine[...]
-    out[:, pl.ds(pl.multiple_of((1 - section) * cols, cols), cols)] = got[...].astype(F32)
-
-
-def normed_kernel(own, other, weight, keep_out, send_out, dots_out, total):
+    cols = kept.shape[1]
+    own = pl.ds(pl.multiple_of(section * cols, cols), cols)
+    out[:, own] = kept[...] + paired[...].astype(F32)
+    other = pl.ds(pl.multiple_of((1 - section) * cols, cols), cols)
+    out[:, other] = side[...].astype(F32) + cross[...].astype(F32)
+
+
+def normed_kernel(own, other, weight, keep_out, send_out, more_out, dots_out, total):
     cols = own.shape[1] - HD
     swap = lax.axis_index("section") == 1
     core = lax.axis_index("mp")
@@ -488,10 +501,12 @@
     second = jnp.where(swap, own[:, :cols], other[:, :cols])
     total[...] = nt_dot(first, weight[:, :cols]) + nt_dot(second, weight[:, cols:])
     keep_out[...] = lanes_at(total, core * quarter, quarter)
-    send_out[:, :quarter] = lanes_at(total, (1 - core) * quarter, quarter).astype(BF16)
+    send = lanes_at(total, (1 - core) * quarter, quarter).astype(BF16)
+    send_out[...] = send[:, : quarter // 2]
+    more_out[:, : quarter // 2] = send[:, quarter // 2 :]
     dots = joined_column(own[:, cols:]) + joined_column(other[:, cols:])
     dots_out[...] = dots
-    send_out[:, quarter:] = split_column(dots)
+    more_out[:, quarter // 2 :] = split_column(dots)
 
 
 def normed_part(own, other, weight):
@@ -501,23 +516,28 @@
     return call(
         normed_kernel,
         "normed_part",
-        [shape((rows, quarter), F32), shape((rows, quarter + HD), BF16), shape((rows, 1), F32)],
+        [
+            shape((rows, quarter), F32),
+            shape((rows, quarter // 2), BF16),
+            shape((rows, quarter // 2 + HD), BF16),
+            shape((rows, 1), F32),
+        ],
         [own, other, weight],
         None,
         [pltpu.VMEM((rows, half), F32)],
     )
 
 
-def hidden_kernel(width, kept, received, dots, hidden, gain, inv_rms, grad_out, dot_out):
-    quarter = kept.shape[1]
+def hidden_kernel(width, kept, received, more, dots, hidden, gain, inv_rms, grad_out, dot_out):
+    part = received.shape[1]
     inv = inv_rms[...]
-    row_dot = (dots[...] + joined_column(received[:, quarter:])) / inv
+    row_dot = (dots[...] + joined_column(more[:, part:])) / inv
     wide = jnp.broadcast_to(row_dot * (1.0 / math.sqrt(width)), (row_dot.shape[0], HD))
     dot_out[...] = wide.T[:1]
-    scaled = gain[...] * (kept[...] + received[:, :quarter].astype(F32))
-    grad_out[...] = (
-        inv * scaled - hidden[...].astype(F32) * (inv * inv * inv * row_dot * (1.0 / width))
-    ).astype(BF16)
+    back = inv * inv * inv * row_dot * (1.0 / width)
+    for span, ref in ((slice(0, part), received), (slice(part, 2 * part), more)):
+        scaled = gain[:, span] * (kept[:, span] + ref[:, :part].astype(F32))
+        grad_out[:, span] = (inv * scaled - hidden[:, span].astype(F32) * back).astype(BF16)
 
 
 def body(
@@ -566,78 +586,76 @@
     def outer_swap(pieces):
         return [swapped(piece, "seq", 2 * (step + 1)) for step, piece in enumerate(pieces)]
 
+    def three_ways(pieces, mask):
+        near, side, cross = pieces
+        pairs = [(s * seq_size + i, (1 - s) * seq_size + (i ^ mask)) for s in range(2) for i in range(seq_size)]
+        return (
+            swapped(near, "seq", mask),
+            swapped(side, "section", 1),
+            lax.ppermute(cross, ("section", "seq"), pairs),
+        )
+
+    steps = list(range(outer))
     *before, turned_kv = attention(0, turned, ())
-    kv_send, kept_first = kv_part(0, turned, turned_kv)
-    pair_first = swapped(kv_send, "seq", 1)
-    columns = columns_for(hn_half, after(led, kept_first), outer, offset)
+    first_send, first_kept = kv_part(0, turned, turned_kv, [steps])
+    first_in = swapped(first_send, "seq", 1)
+    dq, dots, dq_lead, turned_kv = attention(1, first_kept, before)
+    odd_send, odd_kept, even_send, even_kept = kv_part(
+        1, turned, turned_kv, [steps[1::2], steps[::2]]
+    )
+    odd_in = swapped(odd_send, "seq", 1)
+    even_in = swapped(even_send, "seq", 1)
+    columns = columns_for(hn_half, led, outer, offset)
     columns_mine = [columns[0]] + outer_swap(columns[1:])
-    dq, dots, dq_lead, turned_kv = attention(1, columns[0], before)
-    kv_send, kept_second = kv_part(1, turned, turned_kv)
-    dq = after(dq, kept_second)
+    columns_theirs = [swapped(column, "mp", 1) for column in columns_mine]
     carried = lax.ppermute(dq_lead, "seq", [(i, i + 1) for i in range(seq_size - 1)])
-    pair_second = swapped(kv_send, "seq", 1)
-    columns_theirs = [swapped(column, "mp", 1) for column in columns_mine]
-    gathered, order, stacked = outer_gather(dq[None], outer, (kept_second, *columns_theirs))
+    gathered, order, _ = outer_gather(dq[None], outer, ())
 
     own_dq = call(
         functools.partial(own_kernel, offset),
         "own_tokens",
         [shape((row_count, cols + HD), BF16)],
-        [dq, after(dots, stacked), carried],
+        [dq, dots, carried],
     )[0]
     dq_other = swapped(own_dq, "section", 1)
 
-    def fold_on(kept, received, bit, ahead):
-        kept, send = fold(after(kept, ahead), received)
-        return kept, swapped(send, "seq", 2 * bit), 2 * bit
-
-    def folded(kept, received, bit, ahead):
-        while bit < outer:
-            kept, received, bit = fold_on(kept, received, bit, ahead)
-            ahead = kept
+    def folded(kept, received, bit):
+        while 2 * bit < outer:
+            kept, send = fold(kept, received)
+            received = swapped(send, "seq", 2 * bit)
+            bit *= 2
         return kept, received
 
-    first = fold_on(kept_first, pair_first, 1, own_dq) if outer > 1 else (kept_first, pair_first, 1)
-    normed_keep, normed_send, normed_dots = normed_part(
-        own_dq, after(dq_other, first[0]), query_weight
-    )
-    normed_in = swapped(normed_send, "mp", 1)
-    first = folded(*first, normed_dots)
-    second = (kept_second, pair_second, 1)
-    if outer > 1:
-        second = fold_on(*second, first[0])
-
-    columns_mine[0] = after(columns_mine[0], second[0])
-    weight_send, weight_keep = weight_part(order, columns_mine, columns_theirs, gathered)
-    weight_in = swapped(weight_send, "seq", 1)
-
+    first = folded(after(first_kept, *columns_theirs), first_in, 1)
+    odd_sum = added(after(odd_kept, *columns_theirs), odd_in, BF16)
+    second = folded(added(even_kept, even_in, F32), swapped(odd_sum, "seq", 2), 2)
+
+    weight_keep, *weight_send = weight_part(order, columns_mine, columns_theirs, gathered)
+    weight_in = three_ways(weight_send, 1)
+
+    normed_keep, *normed_send, normed_dots = normed_part(own_dq, dq_other, query_weight)
+    normed_in = [swapped(part, "mp", 1) for part in normed_send]
     hidden_grad, norm_dot = call(
         functools.partial(hidden_kernel, model_width),
         "hidden_grad",
         [shape(hidden_part.shape, BF16), shape((1, row_count), F32)],
-        [normed_keep, normed_in, after(normed_dots, weight_keep), hidden_part, gain_part, inv_rms],
-    )
-
-    second = folded(*second, norm_dot)
-
-    weight_shape = weight_keep.shape[1:]
-    mine, theirs = call(
-        weight_sum_kernel,
-        "weight_sum",
-        [shape(weight_shape, F32), shape(weight_shape, BF16)],
-        [after(weight_keep, second[0]), weight_in],
-    )
-    got = swapped(theirs, "section", 1)
-    kv_mine, kv_theirs = outer_sums([after(first[0], mine), first[1], *second])
-    kv_got = swapped(kv_theirs, "section", 1)
+        [normed_keep, *normed_in, normed_dots, hidden_part, gain_part, inv_rms],
+    )
+
+    kv_mine, *kv_send = outer_sums([*first, *second])
+    kv_in = three_ways(kv_send, seq_size // 2)
 
     query_grad = call(
-        side_kernel, "query_grad", [shape((weight_shape[0], local_cols), F32)],
-        [after(mine, kv_mine), got],
+        query_grad_kernel,
+        "query_grad",
+        [shape((weight_keep.shape[0], local_cols), F32)],
+        [weight_keep, *weight_in],
     )[0]
     kv_grad = call(
-        kv_kernel, "kv_grad", [shape((2, piece, local_cols), F32)],
-        [after(kv_mine, query_grad), kv_got],
+        kv_grad_kernel,
+        "kv_grad",
+        [shape((2, piece, local_cols), F32)],
+        [kv_mine, *kv_in],
     )[0]
     return (hidden_grad, query_grad, kv_grad, norm_dot.reshape(row_count))
 

time: 102 us -> 89.9 us (0.88)
  waiting for transfers between devices: 37.8 us -> 18.4 us
  starting transfers between devices: 33.2 us -> 40.2 us
  Pallas kernels: 28 us -> 25.6 us
  local copies, waits for them, and re-layouts: 2.08 us -> 3.92 us
    ppermute x21 -> x22, waiting for transfers between devices: 37.7 us -> 16.1 us  [swapped(): return lax.ppermute(array, axis, [(i, i ^ mask) for i in range(size)])]
    ppermute x21 -> x22, starting transfers between devices: 26 us -> 31.2 us  [swapped(): return lax.ppermute(array, axis, [(i, i ^ mask) for i in range(size)])]
    pallas_call x20 -> x18, Pallas kernels: 28 us -> 25.6 us  [call(): pl.pallas_call(kernel, in_specs=in_specs or [IN_VMEM] * len(operands), ou...]
    ppermute x1, waiting for transfers between devices: 0.01 us -> 2.29 us  [body(): lax.ppermute(cross, ('section', 'seq'), [(s * seq_size + i, (1 - s) * seq...]
    unnamed x24 -> x16, local copies, waits for them, and re-layouts: 2.08 us -> 3.92 us
    ppermute x0 -> x2, starting transfers between devices: none -> 1.82 us  [three_ways(): lax.ppermute(cross, ('section', 'seq'), pairs)]
  transfers between devices with their start and end apart: 25 -> 28, of which waited for: 11 -> 8; matrix products, arithmetic and copies ran while one was open for 0% -> 0% of each run, Pallas kernels for 20% -> 25%
where the time goes in v3:
time: 89.9 us; the launch traced here: 89 us
  starting transfers between devices  40.2 us (45%)
  Pallas kernels  25.6 us (28%)
  waiting for transfers between devices  18.4 us (20%)
  local copies, waits for them, and re-layouts  3.92 us (4%)
    ppermute x22, starting transfers between devices, swapped(): return lax.ppermute(array, axis, [(i, i ^ mask) for i in range(size)])  31.2 us
    pallas_call x18, Pallas kernels, call(): pl.pallas_call(kernel, in_specs=in_specs or [IN_VMEM] * len(operands), ou...  25.6 us
    ppermute x22, waiting for transfers between devices, swapped(): return lax.ppermute(array, axis, [(i, i ^ mask) for i in range(size)])  16.1 us
    unnamed x16, local copies, waits for them, and re-layouts  3.92 us
    ppermute x1, starting transfers between devices, body(): lax.ppermute(dq_lead, 'seq', [(i, i + 1) for i in range(seq_size - 1)])  3.27 us
    ppermute x1, waiting for transfers between devices, body(): lax.ppermute(cross, ('section', 'seq'), [(s * seq_size + i, (1 - s) * seq...  2.29 us
    ppermute x2, starting transfers between devices, three_ways(): lax.ppermute(cross, ('section', 'seq'), pairs)  1.82 us
  transfers between devices with their start and end apart: 28, of which 8 were waited for; matrix products, arithmetic and copies ran while one was open for 0% of the time, Pallas kernels for 25%

profile of v3, /device:TPU:0, one launch (start us, length us, event | category | flops | bytes accessed | tf_op | source)
XLA Modules:
  0.0 89.0 jit_solution(13967650627284219529)
XLA Ops:
  0.7 1.1 %copy-done.3 = bf16[128,1024]{1,0:T(8,128)(2,1)S(1)} copy-done((bf16[128,1024]{1,0:T(8,128)(2,1)S(1)}, bf16[128,1024]{1,0:T(8,128)(2,1)}, u32[]{:S(2)}) %copy-start.3) | copy-done | bytes 262168
  1.7 0.8 copy-done.4
  2.5 3.0 %query_part.1 = (bf16[128,2048]{1,0:T(8,128)(2,1)S(1)}, bf16[64,2048]{1,0:T(8,128)(2,1)S(1)}, f32[128,1]{1,0:T(8,128)S(1)}, f32[128,512]{1,0:T(8,128)S(1)}, bf16...) custom-call(bf16[4096]{0:T(1024)(128)(2,1)S(1)} %copy-done.4, ...), custom_call_target="tpu_custom_call" | custom-call | tf_op jit(solution)/shard_map/query_part/pallas_call | solution.py:34
  5.5 1.3 %collective-permute-start.7 = (bf16[64,2048]{1,0:T(8,128)(2,1)S(1)}, bf16[64,2048]{1,0:T(8,128)(2,1)S(1)}, u32[]{:S(2)}, u32[]{:S(2)}) collective-permute-start(bf16[64,2048]{1,0:T(8,128)(2,1)S(1)} %get-tuple-element.76), channel_id=1, source_target_pairs={{2,0},{4,2},{6,4},{8,6},{10,8},{12,10},{14,12},{3,1},{5,3},{7,5},{... | collective-permute-start | bytes 786440 | tf_op jit(solution)/shard_map/ppermute | solution.py:575
  6.8 3.0 %collective-permute-start = (bf16[128,512]{1,0:T(8,128)(2,1)S(1)}, bf16[128,512]{1,0:T(8,128)(2,1)S(1)}, u32[]{:S(2)}, u32[]{:S(2)}) collective-permute-start(bf16[128,512]{1,0:T(8,128)(2,1)S(1)} %get-tuple-element.55), channel_id=1, source_target_pairs={{0,16},{16,0},{1,17},{17,1},{2,18},{18,2},{3,19},{19,3},{4,20},{20... | collective-permute-start | bytes 393224 | tf_op jit(solution)/shard_map/ppermute | solution.py:52
  9.8 1.3 %collective-permute-start.1 = (bf16[2,64,512]{2,1,0:T(8,128)(2,1)S(1)}, bf16[2,64,512]{2,1,0:T(8,128)(2,1)S(1)}, u32[]{:S(2)}, u32[]{:S(2)}) collective-permute-start(bf16[2,64,512]{2,1,0:T(8,128)(2,1)S(1)} %get-tuple-element.56), channel_id=1, source_target_pairs={{2,0},{4,2},{6,4},{8,6},{10,8},{12,10},{14,12},{3,1},{5,3},{7,5},{... | collective-permute-start | bytes 393224 | tf_op jit(solution)/shard_map/ppermute | solution.py:569
  11.1 1.3 %collective-permute-start.2 = (bf16[64,512]{1,0:T(8,128)(2,1)S(1)}, bf16[64,512]{1,0:T(8,128)(2,1)S(1)}, u32[]{:S(2)}, u32[]{:S(2)}) collective-permute-start(bf16[64,512]{1,0:T(8,128)(2,1)S(1)} %get-tuple-element.57), channel_id=1, source_target_pairs={{2,16},{4,18},{6,20},{8,22},{10,24},{12,26},{14,28},{18,0},{20,2},... | collective-permute-start | bytes 196616 | tf_op jit(solution)/shard_map/ppermute | solution.py:570
  12.4 2.0 %copy-done.2 = bf16[2,896,1024]{2,1,0:T(8,128)(2,1)S(1)} copy-done((bf16[2,896,1024]{2,1,0:T(8,128)(2,1)S(1)}, bf16[2,896,1024]{2,1,0:T(8,128)(2,1)}, u32[]{:S(2)}) %copy-start.2) | copy-done | bytes 3670040
  14.5 5.3 %pool_project.1 = (bf16[2,2048,512]{2,1,0:T(8,128)(2,1)S(1)}, bf16[896,2048]{1,0:T(8,128)(2,1)S(1)}) custom-call(bf16[896]{0:T(1024)(128)(2,1)S(1)} %copy-done.7, bf16[2048,896]{1,0:T(8,128)(2,1)S(1)} %bitcast.3, bf16[2,896,1024]{2,1,0:T(8,128)(2,1)S(1)} %copy-done.2), custom_call_target="tpu_custom_call" | custom-call | tf_op jit(solution)/shard_map/pool_project/pallas_call | solution.py:34
  19.7 2.3 %collective-permute-done.2.cross = bf16[64,512]{1,0:T(8,128)(2,1)S(1)} collective-permute-done((bf16[64,512]{1,0:T(8,128)(2,1)S(1)}, bf16[64,512]{1,0:T(8,128)(2,1)S(1)}, u32[]{:S(2)}, u32[]{:S(2)}) %collective-permute-start.2) | collective-permute-done | bytes 65568 | tf_op jit(solution)/shard_map/ppermute | solution.py:570
  22.1 3.1 %attend_0.1 = (bf16[128,256]{1,0:T(8,128)(2,1)S(1)}, f32[128,1]{1,0:T(8,128)S(1)}, bf16[512,2048]{1,0:T(8,128)(2,1)S(1)}) custom-call(s32[2,16]{1,0:T(2,128)S(1)} %copy-done.5, s32[2]{0:T(128)S(1)} %copy-done.6, f32[128,512]{1,0:T(8,128)S(1)} %get-tuple-element.61.keep, bf16[128,512]{1,0:T(8,128)(2,1)S(1)} %collective-permute-done.other, ...), custom_call_target="tpu_custom_call" | custom-call | tf_op jit(solution)/shard_map/attend_0/pallas_call | solution.py:34
  25.1 2.2 %kv_part_0.1 = (bf16[4,2,56,512]{3,2,1,0:T(8,128)(2,1)S(1)}, f32[4,2,56,512]{3,2,1,0:T(8,128)S(1)}) custom-call(bf16[896,2048]{1,0:T(8,128)(2,1)S(1)} %get-tuple-element.53.turned, bf16[512,2048]{1,0:T(8,128)(2,1)S(1)} %get-tuple-element.59.turned_kv), custom_call_target="tpu_custom_call" | custom-call | tf_op jit(solution)/shard_map/kv_part_0/pallas_call | solution.py:34
  27.3 2.5 %collective-permute-start.20 = (bf16[4,2,56,512]{3,2,1,0:T(8,128)(2,1)S(1)}, bf16[4,2,56,512]{3,2,1,0:T(8,128)(2,1)S(1)}, u32[]{:S(2)}, u32[]{:S(2)}) collective-permute-start(bf16[4,2,56,512]{3,2,1,0:T(8,128)(2,1)S(1)} %get-tuple-element.86), channel_id=1, source_target_pairs={{0,2},{2,0},{4,6},{6,4},{8,10},{10,8},{12,14},{14,12},{1,3},{3,1},... | collective-permute-start | bytes 1376264 | tf_op jit(solution)/shard_map/ppermute | solution.py:52
  29.8 3.1 %attend_1.1 = (bf16[128,512]{1,0:T(8,128)(2,1)S(1)}, bf16[128,128]{1,0:T(8,128)(2,1)S(1)}, bf16[64,640]{1,0:T(8,128)(2,1)S(1)}, bf16[512,2048]{1,0:T(8,128)(2,1)S(1)}) custom-call(s32[2,16]{1,0:T(2,128)S(1)} %copy-done.5, s32[2]{0:T(128)S(1)} %copy-done.6, f32[128,512]{1,0:T(8,128)S(1)} %get-tuple-element.61.keep, ...), custom_call_target="tpu_custom_call" | custom-call | tf_op jit(solution)/shard_map/attend_1/pallas_call | solution.py:34
  32.9 3.7 %collective-permute-start.15 = (bf16[1,128,512]{2,1,0:T(8,128)(2,1)S(1)}, bf16[1,128,512]{2,1,0:T(8,128)(2,1)S(1)}, u32[]{:S(2)}, u32[]{:S(2)}) collective-permute-start(bf16[1,128,512]{2,1,0:T(8,128)(2,1)S(1)} %bitcast.4), channel_id=1, source_target_pairs={{0,8},{2,10},{4,12},{6,14},{8,0},{10,2},{12,4},{14,6},{1,9},{3,11}... | collective-permute-start | bytes 393224 | tf_op jit(solution)/shard_map/ppermute | solution.py:52
  36.6 0.7 hidden_columns.1
  37.3 1.6 %collective-permute-start.8 = (bf16[512,128]{1,0:T(8,128)(2,1)S(1)}, bf16[512,128]{1,0:T(8,128)(2,1)S(1)}, u32[]{:S(2)}, u32[]{:S(2)}) collective-permute-start(bf16[512,128]{1,0:T(8,128)(2,1)S(1)} %get-tuple-element.78), channel_id=1, source_target_pairs={{0,4},{2,6},{4,0},{6,2},{8,12},{10,14},{12,8},{14,10},{1,5},{3,7},... | collective-permute-start | bytes 393224 | tf_op jit(solution)/shard_map/ppermute | solution.py:52
  39.0 2.8 %collective-permute-start.10 = (bf16[512,128]{1,0:T(8,128)(2,1)S(1)}, bf16[512,128]{1,0:T(8,128)(2,1)S(1)}, u32[]{:S(2)}, u32[]{:S(2)}) collective-permute-start(bf16[512,128]{1,0:T(8,128)(2,1)S(1)} %get-tuple-element.80), channel_id=1, source_target_pairs={{0,12},{2,14},{4,8},{6,10},{8,4},{10,6},{12,0},{14,2},{1,13},{3,15... | collective-permute-start | bytes 393224 | tf_op jit(solution)/shard_map/ppermute | solution.py:52
  41.8 1.5 %collective-permute-done.15.refs_1_.refs_9_ = bf16[1,128,512]{2,1,0:T(8,128)(2,1)S(1)} collective-permute-done((bf16[1,128,512]{2,1,0:T(8,128)(2,1)S(1)}, bf16[1,128,512]{2,1,0:T(8,128)(2,1)S(1)}, u32[]{:S(2)}, u32[]{:S(2)}) %collective-permute-start.15) | collective-permute-done | bytes 131104 | tf_op jit(solution)/shard_map/ppermute | solution.py:52
  43.3 0.5 collective-permute-start.12
  43.8 2.4 %kv_part_1.1 = (bf16[2,2,56,512]{3,2,1,0:T(8,128)(2,1)S(1)}, f32[2,2,56,512]{3,2,1,0:T(8,128)S(1)}, bf16[2,2,56,512]{3,2,1,0:T(8,128)(2,1)S(1)}, f32[2,2,56,512]{3,2,1,0:T(8,128)S(1)}) custom-call(bf16[896,2048]{1,0:T(8,128)(2,1)S(1)} %get-tuple-element.53.turned, bf16[512,2048]{1,0:T(8,128)(2,1)S(1)} %get-tuple-element.89.turned_kv), custom_call_target="tpu_custom_call" | custom-call | tf_op jit(solution)/shard_map/kv_part_1/pallas_call | solution.py:34
  46.2 4.1 %collective-permute-done.9.refs_2_ = bf16[512,128]{1,0:T(8,128)(2,1)S(1)} collective-permute-done((bf16[512,128]{1,0:T(8,128)(2,1)S(1)}, bf16[512,128]{1,0:T(8,128)(2,1)S(1)}, u32[]{:S(2)}, u32[]{:S(2)}) %collective-permute-start.9) | collective-permute-done | bytes 131104 | tf_op jit(solution)/shard_map/ppermute | solution.py:52
  50.3 1.4 %collective-permute-start.23 = (bf16[2,2,56,512]{3,2,1,0:T(8,128)(2,1)S(1)}, bf16[2,2,56,512]{3,2,1,0:T(8,128)(2,1)S(1)}, u32[]{:S(2)}, u32[]{:S(2)}) collective-permute-start(bf16[2,2,56,512]{3,2,1,0:T(8,128)(2,1)S(1)} %get-tuple-element.94), channel_id=1, source_target_pairs={{0,2},{2,0},{4,6},{6,4},{8,10},{10,8},{12,14},{14,12},{1,3},{3,1},... | collective-permute-start | bytes 688136 | tf_op jit(solution)/shard_map/ppermute | solution.py:52
  51.8 1.8 %collective-permute-start.16 = (bf16[2,128,512]{2,1,0:T(8,128)(2,1)S(1)}, bf16[2,128,512]{2,1,0:T(8,128)(2,1)S(1)}, u32[]{:S(2)}, u32[]{:S(2)}) collective-permute-start(bf16[2,128,512]{2,1,0:T(8,128)(2,1)S(1)} %stacked.1), channel_id=1, source_target_pairs={{0,4},{2,6},{4,0},{6,2},{8,12},{10,14},{12,8},{14,10},{1,5},{3,7},... | collective-permute-start | bytes 786440 | tf_op jit(solution)/shard_map/ppermute | solution.py:52
  53.6 0.2 collective-permute-start.14
  53.8 3.3 %collective-permute-start.3 = (bf16[64,640]{1,0:T(8,128)(2,1)S(1)}, bf16[64,640]{1,0:T(8,128)(2,1)S(1)}, u32[]{:S(2)}, u32[]{:S(2)}) collective-permute-start(bf16[64,640]{1,0:T(8,128)(2,1)S(1)} %get-tuple-element.66), channel_id=1, source_target_pairs={{0,2},{2,4},{4,6},{6,8},{8,10},{10,12},{12,14},{1,3},{3,5},{5,7},{... | collective-permute-start | bytes 245768 | tf_op jit(solution)/shard_map/ppermute | solution.py:611
  57.1 1.2 %collective-permute-start.22 = (bf16[2,2,56,512]{3,2,1,0:T(8,128)(2,1)S(1)}, bf16[2,2,56,512]{3,2,1,0:T(8,128)(2,1)S(1)}, u32[]{:S(2)}, u32[]{:S(2)}) collective-permute-start(bf16[2,2,56,512]{3,2,1,0:T(8,128)(2,1)S(1)} %get-tuple-element.91), channel_id=1, source_target_pairs={{0,2},{2,0},{4,6},{6,4},{8,10},{10,8},{12,14},{14,12},{1,3},{3,1},... | collective-permute-start | bytes 688136 | tf_op jit(solution)/shard_map/ppermute | solution.py:52
  58.3 3.0 %collective-permute-start.24 = (bf16[2,2,56,512]{3,2,1,0:T(8,128)(2,1)S(1)}, bf16[2,2,56,512]{3,2,1,0:T(8,128)(2,1)S(1)}, u32[]{:S(2)}, u32[]{:S(2)}) collective-permute-start(bf16[2,2,56,512]{3,2,1,0:T(8,128)(2,1)S(1)} %added.3), channel_id=1, source_target_pairs={{0,4},{2,6},{4,0},{6,2},{8,12},{10,14},{12,8},{14,10},{1,5},{3,7},... | collective-permute-start | bytes 688136 | tf_op jit(solution)/shard_map/ppermute | solution.py:52
  61.4 0.1 fold.1
  61.5 0.1 collective-permute-start.21
  61.6 1.6 %collective-permute-start.4 = (bf16[128,640]{1,0:T(8,128)(2,1)S(1)}, bf16[128,640]{1,0:T(8,128)(2,1)S(1)}, u32[]{:S(2)}, u32[]{:S(2)}) collective-permute-start(bf16[128,640]{1,0:T(8,128)(2,1)S(1)} %own_tokens.1.own), channel_id=1, source_target_pairs={{0,16},{16,0},{1,17},{17,1},{2,18},{18,2},{3,19},{19,3},{4,20},{20... | collective-permute-start | bytes 491528 | tf_op jit(solution)/shard_map/ppermute | solution.py:52
  63.2 1.2 %weight_part.1 = (f32[256,512]{1,0:T(8,128)S(1)}, bf16[256,512]{1,0:T(8,128)(2,1)S(1)}, bf16[256,512]{1,0:T(8,128)(2,1)S(1)}, bf16[256,512]{1,0:T(8,128)(2,1)S(1)}) custom-call(bf16[512,128]{1,0:T(8,128)(2,1)S(1)} %get-tuple-element.77.refs_0_, bf16[512,128]{1,0:T(8,128)(2,1)S(1)} %collective-permute-done.8.refs_1_, ...), custom_call_target="tpu_custom_call" | custom-call | tf_op jit(solution)/shard_map/weight_part/pallas_call | solution.py:34
  64.4 1.9 %collective-permute-start.17 = (bf16[256,512]{1,0:T(8,128)(2,1)S(1)}, bf16[256,512]{1,0:T(8,128)(2,1)S(1)}, u32[]{:S(2)}, u32[]{:S(2)}) collective-permute-start(bf16[256,512]{1,0:T(8,128)(2,1)S(1)} %get-tuple-element.82), channel_id=1, source_target_pairs={{0,2},{2,0},{4,6},{6,4},{8,10},{10,8},{12,14},{14,12},{1,3},{3,1},... | collective-permute-start | bytes 786440 | tf_op jit(solution)/shard_map/ppermute | solution.py:52
  66.3 1.0 %collective-permute-done.4.other = bf16[128,640]{1,0:T(8,128)(2,1)S(1)} collective-permute-done((bf16[128,640]{1,0:T(8,128)(2,1)S(1)}, bf16[128,640]{1,0:T(8,128)(2,1)S(1)}, u32[]{:S(2)}, u32[]{:S(2)}) %collective-permute-start.4) | collective-permute-done | bytes 163872 | tf_op jit(solution)/shard_map/ppermute | solution.py:52
  67.2 1.6 %normed_part.1 = (f32[128,1024]{1,0:T(8,128)S(1)}, bf16[128,512]{1,0:T(8,128)(2,1)S(1)}, bf16[128,640]{1,0:T(8,128)(2,1)S(1)}, f32[128,1]{1,0:T(8,128)S(1)}) custom-call(bf16[128,640]{1,0:T(8,128)(2,1)S(1)} %own_tokens.1.own, bf16[128,640]{1,0:T(8,128)(2,1)S(1)} %collective-permute-done.4.other, bf16[2048,1024]{1,0:T(8,128)(2,1)S(1)} %copy-done), custom_call_target="tpu_custom_call" | custom-call | tf_op jit(solution)/shard_map/normed_part/pallas_call | solution.py:34
  68.9 1.6 %collective-permute-start.18 = (bf16[256,512]{1,0:T(8,128)(2,1)S(1)}, bf16[256,512]{1,0:T(8,128)(2,1)S(1)}, u32[]{:S(2)}, u32[]{:S(2)}) collective-permute-start(bf16[256,512]{1,0:T(8,128)(2,1)S(1)} %get-tuple-element.83), channel_id=1, source_target_pairs={{0,16},{16,0},{1,17},{17,1},{2,18},{18,2},{3,19},{19,3},{4,20},{20... | collective-permute-start | bytes 786440 | tf_op jit(solution)/shard_map/ppermute | solution.py:52
  70.5 1.6 %collective-permute-start.19 = (bf16[256,512]{1,0:T(8,128)(2,1)S(1)}, bf16[256,512]{1,0:T(8,128)(2,1)S(1)}, u32[]{:S(2)}, u32[]{:S(2)}) collective-permute-start(bf16[256,512]{1,0:T(8,128)(2,1)S(1)} %get-tuple-element.84), channel_id=1, source_target_pairs={{0,18},{2,16},{4,22},{6,20},{8,26},{10,24},{12,30},{14,28},{16,2},... | collective-permute-start | bytes 786440 | tf_op jit(solution)/shard_map/ppermute | solution.py:595
  72.2 0.1 outer_sums.1
  72.3 1.2 %collective-permute-done.5.received = bf16[128,512]{1,0:T(8,128)(2,1)S(1)} collective-permute-done((bf16[128,512]{1,0:T(8,128)(2,1)S(1)}, bf16[128,512]{1,0:T(8,128)(2,1)S(1)}, u32[]{:S(2)}, u32[]{:S(2)}) %collective-permute-start.5) | collective-permute-done | bytes 131104 | tf_op jit(solution)/shard_map/ppermute | solution.py:52
  73.4 2.7 %collective-permute-start.25 = (bf16[2,56,512]{2,1,0:T(8,128)(2,1)S(1)}, bf16[2,56,512]{2,1,0:T(8,128)(2,1)S(1)}, u32[]{:S(2)}, u32[]{:S(2)}) collective-permute-start(bf16[2,56,512]{2,1,0:T(8,128)(2,1)S(1)} %get-tuple-element.96), channel_id=1, source_target_pairs={{0,8},{2,10},{4,12},{6,14},{8,0},{10,2},{12,4},{14,6},{1,9},{3,11}... | collective-permute-start | bytes 344072 | tf_op jit(solution)/shard_map/ppermute | solution.py:52
  76.1 1.5 %collective-permute-start.26 = (bf16[2,56,512]{2,1,0:T(8,128)(2,1)S(1)}, bf16[2,56,512]{2,1,0:T(8,128)(2,1)S(1)}, u32[]{:S(2)}, u32[]{:S(2)}) collective-permute-start(bf16[2,56,512]{2,1,0:T(8,128)(2,1)S(1)} %get-tuple-element.97), channel_id=1, source_target_pairs={{0,16},{16,0},{1,17},{17,1},{2,18},{18,2},{3,19},{19,3},{4,20},{20... | collective-permute-start | bytes 344072 | tf_op jit(solution)/shard_map/ppermute | solution.py:52
  77.6 0.2 collective-permute-start.27
  77.8 1.0 %hidden_grad.1 = (bf16[128,1024]{1,0:T(8,128)(2,1)}, f32[1,128]{1,0:T(1,128)}) custom-call(f32[128,1024]{1,0:T(8,128)S(1)} %get-tuple-element.67.kept, bf16[128,512]{1,0:T(8,128)(2,1)S(1)} %collective-permute-done.5.received, bf16[128,640]{1,0:T(8,128)(2,1)S(1)} %collective-permute-done.6.more, f32[128,1]{1,0:T(8,128)S(1)} %get-tuple-element.70.dots, ...), custom_call_target="tpu_custom_call" | custom-call | tf_op jit(solution)/shard_map/hidden_grad/pallas_call | solution.py:34
  78.8 5.1 %collective-permute-done.18.side = bf16[256,512]{1,0:T(8,128)(2,1)S(1)} collective-permute-done((bf16[256,512]{1,0:T(8,128)(2,1)S(1)}, bf16[256,512]{1,0:T(8,128)(2,1)S(1)}, u32[]{:S(2)}, u32[]{:S(2)}) %collective-permute-start.18) | collective-permute-done | bytes 262176 | tf_op jit(solution)/shard_map/ppermute | solution.py:52
  83.9 1.1 %query_grad.1 = f32[256,1024]{1,0:T(8,128)} custom-call(f32[256,512]{1,0:T(8,128)S(1)} %get-tuple-element.81.kept, bf16[256,512]{1,0:T(8,128)(2,1)S(1)} %collective-permute-done.17.paired, bf16[256,512]{1,0:T(8,128)(2,1)S(1)} %collective-permute-done.18.side, bf16[256,512]{1,0:T(8,128)(2,1)S(1)} %collective-permute-done.19.cross), custom_call_target="tpu_custom_call" | custom-call | tf_op jit(solution)/shard_map/query_grad/pallas_call | solution.py:34
  84.9 0.3 collective-permute-done.25.following
  85.2 2.9 %collective-permute-done.26.side = bf16[2,56,512]{2,1,0:T(8,128)(2,1)S(1)} collective-permute-done((bf16[2,56,512]{2,1,0:T(8,128)(2,1)S(1)}, bf16[2,56,512]{2,1,0:T(8,128)(2,1)S(1)}, u32[]{:S(2)}, u32[]{:S(2)}) %collective-permute-start.26) | collective-permute-done | bytes 114720 | tf_op jit(solution)/shard_map/ppermute | solution.py:52
  88.2 0.8 kv_grad.1
  (42 shorter events, 0.3 us)
Async XLA Ops:
  0.6 11.8 %copy-start.1 = (bf16[16,128,896]{2,1,0:T(8,128)(2,1)S(1)}, bf16[16,128,896]{2,1,0:T(8,128)(2,1)}, u32[]{:S(2)}) copy-start(bf16[16,128,896]{2,1,0:T(8,128)(2,1)} %param.11) | copy-start | bytes 11010052
  0.6 1.1 %copy-start.3 = (bf16[128,1024]{1,0:T(8,128)(2,1)S(1)}, bf16[128,1024]{1,0:T(8,128)(2,1)}, u32[]{:S(2)}) copy-start(bf16[128,1024]{1,0:T(8,128)(2,1)} %grad_own.3) | copy-start | bytes 786436
  1.7 0.8 copy-start.4
  2.5 9.9 %copy-start.7 = (bf16[896]{0:T(1024)(128)(2,1)S(1)}, bf16[896]{0:T(1024)(128)(2,1)}, u32[]{:S(2)}) copy-start(bf16[896]{0:T(1024)(128)(2,1)} %gain.3) | copy-start | bytes 5380
  5.5 31.2 %collective-permute-start.7 = (bf16[64,2048]{1,0:T(8,128)(2,1)S(1)}, bf16[64,2048]{1,0:T(8,128)(2,1)S(1)}, u32[]{:S(2)}, u32[]{:S(2)}) collective-permute-start(bf16[64,2048]{1,0:T(8,128)(2,1)S(1)} %get-tuple-element.76), channel_id=1, source_target_pairs={{2,0},{4,2},{6,4},{8,6},{10,8},{12,10},{14,12},{3,1},{5,3},{7,5},{... | collective-permute-start | bytes 786440 | tf_op jit(solution)/shard_map/ppermute | solution.py:575
  6.8 15.3 %collective-permute-start = (bf16[128,512]{1,0:T(8,128)(2,1)S(1)}, bf16[128,512]{1,0:T(8,128)(2,1)S(1)}, u32[]{:S(2)}, u32[]{:S(2)}) collective-permute-start(bf16[128,512]{1,0:T(8,128)(2,1)S(1)} %get-tuple-element.55), channel_id=1, source_target_pairs={{0,16},{16,0},{1,17},{17,1},{2,18},{18,2},{3,19},{19,3},{4,20},{20... | collective-permute-start | bytes 393224 | tf_op jit(solution)/shard_map/ppermute | solution.py:52
  9.8 12.2 %collective-permute-start.1 = (bf16[2,64,512]{2,1,0:T(8,128)(2,1)S(1)}, bf16[2,64,512]{2,1,0:T(8,128)(2,1)S(1)}, u32[]{:S(2)}, u32[]{:S(2)}) collective-permute-start(bf16[2,64,512]{2,1,0:T(8,128)(2,1)S(1)} %get-tuple-element.56), channel_id=1, source_target_pairs={{2,0},{4,2},{6,4},{8,6},{10,8},{12,10},{14,12},{3,1},{5,3},{7,5},{... | collective-permute-start | bytes 393224 | tf_op jit(solution)/shard_map/ppermute | solution.py:569
  11.1 10.9 %collective-permute-start.2 = (bf16[64,512]{1,0:T(8,128)(2,1)S(1)}, bf16[64,512]{1,0:T(8,128)(2,1)S(1)}, u32[]{:S(2)}, u32[]{:S(2)}) collective-permute-start(bf16[64,512]{1,0:T(8,128)(2,1)S(1)} %get-tuple-element.57), channel_id=1, source_target_pairs={{2,16},{4,18},{6,20},{8,22},{10,24},{12,26},{14,28},{18,0},{20,2},... | collective-permute-start | bytes 196616 | tf_op jit(solution)/shard_map/ppermute | solution.py:570
  12.4 2.0 %copy-start.2 = (bf16[2,896,1024]{2,1,0:T(8,128)(2,1)S(1)}, bf16[2,896,1024]{2,1,0:T(8,128)(2,1)}, u32[]{:S(2)}) copy-start(bf16[2,896,1024]{2,1,0:T(8,128)(2,1)} %weight.2) | copy-start | bytes 11010052
  14.5 7.6 %copy-start.5 = (s32[2,16]{1,0:T(2,128)S(1)}, s32[2,16]{1,0:T(2,128)}, u32[]{:S(2)}) copy-start(s32[2,16]{1,0:T(2,128)} %ids.3) | copy-start | bytes 388
  14.5 7.6 %copy-start.6 = (s32[2]{0:T(128)S(1)}, s32[2]{0:T(128)}, u32[]{:S(2)}) copy-start(s32[2]{0:T(128)} %counts.3) | copy-start | bytes 28
  27.3 34.1 %collective-permute-start.20 = (bf16[4,2,56,512]{3,2,1,0:T(8,128)(2,1)S(1)}, bf16[4,2,56,512]{3,2,1,0:T(8,128)(2,1)S(1)}, u32[]{:S(2)}, u32[]{:S(2)}) collective-permute-start(bf16[4,2,56,512]{3,2,1,0:T(8,128)(2,1)S(1)} %get-tuple-element.86), channel_id=1, source_target_pairs={{0,2},{2,0},{4,6},{6,4},{8,10},{10,8},{12,14},{14,12},{1,3},{3,1},... | collective-permute-start | bytes 1376264 | tf_op jit(solution)/shard_map/ppermute | solution.py:52
  32.9 10.4 %collective-permute-start.15 = (bf16[1,128,512]{2,1,0:T(8,128)(2,1)S(1)}, bf16[1,128,512]{2,1,0:T(8,128)(2,1)S(1)}, u32[]{:S(2)}, u32[]{:S(2)}) collective-permute-start(bf16[1,128,512]{2,1,0:T(8,128)(2,1)S(1)} %bitcast.4), channel_id=1, source_target_pairs={{0,8},{2,10},{4,12},{6,14},{8,0},{10,2},{12,4},{14,6},{1,9},{3,11}... | collective-permute-start | bytes 393224 | tf_op jit(solution)/shard_map/ppermute | solution.py:52
  37.3 6.0 %collective-permute-start.8 = (bf16[512,128]{1,0:T(8,128)(2,1)S(1)}, bf16[512,128]{1,0:T(8,128)(2,1)S(1)}, u32[]{:S(2)}, u32[]{:S(2)}) collective-permute-start(bf16[512,128]{1,0:T(8,128)(2,1)S(1)} %get-tuple-element.78), channel_id=1, source_target_pairs={{0,4},{2,6},{4,0},{6,2},{8,12},{10,14},{12,8},{14,10},{1,5},{3,7},... | collective-permute-start | bytes 393224 | tf_op jit(solution)/shard_map/ppermute | solution.py:52
  38.9 11.4 %collective-permute-start.9 = (bf16[512,128]{1,0:T(8,128)(2,1)S(1)}, bf16[512,128]{1,0:T(8,128)(2,1)S(1)}, u32[]{:S(2)}, u32[]{:S(2)}) collective-permute-start(bf16[512,128]{1,0:T(8,128)(2,1)S(1)} %get-tuple-element.79), channel_id=1, source_target_pairs={{0,8},{2,10},{4,12},{6,14},{8,0},{10,2},{12,4},{14,6},{1,9},{3,11}... | collective-permute-start | bytes 393224 | tf_op jit(solution)/shard_map/ppermute | solution.py:52
  39.0 12.8 %collective-permute-start.10 = (bf16[512,128]{1,0:T(8,128)(2,1)S(1)}, bf16[512,128]{1,0:T(8,128)(2,1)S(1)}, u32[]{:S(2)}, u32[]{:S(2)}) collective-permute-start(bf16[512,128]{1,0:T(8,128)(2,1)S(1)} %get-tuple-element.80), channel_id=1, source_target_pairs={{0,12},{2,14},{4,8},{6,10},{8,4},{10,6},{12,0},{14,2},{1,13},{3,15... | collective-permute-start | bytes 393224 | tf_op jit(solution)/shard_map/ppermute | solution.py:52
  43.3 8.5 %collective-permute-start.11 = (bf16[512,128]{1,0:T(8,128)(2,1)S(1)}, bf16[512,128]{1,0:T(8,128)(2,1)S(1)}, u32[]{:S(2)}, u32[]{:S(2)}) collective-permute-start(bf16[512,128]{1,0:T(8,128)(2,1)S(1)} %get-tuple-element.77.refs_0_), channel_id=1, source_target_pairs={{0,1},{1,0},{2,3},{3,2},{4,5},{5,4},{6,7},{7,6},{8,9},{9,8},{10,11... | collective-permute-start | bytes 393224 | tf_op jit(solution)/shard_map/ppermute | solution.py:52
  43.3 10.3 %collective-permute-start.12 = (bf16[512,128]{1,0:T(8,128)(2,1)S(1)}, bf16[512,128]{1,0:T(8,128)(2,1)S(1)}, u32[]{:S(2)}, u32[]{:S(2)}) collective-permute-start(bf16[512,128]{1,0:T(8,128)(2,1)S(1)} %collective-permute-done.8.refs_1_), channel_id=1, source_target_pairs={{0,1},{1,0},{2,3},{3,2},{4,5},{5,4},{6,7},{7,6},{8,9},{9,8},{10,11... | collective-permute-start | bytes 393224 | tf_op jit(solution)/shard_map/ppermute | solution.py:52
  46.2 21.0 %copy-start = (bf16[2048,1024]{1,0:T(8,128)(2,1)S(1)}, bf16[2048,1024]{1,0:T(8,128)(2,1)}, u32[]{:S(2)}) copy-start(bf16[2048,1024]{1,0:T(8,128)(2,1)} %weight.3) | copy-start | bytes 12582916
  50.3 8.0 %collective-permute-start.23 = (bf16[2,2,56,512]{3,2,1,0:T(8,128)(2,1)S(1)}, bf16[2,2,56,512]{3,2,1,0:T(8,128)(2,1)S(1)}, u32[]{:S(2)}, u32[]{:S(2)}) collective-permute-start(bf16[2,2,56,512]{3,2,1,0:T(8,128)(2,1)S(1)} %get-tuple-element.94), channel_id=1, source_target_pairs={{0,2},{2,0},{4,6},{6,4},{8,10},{10,8},{12,14},{14,12},{1,3},{3,1},... | collective-permute-start | bytes 688136 | tf_op jit(solution)/shard_map/ppermute | solution.py:52
  51.8 2.1 %collective-permute-start.13 = (bf16[512,128]{1,0:T(8,128)(2,1)S(1)}, bf16[512,128]{1,0:T(8,128)(2,1)S(1)}, u32[]{:S(2)}, u32[]{:S(2)}) collective-permute-start(bf16[512,128]{1,0:T(8,128)(2,1)S(1)} %collective-permute-done.9.refs_2_), channel_id=1, source_target_pairs={{0,1},{1,0},{2,3},{3,2},{4,5},{5,4},{6,7},{7,6},{8,9},{9,8},{10,11... | collective-permute-start | bytes 393224 | tf_op jit(solution)/shard_map/ppermute | solution.py:52
  51.8 11.4 %collective-permute-start.16 = (bf16[2,128,512]{2,1,0:T(8,128)(2,1)S(1)}, bf16[2,128,512]{2,1,0:T(8,128)(2,1)S(1)}, u32[]{:S(2)}, u32[]{:S(2)}) collective-permute-start(bf16[2,128,512]{2,1,0:T(8,128)(2,1)S(1)} %stacked.1), channel_id=1, source_target_pairs={{0,4},{2,6},{4,0},{6,2},{8,12},{10,14},{12,8},{14,10},{1,5},{3,7},... | collective-permute-start | bytes 786440 | tf_op jit(solution)/shard_map/ppermute | solution.py:52
  53.6 3.5 %collective-permute-start.14 = (bf16[512,128]{1,0:T(8,128)(2,1)S(1)}, bf16[512,128]{1,0:T(8,128)(2,1)S(1)}, u32[]{:S(2)}, u32[]{:S(2)}) collective-permute-start(bf16[512,128]{1,0:T(8,128)(2,1)S(1)} %collective-permute-done.10.refs_3_), channel_id=1, source_target_pairs={{0,1},{1,0},{2,3},{3,2},{4,5},{5,4},{6,7},{7,6},{8,9},{9,8},{10,11... | collective-permute-start | bytes 393224 | tf_op jit(solution)/shard_map/ppermute | solution.py:52
  53.8 7.8 %collective-permute-start.3 = (bf16[64,640]{1,0:T(8,128)(2,1)S(1)}, bf16[64,640]{1,0:T(8,128)(2,1)S(1)}, u32[]{:S(2)}, u32[]{:S(2)}) collective-permute-start(bf16[64,640]{1,0:T(8,128)(2,1)S(1)} %get-tuple-element.66), channel_id=1, source_target_pairs={{0,2},{2,4},{4,6},{6,8},{8,10},{10,12},{12,14},{1,3},{3,5},{5,7},{... | collective-permute-start | bytes 245768 | tf_op jit(solution)/shard_map/ppermute | solution.py:611
  57.1 11.8 %collective-permute-start.22 = (bf16[2,2,56,512]{3,2,1,0:T(8,128)(2,1)S(1)}, bf16[2,2,56,512]{3,2,1,0:T(8,128)(2,1)S(1)}, u32[]{:S(2)}, u32[]{:S(2)}) collective-permute-start(bf16[2,2,56,512]{3,2,1,0:T(8,128)(2,1)S(1)} %get-tuple-element.91), channel_id=1, source_target_pairs={{0,2},{2,0},{4,6},{6,4},{8,10},{10,8},{12,14},{14,12},{1,3},{3,1},... | collective-permute-start | bytes 688136 | tf_op jit(solution)/shard_map/ppermute | solution.py:52
  58.3 12.1 %collective-permute-start.24 = (bf16[2,2,56,512]{3,2,1,0:T(8,128)(2,1)S(1)}, bf16[2,2,56,512]{3,2,1,0:T(8,128)(2,1)S(1)}, u32[]{:S(2)}, u32[]{:S(2)}) collective-permute-start(bf16[2,2,56,512]{3,2,1,0:T(8,128)(2,1)S(1)} %added.3), channel_id=1, source_target_pairs={{0,4},{2,6},{4,0},{6,2},{8,12},{10,14},{12,8},{14,10},{1,5},{3,7},... | collective-permute-start | bytes 688136 | tf_op jit(solution)/shard_map/ppermute | solution.py:52
  61.5 10.6 %collective-permute-start.21 = (bf16[2,2,56,512]{3,2,1,0:T(8,128)(2,1)S(1)}, bf16[2,2,56,512]{3,2,1,0:T(8,128)(2,1)S(1)}, u32[]{:S(2)}, u32[]{:S(2)}) collective-permute-start(bf16[2,2,56,512]{3,2,1,0:T(8,128)(2,1)S(1)} %get-tuple-element.88), channel_id=1, source_target_pairs={{0,4},{2,6},{4,0},{6,2},{8,12},{10,14},{12,8},{14,10},{1,5},{3,7},... | collective-permute-start | bytes 688136 | tf_op jit(solution)/shard_map/ppermute | solution.py:52
  61.6 5.6 %collective-permute-start.4 = (bf16[128,640]{1,0:T(8,128)(2,1)S(1)}, bf16[128,640]{1,0:T(8,128)(2,1)S(1)}, u32[]{:S(2)}, u32[]{:S(2)}) collective-permute-start(bf16[128,640]{1,0:T(8,128)(2,1)S(1)} %own_tokens.1.own), channel_id=1, source_target_pairs={{0,16},{16,0},{1,17},{17,1},{2,18},{18,2},{3,19},{19,3},{4,20},{20... | collective-permute-start | bytes 491528 | tf_op jit(solution)/shard_map/ppermute | solution.py:52
  64.4 13.2 %collective-permute-start.17 = (bf16[256,512]{1,0:T(8,128)(2,1)S(1)}, bf16[256,512]{1,0:T(8,128)(2,1)S(1)}, u32[]{:S(2)}, u32[]{:S(2)}) collective-permute-start(bf16[256,512]{1,0:T(8,128)(2,1)S(1)} %get-tuple-element.82), channel_id=1, source_target_pairs={{0,2},{2,0},{4,6},{6,4},{8,10},{10,8},{12,14},{14,12},{1,3},{3,1},... | collective-permute-start | bytes 786440 | tf_op jit(solution)/shard_map/ppermute | solution.py:52
  68.8 7.3 %collective-permute-start.6 = (bf16[128,640]{1,0:T(8,128)(2,1)S(1)}, bf16[128,640]{1,0:T(8,128)(2,1)S(1)}, u32[]{:S(2)}, u32[]{:S(2)}) collective-permute-start(bf16[128,640]{1,0:T(8,128)(2,1)S(1)} %get-tuple-element.69), channel_id=1, source_target_pairs={{0,1},{1,0},{2,3},{3,2},{4,5},{5,4},{6,7},{7,6},{8,9},{9,8},{10,11... | collective-permute-start | bytes 491528 | tf_op jit(solution)/shard_map/ppermute | solution.py:52
  68.9 15.0 %collective-permute-start.18 = (bf16[256,512]{1,0:T(8,128)(2,1)S(1)}, bf16[256,512]{1,0:T(8,128)(2,1)S(1)}, u32[]{:S(2)}, u32[]{:S(2)}) collective-permute-start(bf16[256,512]{1,0:T(8,128)(2,1)S(1)} %get-tuple-element.83), channel_id=1, source_target_pairs={{0,16},{16,0},{1,17},{17,1},{2,18},{18,2},{3,19},{19,3},{4,20},{20... | collective-permute-start | bytes 786440 | tf_op jit(solution)/shard_map/ppermute | solution.py:52
  70.5 13.4 %collective-permute-start.19 = (bf16[256,512]{1,0:T(8,128)(2,1)S(1)}, bf16[256,512]{1,0:T(8,128)(2,1)S(1)}, u32[]{:S(2)}, u32[]{:S(2)}) collective-permute-start(bf16[256,512]{1,0:T(8,128)(2,1)S(1)} %get-tuple-element.84), channel_id=1, source_target_pairs={{0,18},{2,16},{4,22},{6,20},{8,26},{10,24},{12,30},{14,28},{16,2},... | collective-permute-start | bytes 786440 | tf_op jit(solution)/shard_map/ppermute | solution.py:595
  72.1 1.3 %collective-permute-start.5 = (bf16[128,512]{1,0:T(8,128)(2,1)S(1)}, bf16[128,512]{1,0:T(8,128)(2,1)S(1)}, u32[]{:S(2)}, u32[]{:S(2)}) collective-permute-start(bf16[128,512]{1,0:T(8,128)(2,1)S(1)} %get-tuple-element.68), channel_id=1, source_target_pairs={{0,1},{1,0},{2,3},{3,2},{4,5},{5,4},{6,7},{7,6},{8,9},{9,8},{10,11... | collective-permute-start | bytes 393224 | tf_op jit(solution)/shard_map/ppermute | solution.py:52
  73.4 11.8 %collective-permute-start.25 = (bf16[2,56,512]{2,1,0:T(8,128)(2,1)S(1)}, bf16[2,56,512]{2,1,0:T(8,128)(2,1)S(1)}, u32[]{:S(2)}, u32[]{:S(2)}) collective-permute-start(bf16[2,56,512]{2,1,0:T(8,128)(2,1)S(1)} %get-tuple-element.96), channel_id=1, source_target_pairs={{0,8},{2,10},{4,12},{6,14},{8,0},{10,2},{12,4},{14,6},{1,9},{3,11}... | collective-permute-start | bytes 344072 | tf_op jit(solution)/shard_map/ppermute | solution.py:52
  76.1 12.0 %collective-permute-start.26 = (bf16[2,56,512]{2,1,0:T(8,128)(2,1)S(1)}, bf16[2,56,512]{2,1,0:T(8,128)(2,1)S(1)}, u32[]{:S(2)}, u32[]{:S(2)}) collective-permute-start(bf16[2,56,512]{2,1,0:T(8,128)(2,1)S(1)} %get-tuple-element.97), channel_id=1, source_target_pairs={{0,16},{16,0},{1,17},{17,1},{2,18},{18,2},{3,19},{19,3},{4,20},{20... | collective-permute-start | bytes 344072 | tf_op jit(solution)/shard_map/ppermute | solution.py:52
  77.6 10.5 %collective-permute-start.27 = (bf16[2,56,512]{2,1,0:T(8,128)(2,1)S(1)}, bf16[2,56,512]{2,1,0:T(8,128)(2,1)S(1)}, u32[]{:S(2)}, u32[]{:S(2)}) collective-permute-start(bf16[2,56,512]{2,1,0:T(8,128)(2,1)S(1)} %get-tuple-element.98), channel_id=1, source_target_pairs={{0,24},{2,26},{4,28},{6,30},{8,16},{10,18},{12,20},{14,22},{16,8},... | collective-permute-start | bytes 344072 | tf_op jit(solution)/shard_map/ppermute | solution.py:595
